TPU v7x, 32 devices: a whole 2x2x4 slice. The times are simulated.
32 devices in a mesh: grp: 2 (over x), ep: 16 (over z, y, core).
Axes of the slice: x: 2, y: 2, z: 4, core: 2. Of those that a mesh axis runs over, the one named last changes fastest.
Arguments:
- queries: bfloat16 [1024, 4096], P(('grp', 'ep')), parts along dimension 0, may hold values from -6 to 6
- fresh_key_value: bfloat16 [1024, 2, 256], P(('grp', 'ep')), parts along dimension 0, may hold values from -4 to 4
- key_value_cache: bfloat16 [1024, 2, 256, 256], P(('grp', 'ep')), parts along dimension 0, may hold values from -6 to 6
- lengths: int32 [1024], P(('grp', 'ep')), parts along dimension 0, may hold values from 2 to 256, as said below
- hidden: bfloat16 [1024, 4096], P(('grp', 'ep')), parts along dimension 0, may hold values from -420 to 420
- expert_norm_gain: bfloat16 [4096], replicated, may hold values from 0.099609375 to 1.8984375
- routes: int32 [1024, 8], P(('grp', 'ep')), parts along dimension 0, may hold values from 0 to 15, all different within a row; in each aligned block of 32 rows (0 to 31, 32 to 63, ...) at most 16 rows name the same one
- router_scores: float32 [1024, 8], P(('grp', 'ep')), parts along dimension 0, may hold values from -360 to 360
- gate_up_quant_codes: int32 [16, 4096, 512], P('ep'), may hold values from 0 to 4095
- gate_up_code_scale: bfloat16 [16, 64, 1536], P('ep'), may hold values from 0.015625 to 0.0625
- down_quant_codes: int32 [16, 256, 4096], P('ep'), may hold values from 0 to 4095
- down_code_scale: bfloat16 [16, 12, 4096], P('ep'), may hold values from 0.035888672 to 0.14355469
- adapter_input_down: bfloat16 [16, 4096, 32], P('ep'), may hold values from -0.09375 to 0.09375
- adapter_input_up: bfloat16 [16, 2, 16, 768], P('ep'), may hold values from -0.375 to 0.375
- adapter_output_down: bfloat16 [16, 768, 16], P('ep'), may hold values from -0.21875 to 0.21875
- adapter_output_up: bfloat16 [16, 16, 4096], P('ep'), may hold values from -0.375 to 0.375
Outputs:
- context: bfloat16 [1024, 4096], P(('grp', 'ep')), parts along dimension 0
- expert_sum: bfloat16 [1024, 4096], P(('grp', 'ep')), parts along dimension 0
There are 2 independent parts, one for each index of `grp`. A program takes and returns all parts, laid end to end along the dimension named above; an argument that names none is the same for every part. Nothing has to cross between parts.
Inputs may be any that keep to these rules, and one draw needn't show every extreme that they name: `routes`: each row names 8 different experts, and every expert is named by some row. Among the rows of one device, no expert is named more than 16 times, and in every draw some device's rows name some expert exactly 16 times. `lengths`: among the rows of each device, one row has length 256.
All inputs are finite; a program needn't handle non-finite values.
Results may differ from a plain program's by a relative error of at most 0.0081.
Values may be sent and summed in bfloat16 or wider, within the bound.
No kernel may reach another device: no remote copies, remote signals or barrier semaphores. Data moves between devices by JAX's collectives and lax.ppermute only.
A program may use at most 192 MiB of HBM per device.

v0:
```python
import math

import jax
import jax.numpy as jnp
from jax import lax
from jax.sharding import PartitionSpec as P

HEADS = 32
KV_HEADS = 2
HEAD = 128


code_levels = (
    -1.0,
    -0.6961928009986877,
    -0.5250730514526367,
    -0.39491748809814453,
    -0.28444138169288635,
    -0.18477343022823334,
    -0.09105003625154495,
    0.0,
    0.07958029955625534,
    0.16093020141124725,
    0.24611230194568634,
    0.33791524171829224,
    0.44070982933044434,
    0.5626170039176941,
    0.7229568362236023,
    1.0,
)
adapter_scale = 2.0
norm_epsilon = 1e-06


def decode_levels(nibbles):
    decoded = jnp.zeros(nibbles.shape, jnp.float32)
    for code_index in range(16):
        decoded = jnp.where(nibbles == code_index, jnp.float32(code_levels[code_index]), decoded)
    return decoded


def unpack_columns(packed):
    nibbles = [
        jnp.bitwise_and(jnp.right_shift(packed, 4 * nibble_pos), 15) for nibble_pos in range(3)
    ]
    return jnp.concatenate(nibbles, axis=1)


def unpack_rows(packed):
    nibbles = [
        jnp.bitwise_and(jnp.right_shift(packed, 4 * nibble_pos), 15) for nibble_pos in range(3)
    ]
    return jnp.concatenate(nibbles, axis=0)


def dequantize(nibbles, block_scale):
    levels = decode_levels(nibbles)
    blocks = block_scale.shape[0]
    columns = levels.shape[1]
    shaped = (
        levels.reshape(blocks, levels.shape[0] // blocks, columns)
        * block_scale.astype(jnp.float32)[:, None, :]
    )
    return shaped.reshape(levels.shape[0], columns).astype(jnp.bfloat16)


def expert_rows(
    expert_in, weight_both, down_weight_matrix, enter_a, enter_up_map, leave_a, leave_up_map
):
    hidden_units_width = down_weight_matrix.shape[0]
    low_rank_term = leave_a.shape[1]
    middle_hidden = jnp.dot(expert_in, enter_a, preferred_element_type=jnp.float32).astype(
        jnp.bfloat16
    )
    joined_output = jnp.dot(expert_in, weight_both, preferred_element_type=jnp.float32)
    gate_values = joined_output[:, :hidden_units_width] + adapter_scale * jnp.dot(
        middle_hidden[:, :low_rank_term], enter_up_map[0], preferred_element_type=jnp.float32
    )
    upward_hidden = joined_output[:, hidden_units_width:] + adapter_scale * jnp.dot(
        middle_hidden[:, low_rank_term:], enter_up_map[1], preferred_element_type=jnp.float32
    )
    active_rows = (jax.nn.silu(gate_values) * upward_hidden).astype(jnp.bfloat16)
    lowered_hidden = jnp.dot(active_rows, leave_a, preferred_element_type=jnp.float32).astype(
        jnp.bfloat16
    )
    final_output = jnp.dot(
        active_rows, down_weight_matrix, preferred_element_type=jnp.float32
    ) + adapter_scale * jnp.dot(lowered_hidden, leave_up_map, preferred_element_type=jnp.float32)
    return final_output.astype(jnp.bfloat16)


def attend(queries, fresh_key_value, key_value_cache, lengths):
    row_count = queries.shape[0]
    cache_len = key_value_cache.shape[2]
    per_group = HEADS // KV_HEADS
    group_eye = jnp.eye(KV_HEADS, dtype=jnp.bfloat16)
    query_view = queries.reshape(row_count, KV_HEADS, per_group, 1, HEAD)
    spread_query = (query_view * group_eye[None, :, None, :, None]).reshape(
        row_count, HEADS, KV_HEADS * HEAD
    )
    keys_all = key_value_cache[:, 0]
    values_all = key_value_cache[:, 1]
    scaling = 1.0 / math.sqrt(HEAD)
    old_scores = (
        jnp.einsum("thx,tcx->thc", spread_query, keys_all, preferred_element_type=jnp.float32)
        * scaling
    )
    new_scores = (
        jnp.einsum(
            "thx,tx->th", spread_query, fresh_key_value[:, 0], preferred_element_type=jnp.float32
        )
        * scaling
    )
    visible = jnp.arange(cache_len)[None, :] < lengths[:, None]
    old_scores = jnp.where(visible[:, None, :], old_scores, -jnp.inf)
    highest = jnp.maximum(jnp.max(old_scores, axis=-1), new_scores)
    old_exp = jnp.exp(old_scores - highest[..., None])
    new_exp = jnp.exp(new_scores - highest)
    denominator = jnp.sum(old_exp, axis=-1) + new_exp
    old_prob = (old_exp / denominator[..., None]).astype(jnp.bfloat16)
    new_prob = (new_exp / denominator).astype(jnp.bfloat16)
    blended = jnp.einsum("thc,tcx->thx", old_prob, values_all, preferred_element_type=jnp.float32)
    blended = (
        blended
        + new_prob.astype(jnp.float32)[..., None]
        * fresh_key_value[:, 1].astype(jnp.float32)[:, None, :]
    )
    blended = blended.reshape(row_count, KV_HEADS, per_group, KV_HEADS, HEAD)
    own_group = jnp.sum(blended * group_eye.astype(jnp.float32)[None, :, None, :, None], axis=3)
    return own_group.reshape(row_count, HEADS * HEAD).astype(jnp.bfloat16)


def shards(
    queries,
    fresh_key_value,
    key_value_cache,
    lengths,
    hidden,
    expert_norm_gain,
    routes,
    router_scores,
    gate_up_quant_codes,
    gate_up_code_scale,
    down_quant_codes,
    down_code_scale,
    adapter_input_down,
    adapter_input_up,
    adapter_output_down,
    adapter_output_up,
):
    context = attend(queries, fresh_key_value, key_value_cache, lengths)
    hidden_wide = hidden.astype(jnp.float32)
    spread = jnp.mean(hidden_wide * hidden_wide, axis=-1, keepdims=True)
    normed = (
        hidden_wide * lax.rsqrt(spread + norm_epsilon) * expert_norm_gain.astype(jnp.float32)
    ).astype(jnp.bfloat16)
    shares = jax.nn.softmax(router_scores, axis=-1)
    local_rows = hidden.shape[0]
    ep_count = lax.axis_size("ep")
    capacity = local_rows // 2
    weight_both = dequantize(unpack_columns(gate_up_quant_codes[0]), gate_up_code_scale[0])
    down_weight_matrix = dequantize(unpack_rows(down_quant_codes[0]), down_code_scale[0])
    expert_ids = jnp.arange(ep_count, dtype=jnp.int32)
    route_hit = routes[:, :, None] == expert_ids[None, None, :]
    hit_rows = jnp.sum(route_hit.astype(jnp.int32), axis=1)
    before = jnp.cumsum(hit_rows, axis=0) - hit_rows
    slot_of = jnp.sum(jnp.where(route_hit, before[:, None, :], 0), axis=2)
    slot_ids = jnp.arange(capacity, dtype=jnp.int32)
    gathered, gathered_routes = (
        lax.all_gather(normed, "ep", axis=0, tiled=True),
        lax.all_gather(routes.astype(jnp.bfloat16), "ep", axis=0, tiled=True),
    )
    own_expert = lax.axis_index("ep")
    owner_hit = (
        jnp.any(gathered_routes.astype(jnp.int32) == own_expert, axis=1)
        .astype(jnp.int32)
        .reshape(ep_count, local_rows)
    )
    owner_slot = jnp.cumsum(owner_hit, axis=1) - owner_hit
    selector = (
        (owner_slot[:, None, :] == slot_ids[None, :, None]) & (owner_hit[:, None, :] == 1)
    ).astype(jnp.bfloat16)
    received = jnp.einsum(
        "scr,srd->scd",
        selector,
        gathered.reshape(ep_count, local_rows, -1),
        preferred_element_type=jnp.float32,
    ).astype(jnp.bfloat16)
    flattened = received.reshape(-1, received.shape[-1])
    final_output = expert_rows(
        flattened,
        weight_both,
        down_weight_matrix,
        adapter_input_down[0],
        adapter_input_up[0],
        adapter_output_down[0],
        adapter_output_up[0],
    )
    produced = final_output.reshape(received.shape)
    returned = lax.all_to_all(produced, "ep", split_axis=0, concat_axis=0, tiled=True)
    flat_back = returned.reshape(-1, returned.shape[-1])
    picked = flat_back[routes * capacity + slot_of]
    summed_output = jnp.sum(shares[:, :, None] * picked.astype(jnp.float32), axis=1)
    return (context, summed_output.astype(jnp.bfloat16))


def solution(mesh):
    return jax.shard_map(
        shards,
        mesh=mesh,
        in_specs=(
            P(("grp", "ep"), None),
            P(("grp", "ep"), None, None),
            P(("grp", "ep"), None, None, None),
            P(("grp", "ep")),
            P(("grp", "ep"), None),
            P(),
            P(("grp", "ep"), None),
            P(("grp", "ep"), None),
            P("ep", None, None),
            P("ep", None, None),
            P("ep", None, None),
            P("ep", None, None),
            P("ep", None, None),
            P("ep", None, None, None),
            P("ep", None, None),
            P("ep", None, None),
        ),
        out_specs=(P(("grp", "ep"), None), P(("grp", "ep"), None)),
        check_vma=False,
    )
```

profile of v0, /device:TPU:13, one launch (start us, length us, event | category | flops | bytes accessed | tf_op | source)
XLA Modules:
  0.0 174.0 jit_solution(1468743417271459213)
XLA Ops:
  7.2 0.7 convert_element_type.142
  8.0 1.1 fusion.24
  9.1 1.8 %fusion.26 = bf16[32,4096]{1,0:T(8,128)(2,1)} fusion(bf16[32,4096]{1,0:T(8,128)(2,1)} %param.20, f32[4096]{0:T(1024)S(1)} %convert_element_type.142, f32[32]{0:T(128)S(1)} %add_rsqrt_fusion), kind=kLoop, calls=%fused_computation.43 | loop fusion | flops 524288 | bytes 540800 | tf_op jit(solution)/shard_map/convert_element_type | solution.py:156
  10.9 6.6 %shift-right-arithmetic_and_fusion.2 = (s32[1,4096,512]{2,1,0:T(8,128)S(1)}, s32[1,4096,512]{2,1,0:T(8,128)S(1)}, s32[1,4096,512]{2,1,0:T(8,128)}) fusion(s32[1,4096,512]{2,1,0:T(8,128)} %param.24), kind=kLoop, calls=%fused_computation.8 | loop fusion | flops 12582912 | bytes 33554432 | tf_op jit(solution)/shard_map/and | solution.py:44
  17.6 29.9 %multiply_convert_fusion = bf16[64,64,1536]{2,1,0:T(8,128)(2,1)} fusion(s32[64,64,512]{2,1,0:T(8,128)S(1)} %bitcast.96, s32[64,64,512]{2,1,0:T(8,128)} %bitcast.97, s32[64,64,512]{2,1,0:T(8,128)S(1)} %bitcast.95, f32[64,1536]{1,0:T(8,128)S(1)} %bitcast_convert_fusion), kind=kLoop, calls=%fused_computation.2 | loop fusion | flops 226492416 | bytes 38141952 | tf_op jit(solution)/shard_map/convert_element_type | solution.py:64
  47.7 15.8 %all-gather = bf16[16,32,8]{1,2,0:T(8,128)(2,1)S(1)} all-gather(bf16[1,32,8]{1,2,0:T(8,128)(2,1)S(1)} %get-tuple-element.13), channel_id=1, replica_groups=mesh['grp'=2,'ep'=16] {'ep'}, dimensions={0}, use_global_device_ids=true | all-gather | bytes 8704 | tf_op jit(solution)/shard_map/all_gather | solution.py:171
  63.6 0.2 reduce_window_sum.22
  63.8 3.7 %and_bitcast_fusion.2 = (s32[256,4096]{1,0:T(8,128)S(1)}, s32[256,4096]{1,0:T(8,128)S(1)}, s32[256,4096]{1,0:T(8,128)S(1)}) fusion(s32[1,256,4096]{2,1,0:T(8,128)} %param.26), kind=kLoop, calls=%fused_computation.21 | loop fusion | flops 6291456 | bytes 16777216 | tf_op jit(solution)/shard_map/and | solution.py:51
  67.6 14.9 %fusion = bf16[768,4096]{1,0:T(8,128)(2,1)} fusion(s32[256,4096]{1,0:T(8,128)S(1)} %get-tuple-element.6, s32[256,4096]{1,0:T(8,128)S(1)} %get-tuple-element.7, s32[256,4096]{1,0:T(8,128)S(1)} %get-tuple-element.5, f32[12,4096]{1,0:T(8,128)S(1)} %bitcast_convert_fusion.1), kind=kLoop, calls=%fused_computation.5 | loop fusion | flops 113246208 | bytes 19070976 | tf_op jit(solution)/shard_map/convert_element_type | solution.py:64
  82.5 3.0 %convolution_convert_fusion = bf16[16,16,4096]{2,1,0:T(8,128)(2,1)S(1)} fusion(bf16[16,32,4096]{2,1,0:T(8,128)(2,1)} %bitcast.104, s32[16,32]{1,0:T(8,128)S(1)} %convert_subtract_fusion, pred[16,32]{1,0:T(8,128)(4,1)S(1)} %get-tuple-element.14), kind=kOutput, calls=%fused_computation.12 | convolution fusion | flops 68173824 | bytes 6294016 | tf_op jit(solution)/shard_map/scr,srd->scd/dot_general | solution.py:183
  85.5 6.6 %fusion.58 = f32[256,1536]{1,0:T(8,128)S(1)} fusion(bf16[256,4096]{1,0:T(8,128)(2,1)S(1)} %bitcast.101, bf16[4096,1536]{1,0:T(8,128)(2,1)} %bitcast.100), kind=kOutput, calls=%fused_computation.96 | convolution fusion | flops 3221225472 | bytes 16252928 | tf_op jit(solution)/shard_map/dot_general | solution.py:75
  92.1 0.7 convolution_convert_fusion.1
  92.9 0.3 fusion.20
  93.2 0.4 fusion.22
  93.6 3.8 %fusion.59 = f32[256,4096]{1,0:T(8,128)} fusion(bf16[256,768]{1,0:T(8,128)(2,1)S(1)} %fusion.22, bf16[768,4096]{1,0:T(8,128)(2,1)S(1)} %bitcast.99), kind=kOutput, calls=%fused_computation.97 | convolution fusion | flops 1610612736 | bytes 10878976 | tf_op jit(solution)/shard_map/dot_general | solution.py:86
  97.4 4.7 %fusion.2 = bf16[256,4096]{1,0:T(8,128)(2,1)} fusion(f32[256,4096]{1,0:T(8,128)} %fusion.59, bf16[256,768]{1,0:T(8,128)(2,1)S(1)} %fusion.22, bf16[1,16,4096]{2,1,0:T(8,128)(2,1)S(1)} %copy-done.5, bf16[1,768,16]{1,2,0:T(8,128)(2,1)S(1)} %copy-done.8), kind=kOutput, calls=%fused_computation.11 | convolution fusion | flops 42995712 | bytes 6840320 | tf_op jit(solution)/shard_map/dot_general | solution.py:88
  102.1 10.5 %all-to-all-start = ((bf16[16,16,4096]{2,1,0:T(8,128)(2,1)}), bf16[16,16,4096]{2,1,0:T(8,128)(2,1)S(1)}, u32[]{:S(2)}, u32[]{:S(2)}) async-start(bf16[16,16,4096]{2,1,0:T(8,128)(2,1)} %bitcast.103), calls=%async_computation | async-start | bytes 4194304 | tf_op jit(solution)/shard_map/all_to_all | solution.py:200
  112.7 0.1 reshape.220
  112.8 0.1 copy.40
  113.0 0.5 mul.140
  113.5 0.3 mul.141
  113.8 0.1 mul.142
  114.1 0.2 fusion.29
  114.3 3.6 %fusion.57 = (f32[32,32]{1,0:T(8,128)S(1)}, f32[32,32,256]{2,1,0:T(8,128)S(1)}) fusion(bf16[32,2,256,256]{3,2,1,0:T(8,128)(2,1)} %param.18, bf16[32,32,256]{2,1,0:T(8,128)(2,1)S(1)} %mul.141, bf16[32,256]{1,0:T(8,128)(2,1)S(1)} %bitcast.114, pred[32,256]{1,0:T(8,128)(4,1)S(1)} %iota_compare_fusion.2), kind=kOutput, calls=%fused_computation.95 | convolution fusion | flops 135265280 | bytes 5795840 | tf_op jit(solution)/shard_map/thx,tcx->thc/dot_general | solution.py:105
  118.0 0.4 fusion.23
  118.4 4.1 %fusion.13 = f32[32,32,256]{2,1,0:T(8,128)} fusion(bf16[32,2,256,256]{3,2,1,0:T(8,128)(2,1)} %param.18, f32[32,32,256]{2,1,0:T(8,128)S(1)} %get-tuple-element.17, f32[32,256]{1,0:T(8,128)S(1)} %fusion.48, f32[32,32]{1,0:T(8,128)S(1)} %get-tuple-element.9, f32[32,32]{1,0:T(8,128)S(1)} %get-tuple-element.8, f32[32,32]{1,0:T(8,128)S(1)} %multiply_maximum_fusion), kind=kOutput, calls=%fused_computation.25 | convolution fusion | flops 135528448 | bytes 6336512 | tf_op jit(solution)/shard_map/thc,tcx->thx/dot_general | solution.py:122
  122.5 1.7 %reshape.209 = f32[32,2,16,2,128]{4,3,2,1,0:T(2,128)S(1)} reshape(f32[32,32,256]{2,1,0:T(8,128)} %fusion.13) | data formatting | bytes 2097152 | tf_op jit(solution)/shard_map/reshape | solution.py:128
  124.2 1.4 multiply_reduce_fusion
  125.7 0.8 copy.62
  126.5 33.5 %all-to-all-done = bf16[16,16,4096]{2,1,0:T(8,128)(2,1)S(1)} async-done(((bf16[16,16,4096]{2,1,0:T(8,128)(2,1)}), bf16[16,16,4096]{2,1,0:T(8,128)(2,1)S(1)}, u32[]{:S(2)}, u32[]{:S(2)}) %all-to-all-start) | async-done | bytes 2097184 | tf_op jit(solution)/shard_map/all_to_all | solution.py:200
  160.0 3.2 %gather_fusion = bf16[256,4096]{1,0:T(8,128)(2,1)} fusion(bf16[256,4096]{1,0:T(8,128)(2,1)S(1)} %bitcast.94, s32[1024]{0:T(1024)S(1)} %pad_clamp_fusion), kind=kCustom, calls=%fused_computation | custom fusion | bytes 4195328 | tf_op jit(solution)/shard_map/gather | solution.py:202
  163.2 3.9 %fusion.7 = bf16[32,4096]{1,0:T(8,128)(2,1)} fusion(bf16[256,4096]{1,0:T(8,128)(2,1)} %gather_fusion, f32[32,8]{1,0:T(8,128)S(1)} %copy.40), kind=kLoop, calls=%fused_computation.18 | loop fusion | flops 3014656 | bytes 2360320 | tf_op jit(solution)/shard_map/reduce_sum | solution.py:203
  (58 shorter events, 0.9 us)
Async XLA Ops:
  7.2 85.0 %copy-start = (bf16[1,4096,32]{1,2,0:T(8,128)(2,1)S(1)}, bf16[1,4096,32]{1,2,0:T(8,128)(2,1)}, u32[]{:S(2)}) copy-start(bf16[1,4096,32]{1,2,0:T(8,128)(2,1)} %param.28) | copy-start | bytes 786436
  7.2 75.3 %all-gather.3.cloned.1.call-start = ((), (), s32[]{:S(2)}) async-start(), calls=%async_computation.1 | async-start | bytes 4456448 | tf_op jit(solution)/shard_map/all_gather | solution.py:170
  10.9 6.7 %copy-start.2 = (bf16[1,64,1536]{2,1,0:T(8,128)(2,1)S(1)}, bf16[1,64,1536]{2,1,0:T(8,128)(2,1)}, u32[]{:S(2)}) copy-start(bf16[1,64,1536]{2,1,0:T(8,128)(2,1)} %param.25) | copy-start | bytes 589828
  17.6 29.9 %copy-start.6 = (s32[32,8]{0,1:T(8,128)S(1)}, s32[32,8]{0,1:T(8,128)}, u32[]{:S(2)}) copy-start(s32[32,8]{0,1:T(8,128)} %param.22) | copy-start | bytes 3076
  17.6 46.2 %copy-start.3 = (bf16[1,12,4096]{2,1,0:T(8,128)(2,1)S(1)}, bf16[1,12,4096]{2,1,0:T(8,128)(2,1)}, u32[]{:S(2)}) copy-start(bf16[1,12,4096]{2,1,0:T(8,128)(2,1)} %param.27) | copy-start | bytes 294916
  82.5 11.1 %slice-start = ((s8[6291456]{0:T(1024)(128)(4,1)}), s8[4194304]{0:T(1024)(128)(4,1)S(1)}, s32[]{:S(2)}) async-start(s8[6291456]{0:T(1024)(128)(4,1)} %bitcast.98), calls=%async_computation.2 | async-start | bytes 8388608
  85.5 7.4 %copy-start.9 = (bf16[1,2,16,768]{3,2,1,0:T(8,128)(2,1)S(1)}, bf16[1,2,16,768]{3,2,1,0:T(8,128)(2,1)}, u32[]{:S(2)}) copy-start(bf16[1,2,16,768]{3,2,1,0:T(8,128)(2,1)} %param.29) | copy-start | bytes 147460
  85.5 8.1 %slice-start.1 = ((s8[6291456]{0:T(1024)(128)(4,1)}), s8[2097152]{0:T(1024)(128)(4,1)S(1)}, s32[]{:S(2)}) async-start(s8[6291456]{0:T(1024)(128)(4,1)} %bitcast.98), calls=%async_computation.3 | async-start | bytes 4194304
  92.9 4.5 %copy-start.5 = (bf16[1,16,4096]{2,1,0:T(8,128)(2,1)S(1)}, bf16[1,16,4096]{2,1,0:T(8,128)(2,1)}, u32[]{:S(2)}) copy-start(bf16[1,16,4096]{2,1,0:T(8,128)(2,1)} %param.31) | copy-start | bytes 393220
  92.9 4.5 %copy-start.8 = (bf16[1,768,16]{1,2,0:T(8,128)(2,1)S(1)}, bf16[1,768,16]{1,2,0:T(8,128)(2,1)}, u32[]{:S(2)}) copy-start(bf16[1,768,16]{1,2,0:T(8,128)(2,1)} %param.30) | copy-start | bytes 73732
  93.6 19.1 %copy-start.7 = (f32[32,8]{0,1:T(8,128)S(1)}, f32[32,8]{0,1:T(8,128)}, u32[]{:S(2)}) copy-start(f32[32,8]{0,1:T(8,128)} %param.23) | copy-start | bytes 3076
  93.6 19.3 %copy-start.1 = (bf16[32,4096]{1,0:T(8,128)(2,1)S(1)}, bf16[32,4096]{1,0:T(8,128)(2,1)}, u32[]{:S(2)}) copy-start(bf16[32,4096]{1,0:T(8,128)(2,1)} %param.16) | copy-start | bytes 786436
  97.4 16.5 %copy-start.4 = (bf16[32,2,256]{2,1,0:T(2,128)(2,1)S(1)}, bf16[32,2,256]{2,1,0:T(2,128)(2,1)}, u32[]{:S(2)}) copy-start(bf16[32,2,256]{2,1,0:T(2,128)(2,1)} %param.17) | copy-start | bytes 98308
  97.4 16.6 %copy-start.10 = (s32[32]{0:T(128)S(1)}, s32[32]{0:T(128)}, u32[]{:S(2)}) copy-start(s32[32]{0:T(128)} %param.19) | copy-start | bytes 388
  102.1 57.9 %all-to-all-start = ((bf16[16,16,4096]{2,1,0:T(8,128)(2,1)}), bf16[16,16,4096]{2,1,0:T(8,128)(2,1)S(1)}, u32[]{:S(2)}, u32[]{:S(2)}) async-start(bf16[16,16,4096]{2,1,0:T(8,128)(2,1)} %bitcast.103), calls=%async_computation | async-start | bytes 4194304 | tf_op jit(solution)/shard_map/all_to_all | solution.py:200
Sparse Core Ops, SparseCore 0:
  11.0 51.2 all-gather.2
where the time goes:
time: 174 us
  other arithmetic  65.1 us (37%)
  waiting for transfers between devices  33.6 us (19%)
  matrix products  27.4 us (16%)
  blocking collectives  15.8 us (9%)
  between operations  14.4 us (8%)
  starting transfers between devices  10.5 us (6%)
  local copies, waits for them, and re-layouts  7.26 us (4%)
    convert_element_type x2, other arithmetic, dequantize(): return shaped.reshape(levels.shape[0], columns).astype(jnp.bfloat16)  44.8 us
    all_to_all x1, waiting for transfers between devices, shards(): lax.all_to_all(produced, 'ep', split_axis=0, concat_axis=0, tiled=True)  33.5 us
    all_gather x1, blocking collectives, shards(): lax.all_gather(routes.astype(jnp.bfloat16), 'ep', axis=0, tiled=True)  15.8 us
    all_to_all x1, starting transfers between devices, shards(): lax.all_to_all(produced, 'ep', split_axis=0, concat_axis=0, tiled=True)  10.5 us
    and x1, other arithmetic, unpack_columns(): jnp.bitwise_and(jnp.right_shift(packed, 4 * nibble_pos), 15)  6.64 us
    dot_general x1, matrix products, expert_rows(): jnp.dot(expert_in, weight_both, preferred_element_type=jnp.float32)  6.59 us
    dot_general x1, matrix products, expert_rows(): jnp.dot(lowered_hidden, leave_up_map, preferred_element_type=jnp.float32)  4.7 us
    dot_general x1, matrix products, attend(): jnp.einsum('thc,tcx->thx', old_prob, values_all, preferred_element_type=j...  4.08 us
  transfers between devices with their start and end apart: 2, of which 1 were waited for; matrix products, arithmetic and copies ran while one was open for 40% of the time, Pallas kernels for 0%

commit v1 on v0

v1 whole, which is shorter than its diff:
```python
import functools
import math

import jax
import jax.numpy as jnp
from jax import lax
from jax.experimental import pallas as pl
from jax.experimental.pallas import tpu as pltpu
from jax.sharding import PartitionSpec as P

HEADS = 32
KV_HEADS = 2
HEAD = 128
RANK = 16
LANES = 128
GROUP = 64
code_levels = (
    -1.0,
    -0.6961928009986877,
    -0.5250730514526367,
    -0.39491748809814453,
    -0.28444138169288635,
    -0.18477343022823334,
    -0.09105003625154495,
    0.0,
    0.07958029955625534,
    0.16093020141124725,
    0.24611230194568634,
    0.33791524171829224,
    0.44070982933044434,
    0.5626170039176941,
    0.7229568362236023,
    1.0,
)
adapter_scale = 2.0
norm_epsilon = 1e-06
f32 = jnp.float32
bf16 = jnp.bfloat16


def params(mib):
    return pltpu.CompilerParams(vmem_limit_bytes=mib * 2**20)


def whole(shape):
    return pl.BlockSpec(shape, lambda *_: (0,) * len(shape))


def norm_kernel(hidden, gain, routes, scores, out):
    width = hidden.shape[1]
    wide = hidden[...].astype(f32)
    spread = jnp.mean(wide * wide, axis=-1, keepdims=True)
    normed = wide * lax.rsqrt(spread + norm_epsilon) * gain[...].astype(f32)
    out[:, :width] = normed.astype(bf16)
    logits = scores[...]
    parts = jnp.exp(logits - jnp.max(logits, axis=-1, keepdims=True))
    shares = parts / jnp.sum(parts, axis=-1, keepdims=True)
    lane = lax.broadcasted_iota(jnp.int32, (hidden.shape[0], LANES), 1)
    expert = lane & (LANES // 2 - 1)
    table = jnp.zeros(expert.shape, f32)
    for k in range(routes.shape[1]):
        table = table + jnp.where(routes[:, k : k + 1] == expert, shares[:, k : k + 1], 0.0)
    high = table.astype(bf16)
    low = (table - high.astype(f32)).astype(bf16)
    out[:, width:] = jnp.where(lane < LANES // 2, high.astype(f32), low.astype(f32)).astype(bf16)


def norm_rows(hidden, gain, routes, scores):
    rows, width = hidden.shape
    return pl.pallas_call(
        norm_kernel,
        out_shape=jax.ShapeDtypeStruct((rows, width + LANES), bf16),
        compiler_params=params(16),
    )(hidden, gain.reshape(1, width), routes, scores)


def level_tables():
    sub = lax.broadcasted_iota(jnp.int32, (8, LANES), 0)
    low = jnp.zeros((8, LANES), f32)
    high = low
    for i in range(8):
        low = jnp.where(sub == i, code_levels[i], low)
        high = jnp.where(sub == i, code_levels[i + 8], high)
    return low, high


def decode(tables, words, nibble):
    pieces = []
    for q in range(words.shape[0] // 8):
        word = words[8 * q : 8 * q + 8]
        entry = (word >> (4 * nibble)) & 7
        upper = (word & (8 << (4 * nibble))) != 0
        low = jnp.take_along_axis(tables[0], entry, axis=0, mode="promise_in_bounds")
        high = jnp.take_along_axis(tables[1], entry, axis=0, mode="promise_in_bounds")
        pieces.append(jnp.where(upper, high, low))
    return jnp.concatenate(pieces, axis=0)


def enter_kernel(codes, scale, down_map, up_map, out):
    tables = level_tables()
    rows, third = codes.shape
    half = out.shape[0] * LANES
    for tile in range(out.shape[0]):
        adapter = jnp.dot(down_map[...], up_map[tile], preferred_element_type=f32)
        for side in range(2):
            column = side * half + tile * LANES
            nibble, offset = divmod(column, third)
            for g in range(rows // GROUP):
                words = codes[pl.ds(g * GROUP, GROUP), pl.ds(offset, LANES)]
                factor = scale[0, pl.ds(g, 1), pl.ds(column, LANES)].astype(f32)
                value = decode(tables, words, nibble) * factor
                value = value + adapter[g * GROUP : (g + 1) * GROUP, side * LANES : (side + 1) * LANES]
                out[tile, pl.ds(g * GROUP, GROUP), pl.ds(side * LANES, LANES)] = value.astype(bf16)


def enter_weights(codes, scale, down_map, up_map, block=512):
    width, third = codes.shape
    columns = 3 * third
    half = columns // 2
    tiles = half // LANES
    wide = (adapter_scale * up_map.astype(f32)).astype(bf16).reshape(2, RANK, tiles, LANES)
    spread = jnp.zeros((tiles, 2, RANK, 2, LANES), bf16)
    spread = spread.at[:, 0, :, 0].set(wide[0].transpose(1, 0, 2))
    spread = spread.at[:, 1, :, 1].set(wide[1].transpose(1, 0, 2))
    spread = spread.reshape(tiles, 2 * RANK, 2 * LANES)
    return pl.pallas_call(
        enter_kernel,
        grid=(width // block,),
        in_specs=[
            pl.BlockSpec((block, third), lambda i: (i, 0)),
            pl.BlockSpec((1, block // GROUP, columns), lambda i: (i, 0, 0)),
            pl.BlockSpec((block, 2 * RANK), lambda i: (i, 0)),
            whole(spread.shape),
        ],
        out_specs=pl.BlockSpec((tiles, block, 2 * LANES), lambda i: (0, i, 0)),
        out_shape=jax.ShapeDtypeStruct((tiles, width, 2 * LANES), bf16),
        compiler_params=params(40),
        cost_estimate=pl.CostEstimate(flops=4 * 10**9, bytes_accessed=40 * 10**6, transcendentals=0),
    )(codes, scale.reshape(width // block, block // GROUP, columns), down_map, spread)


def leave_kernel(codes, scale, down_map, up_map, out):
    tables = level_tables()
    rows, columns = codes.shape
    adapter = jnp.dot(down_map[...], up_map[...], preferred_element_type=f32) * adapter_scale
    for j in range(columns // LANES):
        lanes = pl.ds(j * LANES, LANES)
        for nibble in range(3):
            for g in range(rows // GROUP):
                row = nibble * rows + g * GROUP
                words = codes[pl.ds(g * GROUP, GROUP), lanes]
                factor = scale[pl.ds(row // GROUP, 1), lanes].astype(f32)
                value = decode(tables, words, nibble) * factor
                value = value + adapter[row : row + GROUP, j * LANES : (j + 1) * LANES]
                out[pl.ds(row, GROUP), lanes] = value.astype(bf16)


def leave_weights(codes, scale, down_map, up_map, block=512):
    third, width = codes.shape
    rows = 3 * third
    return pl.pallas_call(
        leave_kernel,
        grid=(width // block,),
        in_specs=[
            pl.BlockSpec((third, block), lambda i: (0, i)),
            pl.BlockSpec((rows // GROUP, block), lambda i: (0, i)),
            whole((rows, RANK)),
            pl.BlockSpec((RANK, block), lambda i: (0, i)),
        ],
        out_specs=pl.BlockSpec((rows, block), lambda i: (0, i)),
        out_shape=jax.ShapeDtypeStruct((rows, width), bf16),
        compiler_params=params(40),
        cost_estimate=pl.CostEstimate(flops=2 * 10**9, bytes_accessed=20 * 10**6, transcendentals=0),
    )(codes, scale, down_map, up_map)


def expert_kernel(count, tiles, own, *refs):
    blocks = refs[:count]
    enter, leave = refs[count : count + 2]
    outs = refs[count + 2 : 2 * count + 2]
    rows_all, weight, active = refs[2 * count + 2 :]
    step = pl.program_id(0)
    rows = blocks[0].shape[0]
    width = rows_all.shape[1]

    @pl.when(step == 0)
    def _():
        lane = lax.broadcasted_iota(jnp.int32, (rows, LANES), 1)
        mine = (lane & (LANES // 2 - 1)) == own[0]
        for b in range(count):
            here = pl.ds(b * rows, rows)
            rows_all[here, :] = blocks[b][:, :width]
            table = jnp.where(mine, blocks[b][:, width:].astype(f32), 0.0)
            weight[here, :] = jnp.broadcast_to(jnp.sum(table, axis=-1, keepdims=True), (rows, LANES))

    @pl.when(step < tiles)
    def _():
        joined = jnp.dot(rows_all[...], enter[0], preferred_element_type=f32)
        gate = joined[:, :LANES]
        value = gate / (1.0 + jnp.exp(-gate)) * joined[:, LANES:]
        active[step] = value.astype(bf16)

    @pl.when(step >= tiles)
    def _():
        entry = jnp.concatenate([active[t] for t in range(tiles)], axis=1)
        for n in range(leave.shape[1] // 256):
            lanes = pl.ds(n * 256, 256)
            result = jnp.dot(entry, leave[:, lanes], preferred_element_type=f32)
            factor = jnp.concatenate([weight[...], weight[...]], axis=1)
            result = (result * factor).astype(bf16)
            for b in range(count):
                outs[b][:, lanes] = result[b * rows : (b + 1) * rows]


def expert(own, blocks, enter, leave, column_block=1024):
    count = len(blocks)
    rows, padded = blocks[0].shape
    width = padded - LANES
    tiles = enter.shape[0]
    steps = width // column_block
    total = count * rows
    return pl.pallas_call(
        functools.partial(expert_kernel, count, tiles),
        grid=(tiles + steps,),
        in_specs=[pl.BlockSpec(memory_space=pltpu.SMEM)]
        + [whole((rows, padded))] * count
        + [
            pl.BlockSpec((1, width, 2 * LANES), lambda i: (jnp.minimum(i, tiles - 1), 0, 0)),
            pl.BlockSpec((leave.shape[0], column_block), lambda i: (0, jnp.maximum(i - tiles, 0))),
        ],
        out_specs=[pl.BlockSpec((rows, column_block), lambda i: (0, jnp.maximum(i - tiles, 0)))] * count,
        out_shape=[jax.ShapeDtypeStruct((rows, width), bf16)] * count,
        scratch_shapes=[
            pltpu.VMEM((total, width), bf16),
            pltpu.VMEM((total, LANES), f32),
            pltpu.VMEM((tiles, total, LANES), bf16),
        ],
        compiler_params=params(50),
        cost_estimate=pl.CostEstimate(flops=10**10, bytes_accessed=28 * 10**6, transcendentals=0),
    )(own, *blocks, enter, leave)


def attend_kernel(lengths, queries, fresh, cache, out):
    first = pl.program_id(0) * queries.shape[0]
    scaling = 1.0 / math.sqrt(HEAD)
    positions = cache.shape[2]
    head = lax.broadcasted_iota(jnp.int32, (HEADS, HEAD), 0)
    upper = head < HEADS // KV_HEADS
    place = lax.broadcasted_iota(jnp.int32, (HEADS, positions), 1)
    for t in range(queries.shape[0]):
        query = queries[t]
        zero = jnp.zeros_like(query)
        spread = jnp.concatenate([jnp.where(upper, query, zero), jnp.where(upper, zero, query)], axis=1)
        old = lax.dot_general(
            spread, cache[t, 0], (((1,), (1,)), ((), ())), preferred_element_type=f32
        ) * scaling
        old = jnp.where(place < lengths[first + t], old, -jnp.inf)
        new_key = fresh[t, 0:1, :].astype(f32)
        new = jnp.sum(spread.astype(f32) * new_key, axis=-1, keepdims=True) * scaling
        highest = jnp.maximum(jnp.max(old, axis=-1, keepdims=True), new)
        old_exp = jnp.exp(old - highest)
        new_exp = jnp.exp(new - highest)
        denominator = jnp.sum(old_exp, axis=-1, keepdims=True) + new_exp
        old_prob = (old_exp / denominator).astype(bf16)
        new_prob = (new_exp / denominator).astype(bf16).astype(f32)
        blended = jnp.dot(old_prob, cache[t, 1], preferred_element_type=f32)
        blended = blended + new_prob * fresh[t, 1:2, :].astype(f32)
        out[t] = jnp.where(upper, blended[:, :HEAD], blended[:, HEAD:]).astype(bf16)


def attend(queries, fresh_key_value, key_value_cache, lengths, block=8):
    rows = queries.shape[0]
    positions, width = key_value_cache.shape[2:]
    context = pl.pallas_call(
        attend_kernel,
        grid_spec=pltpu.PrefetchScalarGridSpec(
            num_scalar_prefetch=1,
            grid=(rows // block,),
            in_specs=[
                pl.BlockSpec((block, HEADS, HEAD), lambda i, _: (i, 0, 0)),
                pl.BlockSpec((block, 2, width), lambda i, _: (i, 0, 0)),
                pl.BlockSpec((block, 2, positions, width), lambda i, _: (i, 0, 0, 0)),
            ],
            out_specs=pl.BlockSpec((block, HEADS, HEAD), lambda i, _: (i, 0, 0)),
        ),
        out_shape=jax.ShapeDtypeStruct((rows, HEADS, HEAD), bf16),
        compiler_params=params(32),
        cost_estimate=pl.CostEstimate(flops=5 * 10**8, bytes_accessed=20 * 10**6, transcendentals=0),
    )(lengths, queries.reshape(rows, HEADS, HEAD), fresh_key_value, key_value_cache)
    return context.reshape(rows, HEADS * HEAD)


def swap(value, bit):
    count = lax.axis_size("ep")
    return lax.ppermute(value, "ep", [(i, i ^ bit) for i in range(count)])


def add(terms):
    return sum(term.astype(f32) for term in terms[1:]) + terms[0].astype(f32)


def shards(
    queries,
    fresh_key_value,
    key_value_cache,
    lengths,
    hidden,
    expert_norm_gain,
    routes,
    router_scores,
    gate_up_quant_codes,
    gate_up_code_scale,
    down_quant_codes,
    down_code_scale,
    adapter_input_down,
    adapter_input_up,
    adapter_output_down,
    adapter_output_up,
):
    count = lax.axis_size("ep")
    bits = [1 << b for b in range(count.bit_length() - 1)]
    blocks = {0: norm_rows(hidden, expert_norm_gain, routes, router_scores)}
    for bit in reversed(bits):
        for r in list(blocks):
            blocks[r | bit] = swap(blocks[r], bit)
    enter = enter_weights(
        gate_up_quant_codes[0], gate_up_code_scale[0], adapter_input_down[0], adapter_input_up[0]
    )
    leave = leave_weights(
        down_quant_codes[0], down_code_scale[0], adapter_output_down[0], adapter_output_up[0]
    )
    own = lax.axis_index("ep").astype(jnp.int32).reshape(1)
    produced = expert(own, [blocks[r] for r in range(count)], enter, leave)
    sums = {r: [produced[r]] for r in range(count)}
    for bit in bits:
        for r in sorted(sums, reverse=True):
            if r & bit:
                sums[r ^ bit].append(swap(add(sums.pop(r)).astype(bf16), bit))
    context = attend(queries, fresh_key_value, key_value_cache, lengths)
    return (context, add(sums[0]).astype(bf16))


def solution(mesh):
    return jax.shard_map(
        shards,
        mesh=mesh,
        in_specs=(
            P(("grp", "ep"), None),
            P(("grp", "ep"), None, None),
            P(("grp", "ep"), None, None, None),
            P(("grp", "ep")),
            P(("grp", "ep"), None),
            P(),
            P(("grp", "ep"), None),
            P(("grp", "ep"), None),
            P("ep", None, None),
            P("ep", None, None),
            P("ep", None, None),
            P("ep", None, None),
            P("ep", None, None),
            P("ep", None, None, None),
            P("ep", None, None),
            P("ep", None, None),
        ),
        out_specs=(P(("grp", "ep"), None), P(("grp", "ep"), None)),
        check_vma=False,
    )
```

time: 174 us -> 143 us (0.82)
  the two profiles are of different devices: /device:TPU:13 before, /device:TPU:0 now
where the time goes in v1:
time: 143 us
  Pallas kernels  52.8 us (37%)
  waiting for transfers between devices  50.1 us (35%)
  starting transfers between devices  21.6 us (15%)
  local copies, waits for them, and re-layouts  15.1 us (11%)
  other arithmetic  2.26 us (2%)
    ppermute x30, waiting for transfers between devices, swap(): return lax.ppermute(value, 'ep', [(i, i ^ bit) for i in range(count)])  50.1 us
    ppermute x30, starting transfers between devices, swap(): return lax.ppermute(value, 'ep', [(i, i ^ bit) for i in range(count)])  21.6 us
    pallas_call x1, Pallas kernels, expert(): pl.pallas_call(functools.partial(expert_kernel, count, tiles), grid=(tile...  18.6 us
    unnamed x46, local copies, waits for them, and re-layouts  14.1 us
    pallas_call x1, Pallas kernels, enter_weights(): pl.pallas_call(enter_kernel, grid=(width // block,), in_specs=[pl.BlockSp...  13.1 us
    pallas_call x1, Pallas kernels, attend(): pl.pallas_call(attend_kernel, grid_spec=pltpu.PrefetchScalarGridSpec(num_...  13.1 us
    pallas_call x1, Pallas kernels, leave_weights(): pl.pallas_call(leave_kernel, grid=(width // block,), in_specs=[pl.BlockSp...  7.53 us
  transfers between devices with their start and end apart: 30, of which 11 were waited for; matrix products, arithmetic and copies ran while one was open for 3% of the time, Pallas kernels for 24%

profile of v1, /device:TPU:0, one launch (start us, length us, event | category | flops | bytes accessed | tf_op | source)
XLA Modules:
  0.0 142.8 jit_solution(2505457745709702830)
XLA Ops:
  0.6 0.8 copy.24.routes
  1.4 0.8 copy.25.scores
  2.9 0.9 copy-done.4
  4.2 4.1 %collective-permute-start.7 = (bf16[32,4224]{1,0:T(8,128)(2,1)S(1)}, bf16[32,4224]{1,0:T(8,128)(2,1)S(1)}, u32[]{:S(2)}, u32[]{:S(2)}) collective-permute-start(bf16[32,4224]{1,0:T(8,128)(2,1)S(1)} %shard_map.168.refs_0_), channel_id=1, source_target_pairs={{0,8},{1,9},{2,10},{3,11},{4,12},{5,13},{6,14},{7,15},{8,0},{9,1},... | collective-permute-start | bytes 811016 | tf_op jit(solution)/shard_map/ppermute | solution.py:295
  8.3 1.6 %collective-permute-start.3 = (bf16[32,4224]{1,0:T(8,128)(2,1)S(1)}, bf16[32,4224]{1,0:T(8,128)(2,1)S(1)}, u32[]{:S(2)}, u32[]{:S(2)}) collective-permute-start(bf16[32,4224]{1,0:T(8,128)(2,1)S(1)} %shard_map.168.refs_0_), channel_id=1, source_target_pairs={{0,4},{1,5},{2,6},{3,7},{4,0},{5,1},{6,2},{7,3},{8,12},{9,13},{10,... | collective-permute-start | bytes 811016 | tf_op jit(solution)/shard_map/ppermute | solution.py:295
  9.8 1.5 %collective-permute-start.1 = (bf16[32,4224]{1,0:T(8,128)(2,1)S(1)}, bf16[32,4224]{1,0:T(8,128)(2,1)S(1)}, u32[]{:S(2)}, u32[]{:S(2)}) collective-permute-start(bf16[32,4224]{1,0:T(8,128)(2,1)S(1)} %shard_map.168.refs_0_), channel_id=1, source_target_pairs={{0,2},{1,3},{2,0},{3,1},{4,6},{5,7},{6,4},{7,5},{8,10},{9,11},{10,... | collective-permute-start | bytes 811016 | tf_op jit(solution)/shard_map/ppermute | solution.py:295
  11.4 9.3 %collective-permute-done.7.refs_8_ = bf16[32,4224]{1,0:T(8,128)(2,1)S(1)} collective-permute-done((bf16[32,4224]{1,0:T(8,128)(2,1)S(1)}, bf16[32,4224]{1,0:T(8,128)(2,1)S(1)}, u32[]{:S(2)}, u32[]{:S(2)}) %collective-permute-start.7) | collective-permute-done | bytes 270368 | tf_op jit(solution)/shard_map/ppermute | solution.py:295
  21.3 0.8 multiply_convert_fusion
  22.1 1.6 %collective-permute-start.9 = (bf16[32,4224]{1,0:T(8,128)(2,1)S(1)}, bf16[32,4224]{1,0:T(8,128)(2,1)S(1)}, u32[]{:S(2)}, u32[]{:S(2)}) collective-permute-start(bf16[32,4224]{1,0:T(8,128)(2,1)S(1)} %collective-permute-done.7.refs_8_), channel_id=1, source_target_pairs={{0,2},{1,3},{2,0},{3,1},{4,6},{5,7},{6,4},{7,5},{8,10},{9,11},{10,... | collective-permute-start | bytes 811016 | tf_op jit(solution)/shard_map/ppermute | solution.py:295
  24.4 3.8 %collective-permute-done.11.refs_12_ = bf16[32,4224]{1,0:T(8,128)(2,1)S(1)} collective-permute-done((bf16[32,4224]{1,0:T(8,128)(2,1)S(1)}, bf16[32,4224]{1,0:T(8,128)(2,1)S(1)}, u32[]{:S(2)}, u32[]{:S(2)}) %collective-permute-start.11) | collective-permute-done | bytes 270368 | tf_op jit(solution)/shard_map/ppermute | solution.py:295
  28.3 1.3 collective-permute-start.13
  29.9 1.4 copy.26
  31.5 5.9 %collective-permute-done.5.refs_6_ = bf16[32,4224]{1,0:T(8,128)(2,1)} collective-permute-done((bf16[32,4224]{1,0:T(8,128)(2,1)S(1)}, bf16[32,4224]{1,0:T(8,128)(2,1)}, u32[]{:S(2)}, u32[]{:S(2)}) %collective-permute-start.5) | collective-permute-done | bytes 270368 | tf_op jit(solution)/shard_map/ppermute | solution.py:295
  38.0 3.9 %collective-permute-done.13.refs_14_ = bf16[32,4224]{1,0:T(8,128)(2,1)} collective-permute-done((bf16[32,4224]{1,0:T(8,128)(2,1)S(1)}, bf16[32,4224]{1,0:T(8,128)(2,1)}, u32[]{:S(2)}, u32[]{:S(2)}) %collective-permute-start.13) | collective-permute-done | bytes 270368 | tf_op jit(solution)/shard_map/ppermute | solution.py:295
  42.0 3.4 %copy-done = s32[1,4096,512]{2,1,0:T(8,128)S(1)} copy-done((s32[1,4096,512]{2,1,0:T(8,128)S(1)}, s32[1,4096,512]{2,1,0:T(8,128)}, u32[]{:S(2)}) %copy-start) | copy-done | bytes 8388632
  45.3 0.9 copy-done.5
  46.3 13.1 %shard_map.169.refs_16_ = bf16[6,4096,256]{2,1,0:T(8,128)(2,1)} custom-call(s32[4096,512]{1,0:T(8,128)S(1)} %bitcast.25, bf16[8,8,1536]{2,1,0:T(8,128)(2,1)S(1)} %bitcast.33, bf16[4096,32]{1,0:T(8,128)(2,1)S(1)} %bitcast.28, bf16[6,32,256]{2,1,0:T(8,128)(2,1)S(1)} %reshape.126.up_map), custom_call_target="tpu_custom_call" | custom-call | flops 4000000000 | bytes 40000000 | tf_op jit(solution)/shard_map/pallas_call | solution.py:126
  59.7 2.2 %copy-done.2 = s32[1,256,4096]{2,1,0:T(8,128)S(1)} copy-done((s32[1,256,4096]{2,1,0:T(8,128)S(1)}, s32[1,256,4096]{2,1,0:T(8,128)}, u32[]{:S(2)}) %copy-start.2) | copy-done | bytes 4194328
  61.9 7.5 %shard_map.170.refs_17_ = bf16[768,4096]{1,0:T(8,128)(2,1)S(1)} custom-call(s32[256,4096]{1,0:T(8,128)S(1)} %bitcast.29, bf16[12,4096]{1,0:T(8,128)(2,1)S(1)} %bitcast.34, bf16[768,16]{1,0:T(8,128)(2,1)S(1)} %bitcast.32, bf16[16,4096]{1,0:T(8,128)(2,1)S(1)} %bitcast.35), custom_call_target="tpu_custom_call" | custom-call | flops 2000000000 | bytes 20000000 | tf_op jit(solution)/shard_map/pallas_call | solution.py:161
  69.4 2.6 %copy-done.1 = bf16[768,4096]{1,0:T(8,128)(2,1)} copy-done((bf16[768,4096]{1,0:T(8,128)(2,1)}, bf16[768,4096]{1,0:T(8,128)(2,1)S(1)}, u32[]{:S(2)}) %copy-start.1) | copy-done | bytes 6291480
  72.1 18.6 %shard_map.171 = (bf16[32,4096]{1,0:T(8,128)(2,1)S(1)}, bf16[32,4096]{1,0:T(8,128)(2,1)S(1)}, bf16[32,4096]{1,0:T(8,128)(2,1)S(1)}, bf16[32,4096]{1,0:T(8,128)(2...) custom-call(s32[1]{0:T(128)} %bitcast.own, ...), custom_call_target="tpu_custom_call" | custom-call | flops 10000000000 | bytes 28000000 | tf_op jit(solution)/shard_map/pallas_call | solution.py:222
  93.3 0.9 collective-permute-done.26
  94.6 1.5 %collective-permute-start.27 = (bf16[32,4096]{1,0:T(8,128)(2,1)S(1)}, bf16[32,4096]{1,0:T(8,128)(2,1)S(1)}, u32[]{:S(2)}, u32[]{:S(2)}) collective-permute-start(bf16[32,4096]{1,0:T(8,128)(2,1)S(1)} %add_convert_fusion.3), channel_id=1, source_target_pairs={{0,2},{1,3},{2,0},{3,1},{4,6},{5,7},{6,4},{7,5},{8,10},{9,11},{10,... | collective-permute-start | bytes 786440 | tf_op jit(solution)/shard_map/ppermute | solution.py:295
  96.8 7.0 %collective-permute-done.27 = bf16[32,4096]{1,0:T(8,128)(2,1)S(1)} collective-permute-done((bf16[32,4096]{1,0:T(8,128)(2,1)S(1)}, bf16[32,4096]{1,0:T(8,128)(2,1)S(1)}, u32[]{:S(2)}, u32[]{:S(2)}) %collective-permute-start.27) | collective-permute-done | bytes 262176 | tf_op jit(solution)/shard_map/ppermute | solution.py:295
  103.8 1.5 %collective-permute-start.20 = (bf16[32,4096]{1,0:T(8,128)(2,1)S(1)}, bf16[32,4096]{1,0:T(8,128)(2,1)S(1)}, u32[]{:S(2)}, u32[]{:S(2)}) collective-permute-start(bf16[32,4096]{1,0:T(8,128)(2,1)S(1)} %add_convert_fusion.6), channel_id=1, source_target_pairs={{0,2},{1,3},{2,0},{3,1},{4,6},{5,7},{6,4},{7,5},{8,10},{9,11},{10,... | collective-permute-start | bytes 786440 | tf_op jit(solution)/shard_map/ppermute | solution.py:295
  106.0 9.0 %collective-permute-done.20 = bf16[32,4096]{1,0:T(8,128)(2,1)S(1)} collective-permute-done((bf16[32,4096]{1,0:T(8,128)(2,1)S(1)}, bf16[32,4096]{1,0:T(8,128)(2,1)S(1)}, u32[]{:S(2)}, u32[]{:S(2)}) %collective-permute-start.20) | collective-permute-done | bytes 262176 | tf_op jit(solution)/shard_map/ppermute | solution.py:295
  115.7 1.5 %collective-permute-start.21 = (bf16[32,4096]{1,0:T(8,128)(2,1)S(1)}, bf16[32,4096]{1,0:T(8,128)(2,1)S(1)}, u32[]{:S(2)}, u32[]{:S(2)}) collective-permute-start(bf16[32,4096]{1,0:T(8,128)(2,1)S(1)} %add_convert_fusion.5), channel_id=1, source_target_pairs={{0,4},{1,5},{2,6},{3,7},{4,0},{5,1},{6,2},{7,3},{8,12},{9,13},{10,... | collective-permute-start | bytes 786440 | tf_op jit(solution)/shard_map/ppermute | solution.py:295
  117.3 2.6 %collective-permute-done.24 = bf16[32,4096]{1,0:T(8,128)(2,1)S(1)} collective-permute-done((bf16[32,4096]{1,0:T(8,128)(2,1)S(1)}, bf16[32,4096]{1,0:T(8,128)(2,1)S(1)}, u32[]{:S(2)}, u32[]{:S(2)}) %collective-permute-start.24) | collective-permute-done | bytes 262176 | tf_op jit(solution)/shard_map/ppermute | solution.py:295
  119.9 7.2 %collective-permute-done.28 = bf16[32,4096]{1,0:T(8,128)(2,1)S(1)} collective-permute-done((bf16[32,4096]{1,0:T(8,128)(2,1)S(1)}, bf16[32,4096]{1,0:T(8,128)(2,1)S(1)}, u32[]{:S(2)}, u32[]{:S(2)}) %collective-permute-start.28) | collective-permute-done | bytes 262176 | tf_op jit(solution)/shard_map/ppermute | solution.py:295
  128.0 13.1 %shard_map.167 = bf16[32,32,128]{2,1,0:T(8,128)(2,1)S(1)} custom-call(s32[32]{0:T(128)S(1)} %copy-done.9, bf16[32,32,128]{2,1,0:T(8,128)(2,1)S(1)} %bitcast.31, bf16[32,2,256]{2,1,0:T(2,128)(2,1)S(1)} %copy-done.8, bf16[32,2,256,256]{3,2,1,0:T(8,128)(2,1)S(1)} %bitcast.27), custom_call_target="tpu_custom_call" | custom-call | flops 500000000 | bytes 20000000 | tf_op jit(solution)/shard_map/pallas_call | solution.py:274
  141.1 0.8 copy.36
  141.9 0.9 add_convert_fusion
  (98 shorter events, 9.6 us)
Async XLA Ops:
  4.2 16.5 %collective-permute-start.7 = (bf16[32,4224]{1,0:T(8,128)(2,1)S(1)}, bf16[32,4224]{1,0:T(8,128)(2,1)S(1)}, u32[]{:S(2)}, u32[]{:S(2)}) collective-permute-start(bf16[32,4224]{1,0:T(8,128)(2,1)S(1)} %shard_map.168.refs_0_), channel_id=1, source_target_pairs={{0,8},{1,9},{2,10},{3,11},{4,12},{5,13},{6,14},{7,15},{8,0},{9,1},... | collective-permute-start | bytes 811016 | tf_op jit(solution)/shard_map/ppermute | solution.py:295
  8.3 15.4 %collective-permute-start.3 = (bf16[32,4224]{1,0:T(8,128)(2,1)S(1)}, bf16[32,4224]{1,0:T(8,128)(2,1)S(1)}, u32[]{:S(2)}, u32[]{:S(2)}) collective-permute-start(bf16[32,4224]{1,0:T(8,128)(2,1)S(1)} %shard_map.168.refs_0_), channel_id=1, source_target_pairs={{0,4},{1,5},{2,6},{3,7},{4,0},{5,1},{6,2},{7,3},{8,12},{9,13},{10,... | collective-permute-start | bytes 811016 | tf_op jit(solution)/shard_map/ppermute | solution.py:295
  9.8 13.8 %collective-permute-start.1 = (bf16[32,4224]{1,0:T(8,128)(2,1)S(1)}, bf16[32,4224]{1,0:T(8,128)(2,1)S(1)}, u32[]{:S(2)}, u32[]{:S(2)}) collective-permute-start(bf16[32,4224]{1,0:T(8,128)(2,1)S(1)} %shard_map.168.refs_0_), channel_id=1, source_target_pairs={{0,2},{1,3},{2,0},{3,1},{4,6},{5,7},{6,4},{7,5},{8,10},{9,11},{10,... | collective-permute-start | bytes 811016 | tf_op jit(solution)/shard_map/ppermute | solution.py:295
  11.4 12.9 %collective-permute-start = (bf16[32,4224]{1,0:T(8,128)(2,1)S(1)}, bf16[32,4224]{1,0:T(8,128)(2,1)S(1)}, u32[]{:S(2)}, u32[]{:S(2)}) collective-permute-start(bf16[32,4224]{1,0:T(8,128)(2,1)S(1)} %shard_map.168.refs_0_), channel_id=1, source_target_pairs={{0,1},{1,0},{2,3},{3,2},{4,5},{5,4},{6,7},{7,6},{8,9},{9,8},{10,11... | collective-permute-start | bytes 811016 | tf_op jit(solution)/shard_map/ppermute | solution.py:295
  20.6 7.6 %collective-permute-start.11 = (bf16[32,4224]{1,0:T(8,128)(2,1)S(1)}, bf16[32,4224]{1,0:T(8,128)(2,1)S(1)}, u32[]{:S(2)}, u32[]{:S(2)}) collective-permute-start(bf16[32,4224]{1,0:T(8,128)(2,1)S(1)} %collective-permute-done.7.refs_8_), channel_id=1, source_target_pairs={{0,4},{1,5},{2,6},{3,7},{4,0},{5,1},{6,2},{7,3},{8,12},{9,13},{10,... | collective-permute-start | bytes 811016 | tf_op jit(solution)/shard_map/ppermute | solution.py:295
  22.1 9.5 %collective-permute-start.9 = (bf16[32,4224]{1,0:T(8,128)(2,1)S(1)}, bf16[32,4224]{1,0:T(8,128)(2,1)S(1)}, u32[]{:S(2)}, u32[]{:S(2)}) collective-permute-start(bf16[32,4224]{1,0:T(8,128)(2,1)S(1)} %collective-permute-done.7.refs_8_), channel_id=1, source_target_pairs={{0,2},{1,3},{2,0},{3,1},{4,6},{5,7},{6,4},{7,5},{8,10},{9,11},{10,... | collective-permute-start | bytes 811016 | tf_op jit(solution)/shard_map/ppermute | solution.py:295
  23.7 13.8 %collective-permute-start.8 = (bf16[32,4224]{1,0:T(8,128)(2,1)S(1)}, bf16[32,4224]{1,0:T(8,128)(2,1)}, u32[]{:S(2)}, u32[]{:S(2)}) collective-permute-start(bf16[32,4224]{1,0:T(8,128)(2,1)S(1)} %collective-permute-done.7.refs_8_), channel_id=1, source_target_pairs={{0,1},{1,0},{2,3},{3,2},{4,5},{5,4},{6,7},{7,6},{8,9},{9,8},{10,11... | collective-permute-start | bytes 811016 | tf_op jit(solution)/shard_map/ppermute | solution.py:295
  23.7 13.7 %collective-permute-start.5 = (bf16[32,4224]{1,0:T(8,128)(2,1)S(1)}, bf16[32,4224]{1,0:T(8,128)(2,1)}, u32[]{:S(2)}, u32[]{:S(2)}) collective-permute-start(bf16[32,4224]{1,0:T(8,128)(2,1)S(1)} %collective-permute-done.3.refs_4_), channel_id=1, source_target_pairs={{0,2},{1,3},{2,0},{3,1},{4,6},{5,7},{6,4},{7,5},{8,10},{9,11},{10,... | collective-permute-start | bytes 811016 | tf_op jit(solution)/shard_map/ppermute | solution.py:295
  24.3 13.7 %collective-permute-start.4 = (bf16[32,4224]{1,0:T(8,128)(2,1)S(1)}, bf16[32,4224]{1,0:T(8,128)(2,1)}, u32[]{:S(2)}, u32[]{:S(2)}) collective-permute-start(bf16[32,4224]{1,0:T(8,128)(2,1)S(1)} %collective-permute-done.3.refs_4_), channel_id=1, source_target_pairs={{0,1},{1,0},{2,3},{3,2},{4,5},{5,4},{6,7},{7,6},{8,9},{9,8},{10,11... | collective-permute-start | bytes 811016 | tf_op jit(solution)/shard_map/ppermute | solution.py:295
  28.3 13.7 %collective-permute-start.13 = (bf16[32,4224]{1,0:T(8,128)(2,1)S(1)}, bf16[32,4224]{1,0:T(8,128)(2,1)}, u32[]{:S(2)}, u32[]{:S(2)}) collective-permute-start(bf16[32,4224]{1,0:T(8,128)(2,1)S(1)} %collective-permute-done.11.refs_12_), channel_id=1, source_target_pairs={{0,2},{1,3},{2,0},{3,1},{4,6},{5,7},{6,4},{7,5},{8,10},{9,11},{10,... | collective-permute-start | bytes 811016 | tf_op jit(solution)/shard_map/ppermute | solution.py:295
  31.5 40.5 %collective-permute-start.2 = (bf16[32,4224]{1,0:T(8,128)(2,1)S(1)}, bf16[32,4224]{1,0:T(8,128)(2,1)}, u32[]{:S(2)}, u32[]{:S(2)}) collective-permute-start(bf16[32,4224]{1,0:T(8,128)(2,1)S(1)} %collective-permute-done.1.refs_2_), channel_id=1, source_target_pairs={{0,1},{1,0},{2,3},{3,2},{4,5},{5,4},{6,7},{7,6},{8,9},{9,8},{10,11... | collective-permute-start | bytes 811016 | tf_op jit(solution)/shard_map/ppermute | solution.py:295
  37.4 34.6 %collective-permute-start.12 = (bf16[32,4224]{1,0:T(8,128)(2,1)S(1)}, bf16[32,4224]{1,0:T(8,128)(2,1)}, u32[]{:S(2)}, u32[]{:S(2)}) collective-permute-start(bf16[32,4224]{1,0:T(8,128)(2,1)S(1)} %collective-permute-done.11.refs_12_), channel_id=1, source_target_pairs={{0,1},{1,0},{2,3},{3,2},{4,5},{5,4},{6,7},{7,6},{8,9},{9,8},{10,11... | collective-permute-start | bytes 811016 | tf_op jit(solution)/shard_map/ppermute | solution.py:295
  37.4 34.6 %collective-permute-start.10 = (bf16[32,4224]{1,0:T(8,128)(2,1)S(1)}, bf16[32,4224]{1,0:T(8,128)(2,1)}, u32[]{:S(2)}, u32[]{:S(2)}) collective-permute-start(bf16[32,4224]{1,0:T(8,128)(2,1)S(1)} %collective-permute-done.9.refs_10_), channel_id=1, source_target_pairs={{0,1},{1,0},{2,3},{3,2},{4,5},{5,4},{6,7},{7,6},{8,9},{9,8},{10,11... | collective-permute-start | bytes 811016 | tf_op jit(solution)/shard_map/ppermute | solution.py:295
  37.9 34.1 %collective-permute-start.6 = (bf16[32,4224]{1,0:T(8,128)(2,1)}, bf16[32,4224]{1,0:T(8,128)(2,1)}, u32[]{:S(2)}, u32[]{:S(2)}) collective-permute-start(bf16[32,4224]{1,0:T(8,128)(2,1)} %collective-permute-done.5.refs_6_), channel_id=1, source_target_pairs={{0,1},{1,0},{2,3},{3,2},{4,5},{5,4},{6,7},{7,6},{8,9},{9,8},{10,11... | collective-permute-start | bytes 811016 | tf_op jit(solution)/shard_map/ppermute | solution.py:295
  42.0 30.1 %collective-permute-start.14 = (bf16[32,4224]{1,0:T(8,128)(2,1)}, bf16[32,4224]{1,0:T(8,128)(2,1)}, u32[]{:S(2)}, u32[]{:S(2)}) collective-permute-start(bf16[32,4224]{1,0:T(8,128)(2,1)} %collective-permute-done.13.refs_14_), channel_id=1, source_target_pairs={{0,1},{1,0},{2,3},{3,2},{4,5},{5,4},{6,7},{7,6},{8,9},{9,8},{10,11... | collective-permute-start | bytes 811016 | tf_op jit(solution)/shard_map/ppermute | solution.py:295
  72.0 55.9 %slice-start = ((s8[8388608]{0:T(1024)(128)(4,1)}), s8[4194304]{0:T(1024)(128)(4,1)S(1)}, s32[]{:S(2)}) async-start(s8[8388608]{0:T(1024)(128)(4,1)} %bitcast.26), calls=%async_computation | async-start | bytes 8388608
  72.1 55.9 %slice-start.1 = ((s8[8388608]{0:T(1024)(128)(4,1)}), s8[4194304]{0:T(1024)(128)(4,1)S(1)}, s32[]{:S(2)}) async-start(s8[8388608]{0:T(1024)(128)(4,1)} %bitcast.26), calls=%async_computation.1 | async-start | bytes 8388608
  90.7 1.7 %collective-permute-start.16 = (bf16[32,4096]{1,0:T(8,128)(2,1)S(1)}, bf16[32,4096]{1,0:T(8,128)(2,1)S(1)}, u32[]{:S(2)}, u32[]{:S(2)}) collective-permute-start(bf16[32,4096]{1,0:T(8,128)(2,1)S(1)} %get-tuple-element.43), channel_id=1, source_target_pairs={{0,1},{1,0},{2,3},{3,2},{4,5},{5,4},{6,7},{7,6},{8,9},{9,8},{10,11... | collective-permute-start | bytes 786440 | tf_op jit(solution)/shard_map/ppermute | solution.py:295
  91.3 1.6 %collective-permute-start.19 = (bf16[32,4096]{1,0:T(8,128)(2,1)S(1)}, bf16[32,4096]{1,0:T(8,128)(2,1)S(1)}, u32[]{:S(2)}, u32[]{:S(2)}) collective-permute-start(bf16[32,4096]{1,0:T(8,128)(2,1)S(1)} %get-tuple-element.46), channel_id=1, source_target_pairs={{0,1},{1,0},{2,3},{3,2},{4,5},{5,4},{6,7},{7,6},{8,9},{9,8},{10,11... | collective-permute-start | bytes 786440 | tf_op jit(solution)/shard_map/ppermute | solution.py:295
  91.4 14.0 %collective-permute-start.18 = (bf16[32,4096]{1,0:T(8,128)(2,1)S(1)}, bf16[32,4096]{1,0:T(8,128)(2,1)S(1)}, u32[]{:S(2)}, u32[]{:S(2)}) collective-permute-start(bf16[32,4096]{1,0:T(8,128)(2,1)S(1)} %get-tuple-element.45), channel_id=1, source_target_pairs={{0,1},{1,0},{2,3},{3,2},{4,5},{5,4},{6,7},{7,6},{8,9},{9,8},{10,11... | collective-permute-start | bytes 786440 | tf_op jit(solution)/shard_map/ppermute | solution.py:295
  91.8 2.8 %collective-permute-start.23 = (bf16[32,4096]{1,0:T(8,128)(2,1)S(1)}, bf16[32,4096]{1,0:T(8,128)(2,1)S(1)}, u32[]{:S(2)}, u32[]{:S(2)}) collective-permute-start(bf16[32,4096]{1,0:T(8,128)(2,1)S(1)} %get-tuple-element.50), channel_id=1, source_target_pairs={{0,1},{1,0},{2,3},{3,2},{4,5},{5,4},{6,7},{7,6},{8,9},{9,8},{10,11... | collective-permute-start | bytes 786440 | tf_op jit(solution)/shard_map/ppermute | solution.py:295
  91.9 2.3 %collective-permute-start.26 = (bf16[32,4096]{1,0:T(8,128)(2,1)}, bf16[32,4096]{1,0:T(8,128)(2,1)S(1)}, u32[]{:S(2)}, u32[]{:S(2)}) collective-permute-start(bf16[32,4096]{1,0:T(8,128)(2,1)} %get-tuple-element.53), channel_id=1, source_target_pairs={{0,1},{1,0},{2,3},{3,2},{4,5},{5,4},{6,7},{7,6},{8,9},{9,8},{10,11... | collective-permute-start | bytes 786440 | tf_op jit(solution)/shard_map/ppermute | solution.py:295
  92.4 3.8 %collective-permute-start.25 = (bf16[32,4096]{1,0:T(8,128)(2,1)S(1)}, bf16[32,4096]{1,0:T(8,128)(2,1)S(1)}, u32[]{:S(2)}, u32[]{:S(2)}) collective-permute-start(bf16[32,4096]{1,0:T(8,128)(2,1)S(1)} %get-tuple-element.52), channel_id=1, source_target_pairs={{0,1},{1,0},{2,3},{3,2},{4,5},{5,4},{6,7},{7,6},{8,9},{9,8},{10,11... | collective-permute-start | bytes 786440 | tf_op jit(solution)/shard_map/ppermute | solution.py:295
  92.9 22.8 %collective-permute-start.22 = (bf16[32,4096]{1,0:T(8,128)(2,1)S(1)}, bf16[32,4096]{1,0:T(8,128)(2,1)S(1)}, u32[]{:S(2)}, u32[]{:S(2)}) collective-permute-start(bf16[32,4096]{1,0:T(8,128)(2,1)S(1)} %get-tuple-element.49), channel_id=1, source_target_pairs={{0,1},{1,0},{2,3},{3,2},{4,5},{5,4},{6,7},{7,6},{8,9},{9,8},{10,11... | collective-permute-start | bytes 786440 | tf_op jit(solution)/shard_map/ppermute | solution.py:295
  94.2 47.8 %collective-permute-start.15 = (bf16[32,4096]{1,0:T(8,128)(2,1)S(1)}, bf16[32,4096]{1,0:T(8,128)(2,1)S(1)}, u32[]{:S(2)}, u32[]{:S(2)}) collective-permute-start(bf16[32,4096]{1,0:T(8,128)(2,1)S(1)} %get-tuple-element.42), channel_id=1, source_target_pairs={{0,1},{1,0},{2,3},{3,2},{4,5},{5,4},{6,7},{7,6},{8,9},{9,8},{10,11... | collective-permute-start | bytes 786440 | tf_op jit(solution)/shard_map/ppermute | solution.py:295
  94.6 9.2 %collective-permute-start.27 = (bf16[32,4096]{1,0:T(8,128)(2,1)S(1)}, bf16[32,4096]{1,0:T(8,128)(2,1)S(1)}, u32[]{:S(2)}, u32[]{:S(2)}) collective-permute-start(bf16[32,4096]{1,0:T(8,128)(2,1)S(1)} %add_convert_fusion.3), channel_id=1, source_target_pairs={{0,2},{1,3},{2,0},{3,1},{4,6},{5,7},{6,4},{7,5},{8,10},{9,11},{10,... | collective-permute-start | bytes 786440 | tf_op jit(solution)/shard_map/ppermute | solution.py:295
  96.2 45.7 %collective-permute-start.17 = (bf16[32,4096]{1,0:T(8,128)(2,1)S(1)}, bf16[32,4096]{1,0:T(8,128)(2,1)S(1)}, u32[]{:S(2)}, u32[]{:S(2)}) collective-permute-start(bf16[32,4096]{1,0:T(8,128)(2,1)S(1)} %add_convert_fusion.7), channel_id=1, source_target_pairs={{0,2},{1,3},{2,0},{3,1},{4,6},{5,7},{6,4},{7,5},{8,10},{9,11},{10,... | collective-permute-start | bytes 786440 | tf_op jit(solution)/shard_map/ppermute | solution.py:295
  103.8 11.2 %collective-permute-start.20 = (bf16[32,4096]{1,0:T(8,128)(2,1)S(1)}, bf16[32,4096]{1,0:T(8,128)(2,1)S(1)}, u32[]{:S(2)}, u32[]{:S(2)}) collective-permute-start(bf16[32,4096]{1,0:T(8,128)(2,1)S(1)} %add_convert_fusion.6), channel_id=1, source_target_pairs={{0,2},{1,3},{2,0},{3,1},{4,6},{5,7},{6,4},{7,5},{8,10},{9,11},{10,... | collective-permute-start | bytes 786440 | tf_op jit(solution)/shard_map/ppermute | solution.py:295
  105.4 14.5 %collective-permute-start.24 = (bf16[32,4096]{1,0:T(8,128)(2,1)S(1)}, bf16[32,4096]{1,0:T(8,128)(2,1)S(1)}, u32[]{:S(2)}, u32[]{:S(2)}) collective-permute-start(bf16[32,4096]{1,0:T(8,128)(2,1)S(1)} %add_convert_fusion.4), channel_id=1, source_target_pairs={{0,2},{1,3},{2,0},{3,1},{4,6},{5,7},{6,4},{7,5},{8,10},{9,11},{10,... | collective-permute-start | bytes 786440 | tf_op jit(solution)/shard_map/ppermute | solution.py:295
  115.0 12.1 %collective-permute-start.28 = (bf16[32,4096]{1,0:T(8,128)(2,1)S(1)}, bf16[32,4096]{1,0:T(8,128)(2,1)S(1)}, u32[]{:S(2)}, u32[]{:S(2)}) collective-permute-start(bf16[32,4096]{1,0:T(8,128)(2,1)S(1)} %add_convert_fusion.2), channel_id=1, source_target_pairs={{0,4},{1,5},{2,6},{3,7},{4,0},{5,1},{6,2},{7,3},{8,12},{9,13},{10,... | collective-permute-start | bytes 786440 | tf_op jit(solution)/shard_map/ppermute | solution.py:295
  115.7 26.2 %collective-permute-start.21 = (bf16[32,4096]{1,0:T(8,128)(2,1)S(1)}, bf16[32,4096]{1,0:T(8,128)(2,1)S(1)}, u32[]{:S(2)}, u32[]{:S(2)}) collective-permute-start(bf16[32,4096]{1,0:T(8,128)(2,1)S(1)} %add_convert_fusion.5), channel_id=1, source_target_pairs={{0,4},{1,5},{2,6},{3,7},{4,0},{5,1},{6,2},{7,3},{8,12},{9,13},{10,... | collective-permute-start | bytes 786440 | tf_op jit(solution)/shard_map/ppermute | solution.py:295
  127.2 14.7 %collective-permute-start.29 = (bf16[32,4096]{1,0:T(8,128)(2,1)S(1)}, bf16[32,4096]{1,0:T(8,128)(2,1)S(1)}, u32[]{:S(2)}, u32[]{:S(2)}) collective-permute-start(bf16[32,4096]{1,0:T(8,128)(2,1)S(1)} %add_convert_fusion.1), channel_id=1, source_target_pairs={{0,8},{1,9},{2,10},{3,11},{4,12},{5,13},{6,14},{7,15},{8,0},{9,1},... | collective-permute-start | bytes 786440 | tf_op jit(solution)/shard_map/ppermute | solution.py:295
  (18 other events, 477.5 us)

commit v2 on v1

v2 whole, which is shorter than its diff:
```python
import functools
import math

import jax
import jax.numpy as jnp
from jax import lax
from jax.experimental import pallas as pl
from jax.experimental.pallas import tpu as pltpu
from jax.sharding import PartitionSpec as P

HEADS = 32
KV_HEADS = 2
HEAD = 128
RANK = 16
LANES = 128
GROUP = 64
BLOCK = 512
code_levels = (
    -1.0,
    -0.6961928009986877,
    -0.5250730514526367,
    -0.39491748809814453,
    -0.28444138169288635,
    -0.18477343022823334,
    -0.09105003625154495,
    0.0,
    0.07958029955625534,
    0.16093020141124725,
    0.24611230194568634,
    0.33791524171829224,
    0.44070982933044434,
    0.5626170039176941,
    0.7229568362236023,
    1.0,
)
adapter_scale = 2.0
norm_epsilon = 1e-06
f32 = jnp.float32
bf16 = jnp.bfloat16


def params(mib):
    return pltpu.CompilerParams(vmem_limit_bytes=mib * 2**20)


def whole(shape):
    return pl.BlockSpec(shape, lambda *_: (0,) * len(shape))


def norm_kernel(hidden, gain, routes, scores, out):
    rows, width = hidden.shape
    wide = hidden[...].astype(f32)
    spread = jnp.mean(wide * wide, axis=-1, keepdims=True)
    normed = wide * lax.rsqrt(spread + norm_epsilon) * gain[...].astype(f32).reshape(1, width)
    out[:, :width] = normed.astype(bf16)
    logits = scores[...]
    parts = jnp.exp(logits - jnp.max(logits, axis=0, keepdims=True))
    shares = parts / jnp.sum(parts, axis=0, keepdims=True)
    place = lax.broadcasted_iota(jnp.int32, (LANES, rows), 0)
    named = place & (LANES // 2 - 1)
    table = jnp.zeros((LANES, rows), f32)
    for k in range(routes.shape[0]):
        table = table + jnp.where(routes[k : k + 1, :] == named, shares[k : k + 1, :], 0.0)
    high = table.astype(bf16).astype(f32)
    both = jnp.where(place < LANES // 2, high, table - high).astype(bf16)
    out[:, width:] = lax.dot_general(
        unit(rows), both, (((1,), (1,)), ((), ())), preferred_element_type=f32
    ).astype(bf16)


def unit(size):
    row = lax.broadcasted_iota(jnp.int32, (size, size), 0)
    return (row == lax.broadcasted_iota(jnp.int32, (size, size), 1)).astype(f32).astype(bf16)


def norm_rows(hidden, gain, routes, scores):
    rows, width = hidden.shape
    top = routes.shape[1]
    return pl.pallas_call(
        norm_kernel,
        grid=(1,),
        in_specs=[whole((rows, width)), whole((width,)), whole((top, rows)), whole((top, rows))],
        out_specs=whole((rows, width + LANES)),
        out_shape=jax.ShapeDtypeStruct((rows, width + LANES), bf16),
        compiler_params=params(56),
    )(hidden, gain, routes.T, scores.T)


def level_tables():
    sub = lax.broadcasted_iota(jnp.int32, (8, LANES), 0)
    low = jnp.zeros((8, LANES), f32)
    high = low
    for i in range(8):
        low = jnp.where(sub == i, code_levels[i], low)
        high = jnp.where(sub == i, code_levels[i + 8], high)
    return low, high


def decode(tables, words, nibble):
    pieces = []
    for q in range(words.shape[0] // 8):
        word = words[8 * q : 8 * q + 8]
        entry = (word >> (4 * nibble)) & 7
        upper = (word & (8 << (4 * nibble))) != 0
        low = jnp.take_along_axis(tables[0], entry, axis=0, mode="promise_in_bounds")
        high = jnp.take_along_axis(tables[1], entry, axis=0, mode="promise_in_bounds")
        pieces.append(jnp.where(upper, high, low))
    return jnp.concatenate(pieces, axis=0)


def copy(source, target, sem):
    move = pltpu.make_async_copy(source, target, sem)
    move.start()
    return move


def enter_kernel(
    part, codes, scale, down_map, up_map, before, out, made,
    words_of, scale_of, factors, down_of, up_of, spread, weights, small_sem, in_sem, out_sem,
):
    tiles, rows, _ = out.shape
    third = codes.shape[2]
    half = tiles * LANES
    first = part * rows
    blocks = rows // BLOCK
    arriving = [
        copy(scale.at[0, pl.ds(first // GROUP, rows // GROUP)], scale_of, small_sem.at[0]),
        copy(down_map.at[:, pl.ds(first, rows)], down_of, small_sem.at[1]),
        copy(up_map.at[0], up_of, small_sem.at[2]),
    ]

    def arriving_words(k):
        here = pl.multiple_of(k * BLOCK, BLOCK)
        return pltpu.make_async_copy(
            codes.at[0, pl.ds(first + here, BLOCK)], words_of.at[pl.ds(here, BLOCK)], in_sem.at[k]
        )

    for k in range(blocks):
        arriving_words(k).start()
    made[...] = jnp.zeros_like(made)
    tables = level_tables()
    spread[...] = jnp.zeros_like(spread)
    for move in arriving:
        move.wait()
    for tile in range(tiles):
        for side in range(2):
            piece = up_of[side, :, tile * LANES : (tile + 1) * LANES].astype(f32) * adapter_scale
            spread[tile, side * RANK : (side + 1) * RANK, side * LANES : (side + 1) * LANES] = piece.astype(bf16)
    factors[...] = scale_of[...].astype(f32)
    scales = BLOCK // GROUP

    def leaving(k):
        here = pl.ds(pl.multiple_of(k * BLOCK, BLOCK), BLOCK)
        return pltpu.make_async_copy(weights.at[:, here], out.at[:, here], out_sem.at[k])

    @pl.loop(0, blocks)
    def _(k):
        arriving_words(k).wait()
        here = pl.multiple_of(k * BLOCK, BLOCK)
        for tile in range(tiles):
            adapter = lax.dot_general(
                down_of[:, pl.ds(here, BLOCK)],
                spread[tile],
                (((0,), (0,)), ((), ())),
                preferred_element_type=f32,
            )
            for side in range(2):
                column = side * half + tile * LANES
                nibble, offset = divmod(column, third)
                factor = factors[pl.ds(pl.multiple_of(k * scales, scales), scales), pl.ds(column, LANES)]
                for g in range(scales):
                    packed = words_of[pl.ds(here + g * GROUP, GROUP), pl.ds(offset, LANES)]
                    value = decode(tables, packed, nibble) * factor[g : g + 1]
                    value = value + adapter[g * GROUP : (g + 1) * GROUP, side * LANES : (side + 1) * LANES]
                    weights[tile, pl.ds(here + g * GROUP, GROUP), pl.ds(side * LANES, LANES)] = value.astype(bf16)
        leaving(k).start()

    @pl.loop(0, blocks)
    def _(k):
        leaving(k).wait()


def in_hbm(count):
    return [pl.BlockSpec(memory_space=pltpu.HBM)] * count


def enter_weights(part, parts, codes, scale, down_map, up_map, before):
    _, width, third = codes.shape
    tiles = 3 * third // 2 // LANES
    rows = width // parts
    return pl.pallas_call(
        functools.partial(enter_kernel, part),
        in_specs=in_hbm(4) + [pl.BlockSpec(memory_space=pl.ANY)],
        out_specs=in_hbm(1) + [pl.BlockSpec(memory_space=pltpu.VMEM)],
        out_shape=[
            jax.ShapeDtypeStruct((tiles, rows, 2 * LANES), bf16),
            jax.ShapeDtypeStruct((8, LANES), f32),
        ],
        scratch_shapes=[
            pltpu.VMEM((rows, third), jnp.int32),
            pltpu.VMEM((rows // GROUP, 3 * third), bf16),
            pltpu.VMEM((rows // GROUP, 3 * third), f32),
            pltpu.VMEM((2 * RANK, rows), bf16),
            pltpu.VMEM(up_map.shape[1:], bf16),
            pltpu.VMEM((tiles, 2 * RANK, 2 * LANES), bf16),
            pltpu.VMEM((tiles, rows, 2 * LANES), bf16),
            pltpu.SemaphoreType.DMA((3,)),
            pltpu.SemaphoreType.DMA((rows // BLOCK,)),
            pltpu.SemaphoreType.DMA((rows // BLOCK,)),
        ],
        compiler_params=params(58),
        cost_estimate=pl.CostEstimate(flops=4 * 10**9, bytes_accessed=20 * 10**6, transcendentals=0),
    )(codes, scale, down_map[0].T, up_map, before)


def leave_kernel(
    codes, scale, down_map, up_map, before, out, made,
    words_of, scale_of, down_of, up_of, weights, small_sem, in_sem, out_sem,
):
    _, rows, columns = codes.shape
    arriving = [
        copy(scale.at[0], scale_of, small_sem.at[0]),
        copy(down_map, down_of, small_sem.at[1]),
        copy(up_map.at[0], up_of, small_sem.at[2]),
    ]
    blocks = columns // BLOCK

    def wide(k):
        return pl.ds(pl.multiple_of(k * BLOCK, BLOCK), BLOCK)

    def arriving_words(k):
        return pltpu.make_async_copy(codes.at[0, :, wide(k)], words_of.at[:, wide(k)], in_sem.at[k])

    def leaving(k):
        return pltpu.make_async_copy(weights.at[:, wide(k)], out.at[:, wide(k)], out_sem.at[k])

    for k in range(blocks):
        arriving_words(k).start()
    made[...] = jnp.zeros_like(made)
    tables = level_tables()
    for move in arriving:
        move.wait()

    @pl.loop(0, blocks)
    def _(k):
        arriving_words(k).wait()
        adapter = lax.dot_general(
            down_of[...], up_of[:, wide(k)], (((0,), (0,)), ((), ())), preferred_element_type=f32
        ) * adapter_scale
        for j in range(BLOCK // LANES):
            lanes = pl.ds(pl.multiple_of(k * BLOCK, BLOCK) + j * LANES, LANES)
            for nibble in range(3):
                for g in range(rows // GROUP):
                    row = nibble * rows + g * GROUP
                    packed = words_of[pl.ds(g * GROUP, GROUP), lanes]
                    factor = scale_of[pl.ds(row // GROUP, 1), lanes].astype(f32)
                    value = decode(tables, packed, nibble) * factor
                    value = value + adapter[row : row + GROUP, j * LANES : (j + 1) * LANES]
                    weights[pl.ds(row, GROUP), lanes] = value.astype(bf16)
        leaving(k).start()

    @pl.loop(0, blocks)
    def _(k):
        leaving(k).wait()


def leave_weights(codes, scale, down_map, up_map, before):
    _, third, width = codes.shape
    return pl.pallas_call(
        leave_kernel,
        in_specs=in_hbm(4) + [pl.BlockSpec(memory_space=pl.ANY)],
        out_specs=in_hbm(1) + [pl.BlockSpec(memory_space=pltpu.VMEM)],
        out_shape=[
            jax.ShapeDtypeStruct((3 * third, width), bf16),
            jax.ShapeDtypeStruct((8, LANES), f32),
        ],
        scratch_shapes=[
            pltpu.VMEM((third, width), jnp.int32),
            pltpu.VMEM(scale.shape[1:], bf16),
            pltpu.VMEM((RANK, 3 * third), bf16),
            pltpu.VMEM((RANK, width), bf16),
            pltpu.VMEM((3 * third, width), bf16),
            pltpu.SemaphoreType.DMA((3,)),
            pltpu.SemaphoreType.DMA((width // BLOCK,)),
            pltpu.SemaphoreType.DMA((width // BLOCK,)),
        ],
        compiler_params=params(58),
        cost_estimate=pl.CostEstimate(flops=2 * 10**9, bytes_accessed=15 * 10**6, transcendentals=0),
    )(codes, scale, down_map[0].T, up_map, before)


def pick_rows(own, tables, rows, slots):
    cap = rows // 2
    total = rows * len(tables)
    lane = lax.broadcasted_iota(jnp.int32, (rows, LANES), 1)
    columns = []
    for shift in (0, LANES // 2):
        parts = [
            jnp.sum(jnp.where(lane == own + shift, t, 0.0), axis=-1, keepdims=True) for t in tables
        ]
        column = jnp.concatenate(parts, axis=0)
        columns.append(jnp.broadcast_to(column, (total, slots)))
    high, low = columns
    hit = (high != 0.0).astype(f32).astype(bf16)
    high, low = high.astype(bf16), low.astype(bf16)
    row = lax.broadcasted_iota(jnp.int32, (total, total), 0)
    column = lax.broadcasted_iota(jnp.int32, (total, total), 1)
    before = ((row // rows == column // rows) & (row < column)).astype(f32).astype(bf16)
    first = (((0,), (0,)), ((), ()))
    rank_of = lax.dot_general(hit, before, first, preferred_element_type=f32)
    hit_of = lax.dot_general(hit, unit(total), first, preferred_element_type=f32)
    slot = lax.broadcasted_iota(jnp.int32, (slots, total), 0)
    place = lax.broadcasted_iota(jnp.int32, (slots, total), 1)
    taken = (slot // cap == place // rows) & (rank_of == (slot % cap).astype(f32)) & (hit_of > 0.5)
    gather = taken.astype(f32).astype(bf16)
    weight = jnp.dot(gather, high, preferred_element_type=f32)
    weight = weight + jnp.dot(gather, low, preferred_element_type=f32)
    rank = lax.dot_general(before, hit, first, preferred_element_type=f32)
    slot = lax.broadcasted_iota(jnp.int32, (total, slots), 1)
    place = lax.broadcasted_iota(jnp.int32, (total, slots), 0)
    taken = (slot // cap == place // rows) & (rank == (slot % cap).astype(f32)) & (hit.astype(f32) > 0.5)
    return gather, taken.astype(f32).astype(bf16), weight


def expert_kernel(count, pieces, own, *refs):
    blocks, refs = refs[:count], refs[count:]
    enters, leave, _, refs = refs[:pieces], refs[pieces], refs[pieces + 1], refs[pieces + 2 :]
    outs, refs = refs[:count], refs[count:]
    picked, spread, weight, active, enter_of, leave_of, enter_sem, leave_sem = refs
    rows = blocks[0].shape[0]
    width = picked.shape[1]
    sets, _, slots = spread.shape
    _, tiles, depth, _ = enter_of.shape
    each = count // sets
    wide = 4 * LANES
    steps = width // wide

    def enter_move(p, tile):
        return pltpu.make_async_copy(enters[p].at[tile], enter_of.at[p, tile], enter_sem.at[p, tile])

    def leave_move(n):
        lanes = pl.ds(pl.multiple_of(n * wide, wide), wide)
        return pltpu.make_async_copy(leave.at[:, lanes], leave_of.at[n], leave_sem.at[n])

    for tile in range(tiles):
        for p in range(pieces):
            enter_move(p, tile).start()
    for n in range(steps):
        leave_move(n).start()
    for g in range(sets):
        members = blocks[g * each : (g + 1) * each]
        tables = [member[:, width:].astype(f32) for member in members]
        gather, scatter, factor = pick_rows(own[0], tables, rows, slots)
        here = pl.ds(g * slots, slots)
        spread[g] = scatter
        weight[here, :] = factor
        for n in range(steps):
            lanes = pl.ds(n * wide, wide)
            source = jnp.concatenate([member[:, lanes] for member in members], axis=0)
            picked[here, lanes] = jnp.dot(gather, source, preferred_element_type=f32).astype(bf16)

    @pl.loop(0, tiles)
    def _(tile):
        joined = 0.0
        for p in range(pieces):
            enter_move(p, tile).wait()
            part = picked[:, pl.ds(p * depth, depth)]
            joined = joined + jnp.dot(part, enter_of[p, tile], preferred_element_type=f32)
        gate = joined[:, :LANES]
        value = gate / (1.0 + jnp.exp(-gate)) * joined[:, LANES:]
        active[tile] = value.astype(bf16)

    @pl.loop(0, steps)
    def _(n):
        leave_move(n).wait()
        lanes = pl.ds(pl.multiple_of(n * wide, wide), wide)
        entry = jnp.concatenate([active[t] for t in range(tiles)], axis=1)
        factor = jnp.concatenate([weight[...]] * (wide // slots), axis=1)
        result = jnp.dot(entry, leave_of[n], preferred_element_type=f32)
        result = (result * factor).astype(bf16)
        for g in range(sets):
            own_rows = result[g * slots : (g + 1) * slots]
            full = jnp.dot(spread[g], own_rows, preferred_element_type=f32).astype(bf16)
            for b in range(each):
                outs[g * each + b][:, lanes] = full[b * rows : (b + 1) * rows]


def expert(own, blocks, enters, leave, before):
    count = len(blocks)
    pieces = len(enters)
    rows, padded = blocks[0].shape
    width = padded - LANES
    tiles, depth, columns = enters[0].shape
    each = LANES // (rows // 2)
    sets = count // each
    steps = width // (4 * LANES)
    vmem = pl.BlockSpec(memory_space=pltpu.VMEM)
    return pl.pallas_call(
        functools.partial(expert_kernel, count, pieces),
        in_specs=[pl.BlockSpec(memory_space=pltpu.SMEM)]
        + [vmem] * count
        + in_hbm(pieces + 1)
        + [pl.BlockSpec(memory_space=pl.ANY)],
        out_specs=[vmem] * count,
        out_shape=[jax.ShapeDtypeStruct((rows, width), bf16)] * count,
        scratch_shapes=[
            pltpu.VMEM((sets * LANES, width), bf16),
            pltpu.VMEM((sets, each * rows, LANES), bf16),
            pltpu.VMEM((sets * LANES, LANES), f32),
            pltpu.VMEM((tiles, sets * LANES, LANES), bf16),
            pltpu.VMEM((pieces, tiles, depth, columns), bf16),
            pltpu.VMEM((steps, leave.shape[0], 4 * LANES), bf16),
            pltpu.SemaphoreType.DMA((pieces, tiles)),
            pltpu.SemaphoreType.DMA((steps,)),
        ],
        compiler_params=params(50),
        cost_estimate=pl.CostEstimate(flops=10**10, bytes_accessed=28 * 10**6, transcendentals=0),
    )(own, *blocks, *enters, leave, before)


def attend_kernel(lengths, queries, fresh, cache, out):
    rows = queries.shape[0]
    first = pl.program_id(0) * rows
    scaling = 1.0 / math.sqrt(HEAD)
    positions = cache.shape[2]
    lower = lax.broadcasted_iota(jnp.int32, (HEADS, HEAD), 0) < HEADS // KV_HEADS
    place = lax.broadcasted_iota(jnp.int32, (HEADS, positions), 1)
    own_half = lambda both: jnp.where(lower, both[:, :HEAD], both[:, HEAD:])
    old, new = [], []
    for t in range(rows):
        query = queries[t]
        zero = jnp.zeros_like(query)
        both = jnp.concatenate([jnp.where(lower, query, zero), jnp.where(lower, zero, query)], axis=1)
        score = lax.dot_general(
            both, cache[t, 0], (((1,), (1,)), ((), ())), preferred_element_type=f32
        )
        old.append(jnp.where(place < lengths[first + t], score * scaling, -jnp.inf))
        key = own_half(fresh[t, 0:1, :].astype(f32))
        new.append(jnp.sum(query.astype(f32) * key, axis=-1, keepdims=True) * scaling)
    old, new = jnp.concatenate(old, axis=0), jnp.concatenate(new, axis=0)
    highest = jnp.maximum(jnp.max(old, axis=-1, keepdims=True), new)
    old = jnp.exp(old - highest)
    new = jnp.exp(new - highest)
    inverse = 1.0 / (jnp.sum(old, axis=-1, keepdims=True) + new)
    old = (old * inverse).astype(bf16)
    new = (new * inverse).astype(bf16).astype(f32)
    for t in range(rows):
        heads = slice(t * HEADS, (t + 1) * HEADS)
        blended = own_half(jnp.dot(old[heads], cache[t, 1], preferred_element_type=f32))
        out[t] = (blended + new[heads] * own_half(fresh[t, 1:2, :].astype(f32))).astype(bf16)


def attend(queries, fresh_key_value, key_value_cache, lengths, block=8):
    rows = queries.shape[0]
    positions, width = key_value_cache.shape[2:]
    context = pl.pallas_call(
        attend_kernel,
        grid_spec=pltpu.PrefetchScalarGridSpec(
            num_scalar_prefetch=1,
            grid=(rows // block,),
            in_specs=[
                pl.BlockSpec((block, HEADS, HEAD), lambda i, _: (i, 0, 0)),
                pl.BlockSpec((block, 2, width), lambda i, _: (i, 0, 0)),
                pl.BlockSpec((block, 2, positions, width), lambda i, _: (i, 0, 0, 0)),
            ],
            out_specs=pl.BlockSpec((block, HEADS, HEAD), lambda i, _: (i, 0, 0)),
        ),
        out_shape=jax.ShapeDtypeStruct((rows, HEADS, HEAD), bf16),
        compiler_params=params(16),
        cost_estimate=pl.CostEstimate(flops=5 * 10**8, bytes_accessed=20 * 10**6, transcendentals=0),
    )(lengths, queries.reshape(rows, HEADS, HEAD), fresh_key_value, key_value_cache)
    return context.reshape(rows, HEADS * HEAD)


def swap(value, bit):
    count = lax.axis_size("ep")
    return lax.ppermute(value, "ep", [(i, i ^ bit) for i in range(count)])


def add(terms):
    return sum(term.astype(f32) for term in terms[1:]) + terms[0].astype(f32)


def shards(
    queries,
    fresh_key_value,
    key_value_cache,
    lengths,
    hidden,
    expert_norm_gain,
    routes,
    router_scores,
    gate_up_quant_codes,
    gate_up_code_scale,
    down_quant_codes,
    down_code_scale,
    adapter_input_down,
    adapter_input_up,
    adapter_output_down,
    adapter_output_up,
):
    count = lax.axis_size("ep")
    bits = [1 << b for b in range(count.bit_length() - 1)]
    blocks = {0: norm_rows(hidden, expert_norm_gain, routes, router_scores)}
    enter = [
        lambda before, p=p: enter_weights(
            p, 2, gate_up_quant_codes, gate_up_code_scale, adapter_input_down, adapter_input_up, before
        )
        for p in range(2)
    ]
    leave = lambda before: leave_weights(
        down_quant_codes, down_code_scale, adapter_output_down, adapter_output_up, before
    )
    stage = lambda r: sum(1 for bit in bits[1:] if r & bit)
    low_bit = lambda r: r & -r
    even = [r for r in range(count) if r and r % 2 == 0]
    weights = []
    done = jnp.zeros((8, LANES), f32)
    for now in range(max(stage(r) for r in even) + 1):
        for r in sorted(even, key=low_bit, reverse=True):
            if stage(r ^ low_bit(r)) == now:
                blocks[r] = swap(blocks[r ^ low_bit(r)], low_bit(r))
        for r in [0] + even:
            if stage(r) == now:
                blocks[r | 1] = swap(blocks[r], 1)
        arriving = [r for r in blocks if r % 2 == 0 and stage(r) == now + 1]
        if now < 3:
            made, done = (enter + [leave])[now](done)
            weights.append(made)
            *held, done = lax.optimization_barrier((*[blocks[r] for r in arriving], done))
            blocks.update(zip(arriving, held))
    own = lax.axis_index("ep").astype(jnp.int32).reshape(1)
    produced = expert(own, [blocks[r] for r in range(count)], weights[:2], weights[2], done)
    after = lambda earlier, later: list(lax.optimization_barrier((earlier, *later)))
    sums = {r: [produced[r]] for r in range(0, count, 2)}
    other = {r: produced[r | 1] for r in sums}
    first = max(sums)
    sums[first].append(swap(other.pop(first), 1))
    sent = add(sums.pop(first)).astype(bf16)
    sent, queries, *rest = after(sent, [queries] + [other[r] for r in other])
    for r, rows in zip(other, rest):
        sums[r].append(swap(rows, 1))
    near = bits[1]
    arrived = swap(sent, near)
    context = attend(queries, fresh_key_value, key_value_cache, lengths)
    arrived, context = after(arrived, [context])
    sums[first ^ near].append(arrived)
    for r in sorted(sums, reverse=True)[:-1]:
        bit = low_bit(r)
        sent = add(sums.pop(r)).astype(bf16)
        if bit == near:
            arrived, sent = after(arrived, [sent])
        received = swap(sent, bit)
        if bit == near:
            arrived = received
        sums[r ^ bit].append(received)
    return (context, add(sums[0]).astype(bf16))


def solution(mesh):
    return jax.shard_map(
        shards,
        mesh=mesh,
        in_specs=(
            P(("grp", "ep"), None),
            P(("grp", "ep"), None, None),
            P(("grp", "ep"), None, None, None),
            P(("grp", "ep")),
            P(("grp", "ep"), None),
            P(),
            P(("grp", "ep"), None),
            P(("grp", "ep"), None),
            P("ep", None, None),
            P("ep", None, None),
            P("ep", None, None),
            P("ep", None, None),
            P("ep", None, None),
            P("ep", None, None, None),
            P("ep", None, None),
            P("ep", None, None),
        ),
        out_specs=(P(("grp", "ep"), None), P(("grp", "ep"), None)),
        check_vma=False,
    )
```

time: 143 us -> 110 us (0.77)
  waiting for transfers between devices: 50.1 us -> 26.1 us
  local copies, waits for them, and re-layouts: 15.1 us -> 3.4 us
  starting transfers between devices: 21.6 us -> 24.4 us
    ppermute x30, waiting for transfers between devices: 50.1 us -> 26.1 us  [swap(): return lax.ppermute(value, 'ep', [(i, i ^ bit) for i in range(count)])]
    unnamed x46, local copies, waits for them, and re-layouts: 14.1 us -> 2.81 us
    pallas_call x4 -> x5, Pallas kernels: 39.6 us -> 49.3 us  [the longest x2 20.1 us: enter_weights(): pl.pallas_call(functools.partial(enter_kernel, part), in_specs=in_hbm(4)...]
    pallas_call x1, Pallas kernels: 13.1 us -> 4.02 us  [attend(): pl.pallas_call(attend_kernel, grid_spec=pltpu.PrefetchScalarGridSpec(num_...]
    ppermute x30, starting transfers between devices: 21.6 us -> 24.4 us  [swap(): return lax.ppermute(value, 'ep', [(i, i ^ bit) for i in range(count)])]
  transfers between devices with their start and end apart: 30 -> 30, of which waited for: 11 -> 11; matrix products, arithmetic and copies ran while one was open for 3% -> 2% of each run, Pallas kernels for 24% -> 33%
where the time goes in v2:
time: 110 us
  Pallas kernels  53.3 us (48%)
  waiting for transfers between devices  26.1 us (24%)
  starting transfers between devices  24.4 us (22%)
  local copies, waits for them, and re-layouts  3.4 us (3%)
  other arithmetic  1.47 us (1%)
    ppermute x30, waiting for transfers between devices, swap(): return lax.ppermute(value, 'ep', [(i, i ^ bit) for i in range(count)])  26.1 us
    ppermute x30, starting transfers between devices, swap(): return lax.ppermute(value, 'ep', [(i, i ^ bit) for i in range(count)])  24.4 us
    pallas_call x2, Pallas kernels, enter_weights(): pl.pallas_call(functools.partial(enter_kernel, part), in_specs=in_hbm(4)...  20.1 us
    pallas_call x1, Pallas kernels, expert(): pl.pallas_call(functools.partial(expert_kernel, count, pieces), in_specs=...  15.3 us
    pallas_call x1, Pallas kernels, leave_weights(): pl.pallas_call(leave_kernel, in_specs=in_hbm(4) + [pl.BlockSpec(memory_sp...  11.9 us
    pallas_call x1, Pallas kernels, attend(): pl.pallas_call(attend_kernel, grid_spec=pltpu.PrefetchScalarGridSpec(num_...  4.02 us
    unnamed x46, local copies, waits for them, and re-layouts  2.81 us
  transfers between devices with their start and end apart: 30, of which 11 were waited for; matrix products, arithmetic and copies ran while one was open for 2% of the time, Pallas kernels for 33%

profile of v2, /device:TPU:0, one launch (start us, length us, event | category | flops | bytes accessed | tf_op | source)
XLA Modules:
  0.0 109.6 jit_solution(10233317600591093077)
XLA Ops:
  0.6 2.0 %shard_map.167.refs_0_ = bf16[32,4224]{1,0:T(8,128)(2,1)} custom-call(bf16[32,4096]{1,0:T(8,128)(2,1)} %hidden.1, bf16[4096]{0:T(1024)(128)(2,1)} %gain.1, s32[8,32]{1,0:T(8,128)} %bitcast.21, f32[8,32]{1,0:T(8,128)} %bitcast.22), custom_call_target="tpu_custom_call" | custom-call | tf_op jit(solution)/shard_map/pallas_call | solution.py:79
  2.6 3.0 %collective-permute-start.3 = (bf16[32,4224]{1,0:T(8,128)(2,1)}, bf16[32,4224]{1,0:T(8,128)(2,1)S(1)}, u32[]{:S(2)}, u32[]{:S(2)}) collective-permute-start(bf16[32,4224]{1,0:T(8,128)(2,1)} %shard_map.167.refs_0_), channel_id=1, source_target_pairs={{0,2},{1,3},{2,0},{3,1},{4,6},{5,7},{6,4},{7,5},{8,10},{9,11},{10,... | collective-permute-start | bytes 811016 | tf_op jit(solution)/shard_map/ppermute | solution.py:477
  5.6 1.6 %collective-permute-start.2 = (bf16[32,4224]{1,0:T(8,128)(2,1)}, bf16[32,4224]{1,0:T(8,128)(2,1)S(1)}, u32[]{:S(2)}, u32[]{:S(2)}) collective-permute-start(bf16[32,4224]{1,0:T(8,128)(2,1)} %shard_map.167.refs_0_), channel_id=1, source_target_pairs={{0,4},{1,5},{2,6},{3,7},{4,0},{5,1},{6,2},{7,3},{8,12},{9,13},{10,... | collective-permute-start | bytes 811016 | tf_op jit(solution)/shard_map/ppermute | solution.py:477
  7.1 2.6 %collective-permute-start.1 = (bf16[32,4224]{1,0:T(8,128)(2,1)}, bf16[32,4224]{1,0:T(8,128)(2,1)S(1)}, u32[]{:S(2)}, u32[]{:S(2)}) collective-permute-start(bf16[32,4224]{1,0:T(8,128)(2,1)} %shard_map.167.refs_0_), channel_id=1, source_target_pairs={{0,8},{1,9},{2,10},{3,11},{4,12},{5,13},{6,14},{7,15},{8,0},{9,1},... | collective-permute-start | bytes 811016 | tf_op jit(solution)/shard_map/ppermute | solution.py:477
  9.7 0.6 broadcast_in_dim.3.before
  10.3 10.0 %shard_map.168 = (bf16[6,2048,256]{2,1,0:T(8,128)(2,1)}, f32[8,128]{1,0:T(8,128)}) custom-call(s32[1,4096,512]{2,1,0:T(8,128)} %codes.4, bf16[1,64,1536]{2,1,0:T(8,128)(2,1)} %scale.4, bf16[32,4096]{1,0:T(8,128)(2,1)} %bitcast.23, bf16[1,2,16,768]{3,2,1,0:T(8,128)(2,1)} %up_map.4, f32[8,128]{1,0:T(8,128)} %broadcast_in_dim.3.before), custom_call_target="tpu_custom_call" | custom-call | flops 4000000000 | bytes 20000000 | tf_op jit(solution)/shard_map/pallas_call | solution.py:191
  20.4 1.3 %collective-permute-done.1.refs_8_ = bf16[32,4224]{1,0:T(8,128)(2,1)S(1)} collective-permute-done((bf16[32,4224]{1,0:T(8,128)(2,1)}, bf16[32,4224]{1,0:T(8,128)(2,1)S(1)}, u32[]{:S(2)}, u32[]{:S(2)}) %collective-permute-start.1) | collective-permute-done | bytes 270368 | tf_op jit(solution)/shard_map/ppermute | solution.py:477
  22.7 1.5 %collective-permute-start.7 = (bf16[32,4224]{1,0:T(8,128)(2,1)S(1)}, bf16[32,4224]{1,0:T(8,128)(2,1)S(1)}, u32[]{:S(2)}, u32[]{:S(2)}) collective-permute-start(bf16[32,4224]{1,0:T(8,128)(2,1)S(1)} %collective-permute-done.2.refs_4_), channel_id=1, source_target_pairs={{0,2},{1,3},{2,0},{3,1},{4,6},{5,7},{6,4},{7,5},{8,10},{9,11},{10,... | collective-permute-start | bytes 811016 | tf_op jit(solution)/shard_map/ppermute | solution.py:477
  24.2 10.0 %shard_map.169 = (bf16[6,2048,256]{2,1,0:T(8,128)(2,1)}, f32[8,128]{1,0:T(8,128)}) custom-call(s32[1,4096,512]{2,1,0:T(8,128)} %codes.4, bf16[1,64,1536]{2,1,0:T(8,128)(2,1)} %scale.4, bf16[32,4096]{1,0:T(8,128)(2,1)} %bitcast.24, bf16[1,2,16,768]{3,2,1,0:T(8,128)(2,1)} %up_map.4, f32[8,128]{1,0:T(8,128)} %get-tuple-element.52.before), custom_call_target="tpu_custom_call" | custom-call | flops 4000000000 | bytes 20000000 | tf_op jit(solution)/shard_map/pallas_call | solution.py:191
  34.3 0.6 collective-permute-start.13
  35.9 11.9 %shard_map.170 = (bf16[768,4096]{1,0:T(8,128)(2,1)}, f32[8,128]{1,0:T(8,128)}) custom-call(s32[1,256,4096]{2,1,0:T(8,128)} %codes.5, bf16[1,12,4096]{2,1,0:T(8,128)(2,1)} %scale.5, bf16[16,768]{1,0:T(8,128)(2,1)} %bitcast.25, bf16[1,16,4096]{2,1,0:T(8,128)(2,1)} %up_map.5, f32[8,128]{1,0:T(8,128)} %get-tuple-element.57.before), custom_call_target="tpu_custom_call" | custom-call | flops 2000000000 | bytes 15000000 | tf_op jit(solution)/shard_map/pallas_call | solution.py:269
  51.4 0.9 copy-done.2
  52.2 15.3 %shard_map.171 = (bf16[32,4096]{1,0:T(8,128)(2,1)S(1)}, bf16[32,4096]{1,0:T(8,128)(2,1)S(1)}, bf16[32,4096]{1,0:T(8,128)(2,1)S(1)}, bf16[32,4096]{1,0:T(8,128)(2...) custom-call(s32[1]{0:T(128)} %bitcast.own, ...), custom_call_target="tpu_custom_call" | custom-call | flops 10000000000 | bytes 28000000 | tf_op jit(solution)/shard_map/pallas_call | solution.py:398
  67.8 1.6 %collective-permute-done.15 = bf16[32,4096]{1,0:T(8,128)(2,1)S(1)} collective-permute-done((bf16[32,4096]{1,0:T(8,128)(2,1)}, bf16[32,4096]{1,0:T(8,128)(2,1)S(1)}, u32[]{:S(2)}, u32[]{:S(2)}) %collective-permute-start.15) | collective-permute-done | bytes 262176 | tf_op jit(solution)/shard_map/ppermute | solution.py:477
  69.5 1.6 %collective-permute-start.16 = (bf16[32,4096]{1,0:T(8,128)(2,1)S(1)}, bf16[32,4096]{1,0:T(8,128)(2,1)S(1)}, u32[]{:S(2)}, u32[]{:S(2)}) collective-permute-start(bf16[32,4096]{1,0:T(8,128)(2,1)S(1)} %add_convert_fusion.7), channel_id=1, source_target_pairs={{0,2},{1,3},{2,0},{3,1},{4,6},{5,7},{6,4},{7,5},{8,10},{9,11},{10,... | collective-permute-start | bytes 786440 | tf_op jit(solution)/shard_map/ppermute | solution.py:477
  71.1 4.0 %shard_map.172 = bf16[32,32,128]{2,1,0:T(8,128)(2,1)S(1)} custom-call(s32[32]{0:T(128)S(1)} %copy-done.1, bf16[32,32,128]{2,1,0:T(8,128)(2,1)S(1)} %bitcast.18, bf16[32,2,256]{2,1,0:T(2,128)(2,1)S(1)} %copy-done, bf16[32,2,256,256]{3,2,1,0:T(8,128)(2,1)S(1)} %bitcast.16), custom_call_target="tpu_custom_call" | custom-call | flops 500000000 | bytes 20000000 | tf_op jit(solution)/shard_map/pallas_call | solution.py:456
  75.2 0.8 copy.21
  76.0 0.5 collective-permute-start.17
  77.0 0.9 collective-permute-done.16
  77.9 0.5 collective-permute-start.25
  78.8 0.9 collective-permute-done.25
  79.8 1.6 %collective-permute-start.20 = (bf16[32,4096]{1,0:T(8,128)(2,1)S(1)}, bf16[32,4096]{1,0:T(8,128)(2,1)S(1)}, u32[]{:S(2)}, u32[]{:S(2)}) collective-permute-start(bf16[32,4096]{1,0:T(8,128)(2,1)S(1)} %add_convert_fusion.6), channel_id=1, source_target_pairs={{0,4},{1,5},{2,6},{3,7},{4,0},{5,1},{6,2},{7,3},{8,12},{9,13},{10,... | collective-permute-start | bytes 786440 | tf_op jit(solution)/shard_map/ppermute | solution.py:477
  81.4 1.6 %collective-permute-start.22 = (bf16[32,4096]{1,0:T(8,128)(2,1)S(1)}, bf16[32,4096]{1,0:T(8,128)(2,1)S(1)}, u32[]{:S(2)}, u32[]{:S(2)}) collective-permute-start(bf16[32,4096]{1,0:T(8,128)(2,1)S(1)} %add_convert_fusion.5), channel_id=1, source_target_pairs={{0,2},{1,3},{2,0},{3,1},{4,6},{5,7},{6,4},{7,5},{8,10},{9,11},{10,... | collective-permute-start | bytes 786440 | tf_op jit(solution)/shard_map/ppermute | solution.py:477
  83.1 6.5 %collective-permute-done.22 = bf16[32,4096]{1,0:T(8,128)(2,1)S(1)} collective-permute-done((bf16[32,4096]{1,0:T(8,128)(2,1)S(1)}, bf16[32,4096]{1,0:T(8,128)(2,1)S(1)}, u32[]{:S(2)}, u32[]{:S(2)}) %collective-permute-start.22) | collective-permute-done | bytes 262176 | tf_op jit(solution)/shard_map/ppermute | solution.py:477
  89.6 1.5 %collective-permute-start.26 = (bf16[32,4096]{1,0:T(8,128)(2,1)S(1)}, bf16[32,4096]{1,0:T(8,128)(2,1)S(1)}, u32[]{:S(2)}, u32[]{:S(2)}) collective-permute-start(bf16[32,4096]{1,0:T(8,128)(2,1)S(1)} %add_convert_fusion.3), channel_id=1, source_target_pairs={{0,2},{1,3},{2,0},{3,1},{4,6},{5,7},{6,4},{7,5},{8,10},{9,11},{10,... | collective-permute-start | bytes 786440 | tf_op jit(solution)/shard_map/ppermute | solution.py:477
  91.3 1.6 %collective-permute-start.23 = (bf16[32,4096]{1,0:T(8,128)(2,1)S(1)}, bf16[32,4096]{1,0:T(8,128)(2,1)S(1)}, u32[]{:S(2)}, u32[]{:S(2)}) collective-permute-start(bf16[32,4096]{1,0:T(8,128)(2,1)S(1)} %add_convert_fusion.4), channel_id=1, source_target_pairs={{0,8},{1,9},{2,10},{3,11},{4,12},{5,13},{6,14},{7,15},{8,0},{9,1},... | collective-permute-start | bytes 786440 | tf_op jit(solution)/shard_map/ppermute | solution.py:477
  92.9 3.9 %collective-permute-done.26 = bf16[32,4096]{1,0:T(8,128)(2,1)S(1)} collective-permute-done((bf16[32,4096]{1,0:T(8,128)(2,1)S(1)}, bf16[32,4096]{1,0:T(8,128)(2,1)S(1)}, u32[]{:S(2)}, u32[]{:S(2)}) %collective-permute-start.26) | collective-permute-done | bytes 262176 | tf_op jit(solution)/shard_map/ppermute | solution.py:477
  96.9 0.7 collective-permute-start.27
  97.6 1.5 %collective-permute-start.29 = (bf16[32,4096]{1,0:T(8,128)(2,1)S(1)}, bf16[32,4096]{1,0:T(8,128)(2,1)S(1)}, u32[]{:S(2)}, u32[]{:S(2)}) collective-permute-start(bf16[32,4096]{1,0:T(8,128)(2,1)S(1)} %add_convert_fusion.1), channel_id=1, source_target_pairs={{0,2},{1,3},{2,0},{3,1},{4,6},{5,7},{6,4},{7,5},{8,10},{9,11},{10,... | collective-permute-start | bytes 786440 | tf_op jit(solution)/shard_map/ppermute | solution.py:477
  99.1 5.8 %collective-permute-done.23 = bf16[32,4096]{1,0:T(8,128)(2,1)S(1)} collective-permute-done((bf16[32,4096]{1,0:T(8,128)(2,1)S(1)}, bf16[32,4096]{1,0:T(8,128)(2,1)S(1)}, u32[]{:S(2)}, u32[]{:S(2)}) %collective-permute-start.23) | collective-permute-done | bytes 262176 | tf_op jit(solution)/shard_map/ppermute | solution.py:477
  104.9 3.8 %collective-permute-done.27 = bf16[32,4096]{1,0:T(8,128)(2,1)S(1)} collective-permute-done((bf16[32,4096]{1,0:T(8,128)(2,1)S(1)}, bf16[32,4096]{1,0:T(8,128)(2,1)S(1)}, u32[]{:S(2)}, u32[]{:S(2)}) %collective-permute-start.27) | collective-permute-done | bytes 262176 | tf_op jit(solution)/shard_map/ppermute | solution.py:477
  108.7 0.9 add_convert_fusion
  (90 shorter events, 7.1 us)
Async XLA Ops:
  2.6 17.8 %collective-permute-start.3 = (bf16[32,4224]{1,0:T(8,128)(2,1)}, bf16[32,4224]{1,0:T(8,128)(2,1)S(1)}, u32[]{:S(2)}, u32[]{:S(2)}) collective-permute-start(bf16[32,4224]{1,0:T(8,128)(2,1)} %shard_map.167.refs_0_), channel_id=1, source_target_pairs={{0,2},{1,3},{2,0},{3,1},{4,6},{5,7},{6,4},{7,5},{8,10},{9,11},{10,... | collective-permute-start | bytes 811016 | tf_op jit(solution)/shard_map/ppermute | solution.py:477
  5.6 14.8 %collective-permute-start.2 = (bf16[32,4224]{1,0:T(8,128)(2,1)}, bf16[32,4224]{1,0:T(8,128)(2,1)S(1)}, u32[]{:S(2)}, u32[]{:S(2)}) collective-permute-start(bf16[32,4224]{1,0:T(8,128)(2,1)} %shard_map.167.refs_0_), channel_id=1, source_target_pairs={{0,4},{1,5},{2,6},{3,7},{4,0},{5,1},{6,2},{7,3},{8,12},{9,13},{10,... | collective-permute-start | bytes 811016 | tf_op jit(solution)/shard_map/ppermute | solution.py:477
  7.1 14.6 %collective-permute-start.1 = (bf16[32,4224]{1,0:T(8,128)(2,1)}, bf16[32,4224]{1,0:T(8,128)(2,1)S(1)}, u32[]{:S(2)}, u32[]{:S(2)}) collective-permute-start(bf16[32,4224]{1,0:T(8,128)(2,1)} %shard_map.167.refs_0_), channel_id=1, source_target_pairs={{0,8},{1,9},{2,10},{3,11},{4,12},{5,13},{6,14},{7,15},{8,0},{9,1},... | collective-permute-start | bytes 811016 | tf_op jit(solution)/shard_map/ppermute | solution.py:477
  21.8 12.5 %collective-permute-start.8 = (bf16[32,4224]{1,0:T(8,128)(2,1)S(1)}, bf16[32,4224]{1,0:T(8,128)(2,1)S(1)}, u32[]{:S(2)}, u32[]{:S(2)}) collective-permute-start(bf16[32,4224]{1,0:T(8,128)(2,1)S(1)} %collective-permute-done.1.refs_8_), channel_id=1, source_target_pairs={{0,2},{1,3},{2,0},{3,1},{4,6},{5,7},{6,4},{7,5},{8,10},{9,11},{10,... | collective-permute-start | bytes 811016 | tf_op jit(solution)/shard_map/ppermute | solution.py:477
  22.3 12.0 %collective-permute-start.6 = (bf16[32,4224]{1,0:T(8,128)(2,1)S(1)}, bf16[32,4224]{1,0:T(8,128)(2,1)S(1)}, u32[]{:S(2)}, u32[]{:S(2)}) collective-permute-start(bf16[32,4224]{1,0:T(8,128)(2,1)S(1)} %collective-permute-done.1.refs_8_), channel_id=1, source_target_pairs={{0,4},{1,5},{2,6},{3,7},{4,0},{5,1},{6,2},{7,3},{8,12},{9,13},{10,... | collective-permute-start | bytes 811016 | tf_op jit(solution)/shard_map/ppermute | solution.py:477
  22.7 11.6 %collective-permute-start.7 = (bf16[32,4224]{1,0:T(8,128)(2,1)S(1)}, bf16[32,4224]{1,0:T(8,128)(2,1)S(1)}, u32[]{:S(2)}, u32[]{:S(2)}) collective-permute-start(bf16[32,4224]{1,0:T(8,128)(2,1)S(1)} %collective-permute-done.2.refs_4_), channel_id=1, source_target_pairs={{0,2},{1,3},{2,0},{3,1},{4,6},{5,7},{6,4},{7,5},{8,10},{9,11},{10,... | collective-permute-start | bytes 811016 | tf_op jit(solution)/shard_map/ppermute | solution.py:477
  34.3 13.5 %collective-permute-start.13 = (bf16[32,4224]{1,0:T(8,128)(2,1)S(1)}, bf16[32,4224]{1,0:T(8,128)(2,1)S(1)}, u32[]{:S(2)}, u32[]{:S(2)}) collective-permute-start(bf16[32,4224]{1,0:T(8,128)(2,1)S(1)} %collective-permute-done.6.refs_12_), channel_id=1, source_target_pairs={{0,2},{1,3},{2,0},{3,1},{4,6},{5,7},{6,4},{7,5},{8,10},{9,11},{10,... | collective-permute-start | bytes 811016 | tf_op jit(solution)/shard_map/ppermute | solution.py:477
  34.9 13.1 %collective-permute-start = (bf16[32,4224]{1,0:T(8,128)(2,1)S(1)}, bf16[32,4224]{1,0:T(8,128)(2,1)S(1)}, u32[]{:S(2)}, u32[]{:S(2)}) collective-permute-start(bf16[32,4224]{1,0:T(8,128)(2,1)S(1)} %copy-done.3), channel_id=1, source_target_pairs={{0,1},{1,0},{2,3},{3,2},{4,5},{5,4},{6,7},{7,6},{8,9},{9,8},{10,11... | collective-permute-start | bytes 811016 | tf_op jit(solution)/shard_map/ppermute | solution.py:477
  34.9 13.6 %collective-permute-start.4 = (bf16[32,4224]{1,0:T(8,128)(2,1)S(1)}, bf16[32,4224]{1,0:T(8,128)(2,1)S(1)}, u32[]{:S(2)}, u32[]{:S(2)}) collective-permute-start(bf16[32,4224]{1,0:T(8,128)(2,1)S(1)} %collective-permute-done.3.refs_2_), channel_id=1, source_target_pairs={{0,1},{1,0},{2,3},{3,2},{4,5},{5,4},{6,7},{7,6},{8,9},{9,8},{10,11... | collective-permute-start | bytes 811016 | tf_op jit(solution)/shard_map/ppermute | solution.py:477
  35.4 13.1 %collective-permute-start.5 = (bf16[32,4224]{1,0:T(8,128)(2,1)S(1)}, bf16[32,4224]{1,0:T(8,128)(2,1)S(1)}, u32[]{:S(2)}, u32[]{:S(2)}) collective-permute-start(bf16[32,4224]{1,0:T(8,128)(2,1)S(1)} %collective-permute-done.2.refs_4_), channel_id=1, source_target_pairs={{0,1},{1,0},{2,3},{3,2},{4,5},{5,4},{6,7},{7,6},{8,9},{9,8},{10,11... | collective-permute-start | bytes 811016 | tf_op jit(solution)/shard_map/ppermute | solution.py:477
  35.5 13.9 %collective-permute-start.10 = (bf16[32,4224]{1,0:T(8,128)(2,1)S(1)}, bf16[32,4224]{1,0:T(8,128)(2,1)S(1)}, u32[]{:S(2)}, u32[]{:S(2)}) collective-permute-start(bf16[32,4224]{1,0:T(8,128)(2,1)S(1)} %collective-permute-done.1.refs_8_), channel_id=1, source_target_pairs={{0,1},{1,0},{2,3},{3,2},{4,5},{5,4},{6,7},{7,6},{8,9},{9,8},{10,11... | collective-permute-start | bytes 811016 | tf_op jit(solution)/shard_map/ppermute | solution.py:477
  47.9 2.4 %collective-permute-start.12 = (bf16[32,4224]{1,0:T(8,128)(2,1)S(1)}, bf16[32,4224]{1,0:T(8,128)(2,1)S(1)}, u32[]{:S(2)}, u32[]{:S(2)}) collective-permute-start(bf16[32,4224]{1,0:T(8,128)(2,1)S(1)} %collective-permute-done.6.refs_12_), channel_id=1, source_target_pairs={{0,1},{1,0},{2,3},{3,2},{4,5},{5,4},{6,7},{7,6},{8,9},{9,8},{10,11... | collective-permute-start | bytes 811016 | tf_op jit(solution)/shard_map/ppermute | solution.py:477
  48.0 1.9 %collective-permute-start.9 = (bf16[32,4224]{1,0:T(8,128)(2,1)S(1)}, bf16[32,4224]{1,0:T(8,128)(2,1)S(1)}, u32[]{:S(2)}, u32[]{:S(2)}) collective-permute-start(bf16[32,4224]{1,0:T(8,128)(2,1)S(1)} %collective-permute-done.7.refs_6_), channel_id=1, source_target_pairs={{0,1},{1,0},{2,3},{3,2},{4,5},{5,4},{6,7},{7,6},{8,9},{9,8},{10,11... | collective-permute-start | bytes 811016 | tf_op jit(solution)/shard_map/ppermute | solution.py:477
  48.5 1.8 %collective-permute-start.11 = (bf16[32,4224]{1,0:T(8,128)(2,1)S(1)}, bf16[32,4224]{1,0:T(8,128)(2,1)S(1)}, u32[]{:S(2)}, u32[]{:S(2)}) collective-permute-start(bf16[32,4224]{1,0:T(8,128)(2,1)S(1)} %collective-permute-done.8.refs_10_), channel_id=1, source_target_pairs={{0,1},{1,0},{2,3},{3,2},{4,5},{5,4},{6,7},{7,6},{8,9},{9,8},{10,11... | collective-permute-start | bytes 811016 | tf_op jit(solution)/shard_map/ppermute | solution.py:477
  48.7 2.0 %collective-permute-start.14 = (bf16[32,4224]{1,0:T(8,128)(2,1)S(1)}, bf16[32,4224]{1,0:T(8,128)(2,1)S(1)}, u32[]{:S(2)}, u32[]{:S(2)}) collective-permute-start(bf16[32,4224]{1,0:T(8,128)(2,1)S(1)} %collective-permute-done.13.refs_14_), channel_id=1, source_target_pairs={{0,1},{1,0},{2,3},{3,2},{4,5},{5,4},{6,7},{7,6},{8,9},{9,8},{10,11... | collective-permute-start | bytes 811016 | tf_op jit(solution)/shard_map/ppermute | solution.py:477
  51.0 20.1 %slice-start = ((s8[8388608]{0:T(1024)(128)(4,1)}), s8[4194304]{0:T(1024)(128)(4,1)S(1)}, s32[]{:S(2)}) async-start(s8[8388608]{0:T(1024)(128)(4,1)} %bitcast.15), calls=%async_computation | async-start | bytes 8388608
  52.2 18.9 %copy-start.1 = (s32[32]{0:T(128)S(1)}, s32[32]{0:T(128)}, u32[]{:S(2)}) copy-start(s32[32]{0:T(128)} %lengths.1) | copy-start | bytes 388
  67.6 1.8 %collective-permute-start.15 = (bf16[32,4096]{1,0:T(8,128)(2,1)}, bf16[32,4096]{1,0:T(8,128)(2,1)S(1)}, u32[]{:S(2)}, u32[]{:S(2)}) collective-permute-start(bf16[32,4096]{1,0:T(8,128)(2,1)} %get-tuple-element.64), channel_id=1, source_target_pairs={{0,1},{1,0},{2,3},{3,2},{4,5},{5,4},{6,7},{7,6},{8,9},{9,8},{10,11... | collective-permute-start | bytes 786440 | tf_op jit(solution)/shard_map/ppermute | solution.py:477
  69.5 8.4 %collective-permute-start.16 = (bf16[32,4096]{1,0:T(8,128)(2,1)S(1)}, bf16[32,4096]{1,0:T(8,128)(2,1)S(1)}, u32[]{:S(2)}, u32[]{:S(2)}) collective-permute-start(bf16[32,4096]{1,0:T(8,128)(2,1)S(1)} %add_convert_fusion.7), channel_id=1, source_target_pairs={{0,2},{1,3},{2,0},{3,1},{4,6},{5,7},{6,4},{7,5},{8,10},{9,11},{10,... | collective-permute-start | bytes 786440 | tf_op jit(solution)/shard_map/ppermute | solution.py:477
  71.0 6.8 %collective-permute-start.19 = (bf16[32,4096]{1,0:T(8,128)(2,1)S(1)}, bf16[32,4096]{1,0:T(8,128)(2,1)S(1)}, u32[]{:S(2)}, u32[]{:S(2)}) collective-permute-start(bf16[32,4096]{1,0:T(8,128)(2,1)S(1)} %get-tuple-element.78), channel_id=1, source_target_pairs={{0,1},{1,0},{2,3},{3,2},{4,5},{5,4},{6,7},{7,6},{8,9},{9,8},{10,11... | collective-permute-start | bytes 786440 | tf_op jit(solution)/shard_map/ppermute | solution.py:477
  76.0 23.1 %collective-permute-start.17 = (bf16[32,4096]{1,0:T(8,128)(2,1)S(1)}, bf16[32,4096]{1,0:T(8,128)(2,1)S(1)}, u32[]{:S(2)}, u32[]{:S(2)}) collective-permute-start(bf16[32,4096]{1,0:T(8,128)(2,1)S(1)} %get-tuple-element.76), channel_id=1, source_target_pairs={{0,1},{1,0},{2,3},{3,2},{4,5},{5,4},{6,7},{7,6},{8,9},{9,8},{10,11... | collective-permute-start | bytes 786440 | tf_op jit(solution)/shard_map/ppermute | solution.py:477
  76.5 14.6 %collective-permute-start.18 = (bf16[32,4096]{1,0:T(8,128)(2,1)S(1)}, bf16[32,4096]{1,0:T(8,128)(2,1)S(1)}, u32[]{:S(2)}, u32[]{:S(2)}) collective-permute-start(bf16[32,4096]{1,0:T(8,128)(2,1)S(1)} %get-tuple-element.77), channel_id=1, source_target_pairs={{0,1},{1,0},{2,3},{3,2},{4,5},{5,4},{6,7},{7,6},{8,9},{9,8},{10,11... | collective-permute-start | bytes 786440 | tf_op jit(solution)/shard_map/ppermute | solution.py:477
  76.5 2.0 %collective-permute-start.21 = (bf16[32,4096]{1,0:T(8,128)(2,1)S(1)}, bf16[32,4096]{1,0:T(8,128)(2,1)S(1)}, u32[]{:S(2)}, u32[]{:S(2)}) collective-permute-start(bf16[32,4096]{1,0:T(8,128)(2,1)S(1)} %get-tuple-element.81), channel_id=1, source_target_pairs={{0,1},{1,0},{2,3},{3,2},{4,5},{5,4},{6,7},{7,6},{8,9},{9,8},{10,11... | collective-permute-start | bytes 786440 | tf_op jit(solution)/shard_map/ppermute | solution.py:477
  77.9 15.0 %collective-permute-start.24 = (bf16[32,4096]{1,0:T(8,128)(2,1)S(1)}, bf16[32,4096]{1,0:T(8,128)(2,1)S(1)}, u32[]{:S(2)}, u32[]{:S(2)}) collective-permute-start(bf16[32,4096]{1,0:T(8,128)(2,1)S(1)} %get-tuple-element.85), channel_id=1, source_target_pairs={{0,1},{1,0},{2,3},{3,2},{4,5},{5,4},{6,7},{7,6},{8,9},{9,8},{10,11... | collective-permute-start | bytes 786440 | tf_op jit(solution)/shard_map/ppermute | solution.py:477
  77.9 1.9 %collective-permute-start.25 = (bf16[32,4096]{1,0:T(8,128)(2,1)S(1)}, bf16[32,4096]{1,0:T(8,128)(2,1)S(1)}, u32[]{:S(2)}, u32[]{:S(2)}) collective-permute-start(bf16[32,4096]{1,0:T(8,128)(2,1)S(1)} %get-tuple-element.86), channel_id=1, source_target_pairs={{0,1},{1,0},{2,3},{3,2},{4,5},{5,4},{6,7},{7,6},{8,9},{9,8},{10,11... | collective-permute-start | bytes 786440 | tf_op jit(solution)/shard_map/ppermute | solution.py:477
  78.5 2.9 %collective-permute-start.28 = (bf16[32,4096]{1,0:T(8,128)(2,1)S(1)}, bf16[32,4096]{1,0:T(8,128)(2,1)S(1)}, u32[]{:S(2)}, u32[]{:S(2)}) collective-permute-start(bf16[32,4096]{1,0:T(8,128)(2,1)S(1)} %get-tuple-element.90), channel_id=1, source_target_pairs={{0,1},{1,0},{2,3},{3,2},{4,5},{5,4},{6,7},{7,6},{8,9},{9,8},{10,11... | collective-permute-start | bytes 786440 | tf_op jit(solution)/shard_map/ppermute | solution.py:477
  79.8 11.3 %collective-permute-start.20 = (bf16[32,4096]{1,0:T(8,128)(2,1)S(1)}, bf16[32,4096]{1,0:T(8,128)(2,1)S(1)}, u32[]{:S(2)}, u32[]{:S(2)}) collective-permute-start(bf16[32,4096]{1,0:T(8,128)(2,1)S(1)} %add_convert_fusion.6), channel_id=1, source_target_pairs={{0,4},{1,5},{2,6},{3,7},{4,0},{5,1},{6,2},{7,3},{8,12},{9,13},{10,... | collective-permute-start | bytes 786440 | tf_op jit(solution)/shard_map/ppermute | solution.py:477
  81.4 8.1 %collective-permute-start.22 = (bf16[32,4096]{1,0:T(8,128)(2,1)S(1)}, bf16[32,4096]{1,0:T(8,128)(2,1)S(1)}, u32[]{:S(2)}, u32[]{:S(2)}) collective-permute-start(bf16[32,4096]{1,0:T(8,128)(2,1)S(1)} %add_convert_fusion.5), channel_id=1, source_target_pairs={{0,2},{1,3},{2,0},{3,1},{4,6},{5,7},{6,4},{7,5},{8,10},{9,11},{10,... | collective-permute-start | bytes 786440 | tf_op jit(solution)/shard_map/ppermute | solution.py:477
  89.6 7.2 %collective-permute-start.26 = (bf16[32,4096]{1,0:T(8,128)(2,1)S(1)}, bf16[32,4096]{1,0:T(8,128)(2,1)S(1)}, u32[]{:S(2)}, u32[]{:S(2)}) collective-permute-start(bf16[32,4096]{1,0:T(8,128)(2,1)S(1)} %add_convert_fusion.3), channel_id=1, source_target_pairs={{0,2},{1,3},{2,0},{3,1},{4,6},{5,7},{6,4},{7,5},{8,10},{9,11},{10,... | collective-permute-start | bytes 786440 | tf_op jit(solution)/shard_map/ppermute | solution.py:477
  91.3 13.6 %collective-permute-start.23 = (bf16[32,4096]{1,0:T(8,128)(2,1)S(1)}, bf16[32,4096]{1,0:T(8,128)(2,1)S(1)}, u32[]{:S(2)}, u32[]{:S(2)}) collective-permute-start(bf16[32,4096]{1,0:T(8,128)(2,1)S(1)} %add_convert_fusion.4), channel_id=1, source_target_pairs={{0,8},{1,9},{2,10},{3,11},{4,12},{5,13},{6,14},{7,15},{8,0},{9,1},... | collective-permute-start | bytes 786440 | tf_op jit(solution)/shard_map/ppermute | solution.py:477
  96.9 11.8 %collective-permute-start.27 = (bf16[32,4096]{1,0:T(8,128)(2,1)S(1)}, bf16[32,4096]{1,0:T(8,128)(2,1)S(1)}, u32[]{:S(2)}, u32[]{:S(2)}) collective-permute-start(bf16[32,4096]{1,0:T(8,128)(2,1)S(1)} %add_convert_fusion.2), channel_id=1, source_target_pairs={{0,4},{1,5},{2,6},{3,7},{4,0},{5,1},{6,2},{7,3},{8,12},{9,13},{10,... | collective-permute-start | bytes 786440 | tf_op jit(solution)/shard_map/ppermute | solution.py:477
  97.6 11.1 %collective-permute-start.29 = (bf16[32,4096]{1,0:T(8,128)(2,1)S(1)}, bf16[32,4096]{1,0:T(8,128)(2,1)S(1)}, u32[]{:S(2)}, u32[]{:S(2)}) collective-permute-start(bf16[32,4096]{1,0:T(8,128)(2,1)S(1)} %add_convert_fusion.1), channel_id=1, source_target_pairs={{0,2},{1,3},{2,0},{3,1},{4,6},{5,7},{6,4},{7,5},{8,10},{9,11},{10,... | collective-permute-start | bytes 786440 | tf_op jit(solution)/shard_map/ppermute | solution.py:477
  (20 other events, 173.6 us)

commit v3 on v2

v3 whole, which is shorter than its diff:
```python
import functools
import math

import jax
import jax.numpy as jnp
from jax import lax
from jax.experimental import pallas as pl
from jax.experimental.pallas import tpu as pltpu
from jax.sharding import PartitionSpec as P

HEADS = 32
KV_HEADS = 2
HEAD = 128
RANK = 16
LANES = 128
GROUP = 64
FLYING = 3
AHEAD = 2
BLOCK = 512
code_levels = (
    -1.0,
    -0.6961928009986877,
    -0.5250730514526367,
    -0.39491748809814453,
    -0.28444138169288635,
    -0.18477343022823334,
    -0.09105003625154495,
    0.0,
    0.07958029955625534,
    0.16093020141124725,
    0.24611230194568634,
    0.33791524171829224,
    0.44070982933044434,
    0.5626170039176941,
    0.7229568362236023,
    1.0,
)
adapter_scale = 2.0
norm_epsilon = 1e-06
f32 = jnp.float32
bf16 = jnp.bfloat16


def params(mib):
    return pltpu.CompilerParams(vmem_limit_bytes=mib * 2**20)


def whole(shape):
    return pl.BlockSpec(shape, lambda *_: (0,) * len(shape))


def norm_kernel(hidden, gain, routes, scores, out):
    rows, width = hidden.shape
    wide = hidden[...].astype(f32)
    spread = jnp.mean(wide * wide, axis=-1, keepdims=True)
    normed = wide * lax.rsqrt(spread + norm_epsilon) * gain[...].astype(f32).reshape(1, width)
    out[:, :width] = normed.astype(bf16)
    logits = scores[...]
    parts = jnp.exp(logits - jnp.max(logits, axis=0, keepdims=True))
    shares = parts / jnp.sum(parts, axis=0, keepdims=True)
    place = lax.broadcasted_iota(jnp.int32, (LANES, rows), 0)
    named = place & (LANES // 2 - 1)
    table = jnp.zeros((LANES, rows), f32)
    for k in range(routes.shape[0]):
        table = table + jnp.where(routes[k : k + 1, :] == named, shares[k : k + 1, :], 0.0)
    high = table.astype(bf16).astype(f32)
    both = jnp.where(place < LANES // 2, high, table - high).astype(bf16)
    out[:, width:] = lax.dot_general(
        unit(rows), both, (((1,), (1,)), ((), ())), preferred_element_type=f32
    ).astype(bf16)


def unit(size):
    row = lax.broadcasted_iota(jnp.int32, (size, size), 0)
    return (row == lax.broadcasted_iota(jnp.int32, (size, size), 1)).astype(f32).astype(bf16)


def norm_rows(hidden, gain, routes, scores):
    rows, width = hidden.shape
    top = routes.shape[1]
    return pl.pallas_call(
        norm_kernel,
        grid=(1,),
        in_specs=[whole((rows, width)), whole((width,)), whole((top, rows)), whole((top, rows))],
        out_specs=whole((rows, width + LANES)),
        out_shape=jax.ShapeDtypeStruct((rows, width + LANES), bf16),
        compiler_params=params(56),
    )(hidden, gain, routes.T, scores.T)


def level_tables():
    sub = lax.broadcasted_iota(jnp.int32, (8, LANES), 0)
    low = jnp.zeros((8, LANES), f32)
    high = low
    for i in range(8):
        low = jnp.where(sub == i, code_levels[i], low)
        high = jnp.where(sub == i, code_levels[i + 8], high)
    return low, high


def decode(tables, words, nibble):
    pieces = []
    for q in range(words.shape[0] // 8):
        word = words[8 * q : 8 * q + 8]
        entry = (word >> (4 * nibble)) & 7
        upper = (word & (8 << (4 * nibble))) != 0
        low = jnp.take_along_axis(tables[0], entry, axis=0, mode="promise_in_bounds")
        high = jnp.take_along_axis(tables[1], entry, axis=0, mode="promise_in_bounds")
        pieces.append(jnp.where(upper, high, low))
    return jnp.concatenate(pieces, axis=0)


def copy(source, target, sem):
    move = pltpu.make_async_copy(source, target, sem)
    move.start()
    return move


def enter_kernel(
    part, rows, codes, scale, down_map, up_map, before, held, out, made,
    words_of, scale_of, factors, down_of, up_of, spread, weights, small_sem, in_sem, out_sem,
):
    tiles = out.shape[0]
    third = codes.shape[2]
    half = tiles * LANES
    first = part * rows
    blocks = rows // BLOCK
    arriving = [
        copy(scale.at[0, pl.ds(first // GROUP, rows // GROUP)], scale_of, small_sem.at[0]),
        copy(down_map.at[:, pl.ds(first, rows)], down_of, small_sem.at[1]),
        copy(up_map.at[0], up_of, small_sem.at[2]),
    ]

    def arriving_words(k):
        here = pl.multiple_of(k * BLOCK, BLOCK)
        return pltpu.make_async_copy(
            codes.at[0, pl.ds(first + here, BLOCK)], words_of.at[pl.ds(here, BLOCK)], in_sem.at[k]
        )

    for k in range(AHEAD):
        arriving_words(k).start()
    made[...] = jnp.zeros_like(made)
    tables = level_tables()
    spread[...] = jnp.zeros_like(spread)
    for move in arriving:
        move.wait()
    for tile in range(tiles):
        for side in range(2):
            piece = up_of[side, :, tile * LANES : (tile + 1) * LANES].astype(f32) * adapter_scale
            spread[tile, side * RANK : (side + 1) * RANK, side * LANES : (side + 1) * LANES] = piece.astype(bf16)
    factors[...] = scale_of[...].astype(f32)
    scales = BLOCK // GROUP

    def leaving(k):
        here = pl.ds(pl.multiple_of(k * BLOCK, BLOCK), BLOCK)
        there = pl.ds(pl.multiple_of(first + k * BLOCK, BLOCK), BLOCK)
        return pltpu.make_async_copy(weights.at[:, here], out.at[:, there], out_sem.at[k])

    @pl.loop(0, blocks)
    def _(k):
        arriving_words(k).wait()

        @pl.when(k + AHEAD < blocks)
        def _():
            arriving_words(k + AHEAD).start()

        here = pl.multiple_of(k * BLOCK, BLOCK)
        for tile in range(tiles):
            adapter = lax.dot_general(
                down_of[:, pl.ds(here, BLOCK)],
                spread[tile],
                (((0,), (0,)), ((), ())),
                preferred_element_type=f32,
            )
            for side in range(2):
                column = side * half + tile * LANES
                nibble, offset = divmod(column, third)
                factor = factors[pl.ds(pl.multiple_of(k * scales, scales), scales), pl.ds(column, LANES)]
                for g in range(scales):
                    packed = words_of[pl.ds(here + g * GROUP, GROUP), pl.ds(offset, LANES)]
                    value = decode(tables, packed, nibble) * factor[g : g + 1]
                    value = value + adapter[g * GROUP : (g + 1) * GROUP, side * LANES : (side + 1) * LANES]
                    weights[tile, pl.ds(here + g * GROUP, GROUP), pl.ds(side * LANES, LANES)] = value.astype(bf16)
        leaving(k).start()

    @pl.loop(0, blocks)
    def _(k):
        leaving(k).wait()


def in_hbm(count):
    return [pl.BlockSpec(memory_space=pltpu.HBM)] * count


def enter_weights(part, parts, codes, scale, down_map, up_map, before, held):
    _, width, third = codes.shape
    tiles = 3 * third // 2 // LANES
    rows = width // parts
    return pl.pallas_call(
        functools.partial(enter_kernel, part, rows),
        in_specs=in_hbm(4) + [pl.BlockSpec(memory_space=pl.ANY)] * 2,
        out_specs=in_hbm(1) + [pl.BlockSpec(memory_space=pltpu.VMEM)],
        input_output_aliases={5: 0} if part else {},
        out_shape=[
            jax.ShapeDtypeStruct((tiles, width, 2 * LANES), bf16),
            jax.ShapeDtypeStruct((8, LANES), f32),
        ],
        scratch_shapes=[
            pltpu.VMEM((rows, third), jnp.int32),
            pltpu.VMEM((rows // GROUP, 3 * third), bf16),
            pltpu.VMEM((rows // GROUP, 3 * third), f32),
            pltpu.VMEM((2 * RANK, rows), bf16),
            pltpu.VMEM(up_map.shape[1:], bf16),
            pltpu.VMEM((tiles, 2 * RANK, 2 * LANES), bf16),
            pltpu.VMEM((tiles, rows, 2 * LANES), bf16),
            pltpu.SemaphoreType.DMA((3,)),
            pltpu.SemaphoreType.DMA((rows // BLOCK,)),
            pltpu.SemaphoreType.DMA((rows // BLOCK,)),
        ],
        compiler_params=params(56),
        cost_estimate=pl.CostEstimate(flops=4 * 10**9, bytes_accessed=20 * 10**6, transcendentals=0),
    )(codes, scale, down_map[0].T, up_map, before, held)


class Leave:
    def __init__(self, codes, scale, down_map, up_map, scratch):
        self.words, self.scale, self.down, self.up, self.weights, self.sems = scratch
        self.pairs = [
            (codes.at[0], self.words),
            (scale.at[0], self.scale),
            (down_map, self.down),
            (up_map.at[0], self.up),
        ]

    @staticmethod
    def scratch(codes, scale, up_map):
        _, third, width = codes.shape
        return [
            pltpu.VMEM((third, width), jnp.int32),
            pltpu.VMEM(scale.shape[1:], bf16),
            pltpu.VMEM((RANK, 3 * third), bf16),
            pltpu.VMEM(up_map.shape[1:], bf16),
            pltpu.VMEM((3 * third, width), bf16),
            pltpu.SemaphoreType.DMA((4,)),
        ]

    def start(self):
        self.moves = [copy(a, b, self.sems.at[i]) for i, (a, b) in enumerate(self.pairs)]

    def ready(self):
        for move in self.moves:
            move.wait()

    def decode(self, tables, strip, strips):
        rows = self.words.shape[0]
        first = strip * LANES if isinstance(strip, int) else pl.multiple_of(strip * LANES, LANES)
        adapter = lax.dot_general(
            self.down[...],
            self.up[:, pl.ds(first, strips * LANES)],
            (((0,), (0,)), ((), ())),
            preferred_element_type=f32,
        ) * adapter_scale
        for j in range(strips):
            here = pl.ds(first + j * LANES, LANES)
            for nibble in range(3):
                for g in range(rows // GROUP):
                    row = nibble * rows + g * GROUP
                    packed = self.words[pl.ds(g * GROUP, GROUP), here]
                    factor = self.scale[pl.ds(row // GROUP, 1), here].astype(f32)
                    value = decode(tables, packed, nibble) * factor
                    value = value + adapter[row : row + GROUP, j * LANES : (j + 1) * LANES]
                    self.weights[pl.ds(row, GROUP), here] = value.astype(bf16)


def pick_rows(own, tables, rows, slots):
    cap = rows // 2
    total = rows * len(tables)
    lane = lax.broadcasted_iota(jnp.int32, (rows, LANES), 1)
    columns = []
    for shift in (0, LANES // 2):
        parts = [
            jnp.sum(jnp.where(lane == own + shift, t, 0.0), axis=-1, keepdims=True) for t in tables
        ]
        column = jnp.concatenate(parts, axis=0)
        columns.append(jnp.broadcast_to(column, (total, slots)))
    high, low = columns
    hit = (high != 0.0).astype(f32).astype(bf16)
    high, low = high.astype(bf16), low.astype(bf16)
    row = lax.broadcasted_iota(jnp.int32, (total, total), 0)
    column = lax.broadcasted_iota(jnp.int32, (total, total), 1)
    before = ((row // rows == column // rows) & (row < column)).astype(f32).astype(bf16)
    first = (((0,), (0,)), ((), ()))
    rank_of = lax.dot_general(hit, before, first, preferred_element_type=f32)
    hit_of = lax.dot_general(hit, unit(total), first, preferred_element_type=f32)
    slot = lax.broadcasted_iota(jnp.int32, (slots, total), 0)
    place = lax.broadcasted_iota(jnp.int32, (slots, total), 1)
    taken = (slot // cap == place // rows) & (rank_of == (slot % cap).astype(f32)) & (hit_of > 0.5)
    gather = taken.astype(f32).astype(bf16)
    weight = jnp.dot(gather, high, preferred_element_type=f32)
    weight = weight + jnp.dot(gather, low, preferred_element_type=f32)
    rank = lax.dot_general(before, hit, first, preferred_element_type=f32)
    slot = lax.broadcasted_iota(jnp.int32, (total, slots), 1)
    place = lax.broadcasted_iota(jnp.int32, (total, slots), 0)
    taken = (slot // cap == place // rows) & (rank == (slot % cap).astype(f32)) & (hit.astype(f32) > 0.5)
    return gather, taken.astype(f32).astype(bf16), weight


def expert_kernel(count, own, *refs):
    blocks, refs = refs[:count], refs[count:]
    enter, codes, scale, down_map, up_map, _ = refs[:6]
    outs, refs = refs[6 : count + 6], refs[count + 6 :]
    picked, spread, weight, active, enter_of, enter_sem = refs[:6]
    leave = Leave(codes, scale, down_map, up_map, refs[6:])
    leave.start()
    rows = blocks[0].shape[0]
    width = picked.shape[1]
    sets, span, slots = spread.shape
    tiles = enter_of.shape[0]
    each = count // sets
    wide = 8 * LANES

    def arriving(tile):
        return pltpu.make_async_copy(enter.at[tile], enter_of.at[tile], enter_sem.at[tile])

    for tile in range(FLYING):
        arriving(tile).start()
    for g in range(sets):
        members = blocks[g * each : (g + 1) * each]
        tables = [member[:, width:].astype(f32) for member in members]
        gather, scatter, factor = pick_rows(own[0], tables, rows, slots)
        here = pl.ds(g * slots, slots)
        spread[g] = scatter
        weight[here, :] = factor
        for n in range(width // wide):
            lanes = pl.ds(n * wide, wide)
            source = jnp.concatenate([member[:, lanes] for member in members], axis=0)
            picked[here, lanes] = jnp.dot(gather, source, preferred_element_type=f32).astype(bf16)
    levels = level_tables()
    leave.ready()
    strips = width // LANES
    per_tile = strips // tiles

    @pl.loop(0, tiles)
    def _(tile):
        arriving(tile).wait()

        @pl.when(tile + FLYING < tiles)
        def _():
            arriving(tile + FLYING).start()

        joined = jnp.dot(picked[...], enter_of[tile], preferred_element_type=f32)
        leave.decode(levels, tile * per_tile, per_tile)
        gate = joined[:, :LANES]
        value = gate / (1.0 + jnp.exp(-gate)) * joined[:, LANES:]
        active[tile] = value.astype(bf16)

    if tiles * per_tile < strips:
        leave.decode(levels, tiles * per_tile, strips - tiles * per_tile)

    @pl.loop(0, width // wide)
    def _(n):
        lanes = pl.ds(pl.multiple_of(n * wide, wide), wide)
        entry = jnp.concatenate([active[t] for t in range(tiles)], axis=1)
        factor = jnp.concatenate([weight[...]] * (wide // slots), axis=1)
        result = jnp.dot(entry, leave.weights[:, lanes], preferred_element_type=f32)
        result = (result * factor).astype(bf16)
        for g in range(sets):
            own_rows = result[g * slots : (g + 1) * slots]
            full = jnp.dot(spread[g], own_rows, preferred_element_type=f32).astype(bf16)
            for b in range(each):
                outs[g * each + b][:, lanes] = full[b * rows : (b + 1) * rows]


def expert(own, blocks, enter, codes, scale, down_map, up_map, before):
    count = len(blocks)
    tiles = enter.shape[0]
    rows, padded = blocks[0].shape
    width = padded - LANES
    each = LANES // (rows // 2)
    sets = count // each
    vmem = pl.BlockSpec(memory_space=pltpu.VMEM)
    return pl.pallas_call(
        functools.partial(expert_kernel, count),
        in_specs=[pl.BlockSpec(memory_space=pltpu.SMEM)]
        + [vmem] * count
        + in_hbm(5)
        + [pl.BlockSpec(memory_space=pl.ANY)],
        out_specs=[vmem] * count,
        out_shape=[jax.ShapeDtypeStruct((rows, width), bf16)] * count,
        scratch_shapes=[
            pltpu.VMEM((sets * LANES, width), bf16),
            pltpu.VMEM((sets, each * rows, LANES), bf16),
            pltpu.VMEM((sets * LANES, LANES), f32),
            pltpu.VMEM((tiles, sets * LANES, LANES), bf16),
            pltpu.VMEM(enter.shape, bf16),
            pltpu.SemaphoreType.DMA((tiles,)),
        ]
        + Leave.scratch(codes, scale, up_map),
        compiler_params=params(46),
        cost_estimate=pl.CostEstimate(flops=8 * 10**9, bytes_accessed=22 * 10**6, transcendentals=0),
    )(own, *blocks, enter, codes, scale, down_map[0].T, up_map, before)


def attend_kernel(
    lengths, queries, fresh, cache, _, out, queries_of, fresh_of, cache_of, small_sem, cache_sem, *, first, block
):
    rows = out.shape[0]
    mine = pl.ds(first, rows)
    scaling = 1.0 / math.sqrt(HEAD)
    positions = cache.shape[2]
    small = [copy(queries.at[mine], queries_of, small_sem.at[0]), copy(fresh.at[mine], fresh_of, small_sem.at[1])]

    def arriving(k):
        there = pl.ds(first + k * block, block)
        return pltpu.make_async_copy(cache.at[there], cache_of.at[pl.ds(k * block, block)], cache_sem.at[k])

    for k in range(rows // block):
        arriving(k).start()
    lower = lax.broadcasted_iota(jnp.int32, (HEADS, HEAD), 0) < HEADS // KV_HEADS
    place = lax.broadcasted_iota(jnp.int32, (HEADS, positions), 1)
    own_half = lambda both: jnp.where(lower, both[:, :HEAD], both[:, HEAD:])
    for move in small:
        move.wait()

    @pl.loop(0, rows // block)
    def _(k):
        arriving(k).wait()
        old, new = [], []
        for t in range(block):
            row = k * block + t
            query = queries_of[row]
            zero = jnp.zeros_like(query)
            both = jnp.concatenate([jnp.where(lower, query, zero), jnp.where(lower, zero, query)], axis=1)
            score = lax.dot_general(
                both, cache_of[row, 0], (((1,), (1,)), ((), ())), preferred_element_type=f32
            )
            old.append(jnp.where(place < lengths[first + row], score * scaling, -jnp.inf))
            key = own_half(fresh_of[row, 0:1, :].astype(f32))
            new.append(jnp.sum(query.astype(f32) * key, axis=-1, keepdims=True) * scaling)
        old, new = jnp.concatenate(old, axis=0), jnp.concatenate(new, axis=0)
        highest = jnp.maximum(jnp.max(old, axis=-1, keepdims=True), new)
        old = jnp.exp(old - highest)
        new = jnp.exp(new - highest)
        inverse = 1.0 / (jnp.sum(old, axis=-1, keepdims=True) + new)
        old = (old * inverse).astype(bf16)
        new = (new * inverse).astype(bf16).astype(f32)
        for t in range(block):
            row = k * block + t
            heads = slice(t * HEADS, (t + 1) * HEADS)
            blended = own_half(jnp.dot(old[heads], cache_of[row, 1], preferred_element_type=f32))
            out[row] = (blended + new[heads] * own_half(fresh_of[row, 1:2, :].astype(f32))).astype(bf16)


def attend(queries, fresh_key_value, key_value_cache, lengths, before, part, parts, block=8):
    rows = queries.shape[0] // parts
    return pl.pallas_call(
        functools.partial(attend_kernel, first=part * rows, block=block),
        in_specs=[pl.BlockSpec(memory_space=pltpu.SMEM)] + in_hbm(3) + [pl.BlockSpec(memory_space=pl.ANY)],
        out_specs=pl.BlockSpec(memory_space=pltpu.VMEM),
        out_shape=jax.ShapeDtypeStruct((rows, HEADS, HEAD), bf16),
        scratch_shapes=[
            pltpu.VMEM((rows, HEADS, HEAD), bf16),
            pltpu.VMEM((rows, *fresh_key_value.shape[1:]), bf16),
            pltpu.VMEM((rows, *key_value_cache.shape[1:]), bf16),
            pltpu.SemaphoreType.DMA((2,)),
            pltpu.SemaphoreType.DMA((rows // block,)),
        ],
        compiler_params=params(49),
        cost_estimate=pl.CostEstimate(flops=5 * 10**8, bytes_accessed=20 * 10**6, transcendentals=0),
    )(lengths, queries, fresh_key_value, key_value_cache, before)


def swap(value, bit):
    count = lax.axis_size("ep")
    return lax.ppermute(value, "ep", [(i, i ^ bit) for i in range(count)])


def add(terms):
    return sum(term.astype(f32) for term in terms[1:]) + terms[0].astype(f32)


def shards(
    queries,
    fresh_key_value,
    key_value_cache,
    lengths,
    hidden,
    expert_norm_gain,
    routes,
    router_scores,
    gate_up_quant_codes,
    gate_up_code_scale,
    down_quant_codes,
    down_code_scale,
    adapter_input_down,
    adapter_input_up,
    adapter_output_down,
    adapter_output_up,
):
    count = lax.axis_size("ep")
    bits = [1 << b for b in range(count.bit_length() - 1)]
    rows = hidden.shape[0]
    blocks = {0: norm_rows(hidden, expert_norm_gain, routes, router_scores)}
    leave_args = (down_quant_codes, down_code_scale, adapter_output_down, adapter_output_up)

    heads = queries.reshape(rows, HEADS, HEAD)
    attention = functools.partial(attend, heads, fresh_key_value, key_value_cache, lengths, parts=2)

    def make_enter(part, before, held):
        return enter_weights(
            part, 2, gate_up_quant_codes, gate_up_code_scale, adapter_input_down, adapter_input_up, before, held
        )

    stage = lambda r: sum(1 for bit in bits[1:] if r & bit)
    low_bit = lambda r: r & -r
    even = [r for r in range(count) if r and r % 2 == 0]
    done = blocks[0]
    for now in range(max(stage(r) for r in even) + 1):
        for r in sorted(even, key=low_bit, reverse=True):
            if stage(r ^ low_bit(r)) == now:
                blocks[r] = swap(blocks[r ^ low_bit(r)], low_bit(r))
        for r in [0] + even:
            if stage(r) == now:
                blocks[r | 1] = swap(blocks[r], 1)
        arriving = [r for r in blocks if r % 2 == 0 and stage(r) == now + 1]
        held = [blocks[r] for r in arriving]
        if now < 2:
            weights, done = make_enter(now, done, weights if now else done)
        elif now == 2:
            done = context = attention(done, 0)
        *held, done = lax.optimization_barrier((*held, done))
        if now == 2:
            context = done
        blocks.update(zip(arriving, held))
    own = lax.axis_index("ep").astype(jnp.int32).reshape(1)
    produced = expert(own, [blocks[r] for r in range(count)], weights, *leave_args, done)

    tie = lambda *values: list(lax.optimization_barrier(values))
    sums = {r: [produced[r]] for r in range(0, count, 2)}
    first = count - 2
    sent = add([sums.pop(first)[0], swap(produced[first + 1], 1)]).astype(bf16)
    sent, *others = tie(sent, *[produced[r + 1] for r in sums])
    arrived = swap(sent, bits[1])
    for r, value in zip(sums, others):
        sums[r].append(swap(value, 1))
    early = (first - 2, first - 4)
    before, *held = tie(sent, *[sums[r][1] for r in early])
    for r, value in zip(early, held):
        sums[r][1] = value
    later = attention(before, 1)
    arrived, later = tie(arrived, later)
    context = jnp.concatenate([context, later]).reshape(rows, HEADS * HEAD)
    sums[first ^ bits[1]].append(arrived)
    for r in range(first - 2, 0, -4):
        pair = tie(*[add(sums.pop(q)).astype(bf16) for q in (r, r - 2)])
        for q, value in zip((r, r - 2), pair):
            sums[q ^ low_bit(q)].append(swap(value, low_bit(q)))
    return (context, add(sums[0]).astype(bf16))


def solution(mesh):
    return jax.shard_map(
        shards,
        mesh=mesh,
        in_specs=(
            P(("grp", "ep"), None),
            P(("grp", "ep"), None, None),
            P(("grp", "ep"), None, None, None),
            P(("grp", "ep")),
            P(("grp", "ep"), None),
            P(),
            P(("grp", "ep"), None),
            P(("grp", "ep"), None),
            P("ep", None, None),
            P("ep", None, None),
            P("ep", None, None),
            P("ep", None, None),
            P("ep", None, None),
            P("ep", None, None, None),
            P("ep", None, None),
            P("ep", None, None),
        ),
        out_specs=(P(("grp", "ep"), None), P(("grp", "ep"), None)),
        check_vma=False,
    )
```

time: 110 us -> 101 us (0.918)
  Pallas kernels: 53.3 us -> 47 us
  waiting for transfers between devices: 26.1 us -> 23.2 us
    pallas_call x5, Pallas kernels: 51.3 us -> 45.1 us  [the longest x2 19.2 us: enter_weights(): pl.pallas_call(functools.partial(enter_kernel, part, rows), in_specs=in_h...]
    ppermute x30, waiting for transfers between devices: 26.1 us -> 23.2 us  [swap(): return lax.ppermute(value, 'ep', [(i, i ^ bit) for i in range(count)])]
    unnamed x46 -> x18, local copies, waits for them, and re-layouts: 2.81 us -> 3.2 us
  transfers between devices with their start and end apart: 30 -> 30, of which waited for: 11 -> 13; matrix products, arithmetic and copies ran while one was open for 2% -> 1% of each run, Pallas kernels for 33% -> 27%
where the time goes in v3:
time: 101 us
  Pallas kernels  47 us (47%)
  starting transfers between devices  24.8 us (25%)
  waiting for transfers between devices  23.2 us (23%)
  local copies, waits for them, and re-layouts  3.2 us (3%)
  other arithmetic  1.49 us (1%)
    ppermute x30, starting transfers between devices, swap(): return lax.ppermute(value, 'ep', [(i, i ^ bit) for i in range(count)])  24.8 us
    ppermute x30, waiting for transfers between devices, swap(): return lax.ppermute(value, 'ep', [(i, i ^ bit) for i in range(count)])  23.2 us
    pallas_call x2, Pallas kernels, enter_weights(): pl.pallas_call(functools.partial(enter_kernel, part, rows), in_specs=in_h...  19.2 us
    pallas_call x1, Pallas kernels, expert(): pl.pallas_call(functools.partial(expert_kernel, count), in_specs=[pl.Bloc...  17.7 us
    pallas_call x2, Pallas kernels, attend(): pl.pallas_call(functools.partial(attend_kernel, first=part * rows, block=...  8.16 us
    unnamed x18, local copies, waits for them, and re-layouts  3.2 us
  transfers between devices with their start and end apart: 30, of which 13 were waited for; matrix products, arithmetic and copies ran while one was open for 1% of the time, Pallas kernels for 27%

profile of v3, /device:TPU:0, one launch (start us, length us, event | category | flops | bytes accessed | tf_op | source)
XLA Modules:
  0.0 100.6 jit_solution(13408000376194945039)
XLA Ops:
  0.6 1.9 %shard_map.167.before.held.refs_0_ = bf16[32,4224]{1,0:T(8,128)(2,1)} custom-call(bf16[32,4096]{1,0:T(8,128)(2,1)} %hidden.1, bf16[4096]{0:T(1024)(128)(2,1)} %gain.1, s32[8,32]{1,0:T(8,128)} %bitcast.23, f32[8,32]{1,0:T(8,128)} %bitcast.24), custom_call_target="tpu_custom_call" | custom-call | tf_op jit(solution)/shard_map/pallas_call | solution.py:81
  2.6 4.0 %collective-permute-start = (bf16[32,4224]{1,0:T(8,128)(2,1)}, bf16[32,4224]{1,0:T(8,128)(2,1)S(1)}, u32[]{:S(2)}, u32[]{:S(2)}) collective-permute-start(bf16[32,4224]{1,0:T(8,128)(2,1)} %shard_map.167.before.held.refs_0_), channel_id=1, source_target_pairs={{0,8},{1,9},{2,10},{3,11},{4,12},{5,13},{6,14},{7,15},{8,0},{9,1},... | collective-permute-start | bytes 811016 | tf_op jit(solution)/shard_map/ppermute | solution.py:475
  6.6 1.6 %collective-permute-start.1 = (bf16[32,4224]{1,0:T(8,128)(2,1)}, bf16[32,4224]{1,0:T(8,128)(2,1)S(1)}, u32[]{:S(2)}, u32[]{:S(2)}) collective-permute-start(bf16[32,4224]{1,0:T(8,128)(2,1)} %shard_map.167.before.held.refs_0_), channel_id=1, source_target_pairs={{0,4},{1,5},{2,6},{3,7},{4,0},{5,1},{6,2},{7,3},{8,12},{9,13},{10,... | collective-permute-start | bytes 811016 | tf_op jit(solution)/shard_map/ppermute | solution.py:475
  8.2 1.5 %collective-permute-start.2 = (bf16[32,4224]{1,0:T(8,128)(2,1)}, bf16[32,4224]{1,0:T(8,128)(2,1)S(1)}, u32[]{:S(2)}, u32[]{:S(2)}) collective-permute-start(bf16[32,4224]{1,0:T(8,128)(2,1)} %shard_map.167.before.held.refs_0_), channel_id=1, source_target_pairs={{0,2},{1,3},{2,0},{3,1},{4,6},{5,7},{6,4},{7,5},{8,10},{9,11},{10,... | collective-permute-start | bytes 811016 | tf_op jit(solution)/shard_map/ppermute | solution.py:475
  9.7 9.6 %shard_map.168 = (bf16[6,4096,256]{2,1,0:T(8,128)(2,1)}, f32[8,128]{1,0:T(8,128)}) custom-call(s32[1,4096,512]{2,1,0:T(8,128)} %codes.3, bf16[1,64,1536]{2,1,0:T(8,128)(2,1)} %scale.3, bf16[32,4096]{1,0:T(8,128)(2,1)} %bitcast.19, bf16[1,2,16,768]{3,2,1,0:T(8,128)(2,1)} %up_map.3, bf16[32,4224]{1,0:T(8,128)(2,1)} %shard_map.167.before.held.refs_0_, ...), custom_call_target="tpu_custom_call" | custom-call | flops 4000000000 | bytes 20000000 | tf_op jit(solution)/shard_map/pallas_call | solution.py:199
  19.4 1.5 %collective-permute-start.3 = (bf16[32,4224]{1,0:T(8,128)(2,1)S(1)}, bf16[32,4224]{1,0:T(8,128)(2,1)S(1)}, u32[]{:S(2)}, u32[]{:S(2)}) collective-permute-start(bf16[32,4224]{1,0:T(8,128)(2,1)S(1)} %collective-permute-done.refs_8_), channel_id=1, source_target_pairs={{0,4},{1,5},{2,6},{3,7},{4,0},{5,1},{6,2},{7,3},{8,12},{9,13},{10,... | collective-permute-start | bytes 811016 | tf_op jit(solution)/shard_map/ppermute | solution.py:475
  20.9 1.5 %collective-permute-start.5 = (bf16[32,4224]{1,0:T(8,128)(2,1)S(1)}, bf16[32,4224]{1,0:T(8,128)(2,1)S(1)}, u32[]{:S(2)}, u32[]{:S(2)}) collective-permute-start(bf16[32,4224]{1,0:T(8,128)(2,1)S(1)} %collective-permute-done.refs_8_), channel_id=1, source_target_pairs={{0,2},{1,3},{2,0},{3,1},{4,6},{5,7},{6,4},{7,5},{8,10},{9,11},{10,... | collective-permute-start | bytes 811016 | tf_op jit(solution)/shard_map/ppermute | solution.py:475
  22.9 9.6 %shard_map.169 = (bf16[6,4096,256]{2,1,0:T(8,128)(2,1)}, f32[8,128]{1,0:T(8,128)}) custom-call(s32[1,4096,512]{2,1,0:T(8,128)} %codes.3, bf16[1,64,1536]{2,1,0:T(8,128)(2,1)} %scale.3, bf16[32,4096]{1,0:T(8,128)(2,1)} %bitcast.20, bf16[1,2,16,768]{3,2,1,0:T(8,128)(2,1)} %up_map.3, ...), custom_call_target="tpu_custom_call", output_to_operand_aliasing={{0}: (5, {})} | custom-call | flops 4000000000 | bytes 20000000 | tf_op jit(solution)/shard_map/pallas_call | solution.py:199
  32.6 1.3 %collective-permute-done.4.refs_6_ = bf16[32,4224]{1,0:T(8,128)(2,1)S(1)} collective-permute-done((bf16[32,4224]{1,0:T(8,128)(2,1)S(1)}, bf16[32,4224]{1,0:T(8,128)(2,1)S(1)}, u32[]{:S(2)}, u32[]{:S(2)}) %collective-permute-start.4) | collective-permute-done | bytes 270368 | tf_op jit(solution)/shard_map/ppermute | solution.py:475
  33.8 1.5 %collective-permute-start.6 = (bf16[32,4224]{1,0:T(8,128)(2,1)S(1)}, bf16[32,4224]{1,0:T(8,128)(2,1)}, u32[]{:S(2)}, u32[]{:S(2)}) collective-permute-start(bf16[32,4224]{1,0:T(8,128)(2,1)S(1)} %collective-permute-done.3.refs_12_), channel_id=1, source_target_pairs={{0,2},{1,3},{2,0},{3,1},{4,6},{5,7},{6,4},{7,5},{8,10},{9,11},{10,... | collective-permute-start | bytes 811016 | tf_op jit(solution)/shard_map/ppermute | solution.py:475
  35.9 0.6 collective-permute-start.8
  36.5 0.7 copy-done.2
  37.2 4.1 %shard_map.170.refs_21_ = bf16[16,32,128]{2,1,0:T(8,128)(2,1)S(1)} custom-call(s32[32]{0:T(128)S(1)} %copy-done.3, bf16[32,32,128]{2,1,0:T(8,128)(2,1)S(1)} %bitcast.15, bf16[32,2,256]{2,1,0:T(2,128)(2,1)S(1)} %copy-done.1, bf16[32,2,256,256]{3,2,1,0:T(8,128)(2,1)} %cache.3, f32[8,128]{1,0:T(8,128)S(1)} %copy-done.2), custom_call_target="tpu_custom_call" | custom-call | flops 500000000 | bytes 20000000 | tf_op jit(solution)/shard_map/pallas_call | solution.py:456
  42.4 0.6 collective-permute-done.13.refs_13_
  43.4 0.8 collective-permute-done.12.refs_11_
  44.4 0.9 copy-done.5
  45.3 0.7 copy-done.6
  46.1 17.7 %shard_map.171 = (bf16[32,4096]{1,0:T(8,128)(2,1)S(1)}, bf16[32,4096]{1,0:T(8,128)(2,1)S(1)}, bf16[32,4096]{1,0:T(8,128)(2,1)S(1)}, bf16[32,4096]{1,0:T(8,128)(2...) custom-call(s32[1]{0:T(128)} %bitcast.5.own, ...), custom_call_target="tpu_custom_call" | custom-call | flops 8000000000 | bytes 22000000 | tf_op jit(solution)/shard_map/pallas_call | solution.py:382
  64.0 1.4 %collective-permute-done.15 = bf16[32,4096]{1,0:T(8,128)(2,1)S(1)} collective-permute-done((bf16[32,4096]{1,0:T(8,128)(2,1)S(1)}, bf16[32,4096]{1,0:T(8,128)(2,1)S(1)}, u32[]{:S(2)}, u32[]{:S(2)}) %collective-permute-start.15) | collective-permute-done | bytes 262176 | tf_op jit(solution)/shard_map/ppermute | solution.py:475
  66.0 0.6 collective-permute-start.16
  67.6 4.1 %shard_map.172 = bf16[16,32,128]{2,1,0:T(8,128)(2,1)S(1)} custom-call(s32[32]{0:T(128)S(1)} %copy-done.3, bf16[32,32,128]{2,1,0:T(8,128)(2,1)S(1)} %bitcast.16, bf16[32,2,256]{2,1,0:T(2,128)(2,1)S(1)} %copy-done.1, bf16[32,2,256,256]{3,2,1,0:T(8,128)(2,1)} %cache.3, bf16[32,4096]{1,0:T(8,128)(2,1)S(1)} %add_convert_fusion.7._), custom_call_target="tpu_custom_call" | custom-call | flops 500000000 | bytes 20000000 | tf_op jit(solution)/shard_map/pallas_call | solution.py:456
  71.7 2.7 %collective-permute-done.16 = bf16[32,4096]{1,0:T(8,128)(2,1)S(1)} collective-permute-done((bf16[32,4096]{1,0:T(8,128)(2,1)S(1)}, bf16[32,4096]{1,0:T(8,128)(2,1)S(1)}, u32[]{:S(2)}, u32[]{:S(2)}) %collective-permute-start.16) | collective-permute-done | bytes 262176 | tf_op jit(solution)/shard_map/ppermute | solution.py:475
  75.0 0.7 collective-permute-start.22
  75.8 6.3 %collective-permute-done.21 = bf16[32,4096]{1,0:T(8,128)(2,1)S(1)} collective-permute-done((bf16[32,4096]{1,0:T(8,128)(2,1)S(1)}, bf16[32,4096]{1,0:T(8,128)(2,1)S(1)}, u32[]{:S(2)}, u32[]{:S(2)}) %collective-permute-start.21) | collective-permute-done | bytes 262176 | tf_op jit(solution)/shard_map/ppermute | solution.py:475
  82.4 0.7 collective-permute-start.26
  83.2 4.3 %collective-permute-start.24 = (bf16[32,4096]{1,0:T(8,128)(2,1)S(1)}, bf16[32,4096]{1,0:T(8,128)(2,1)S(1)}, u32[]{:S(2)}, u32[]{:S(2)}) collective-permute-start(bf16[32,4096]{1,0:T(8,128)(2,1)S(1)} %add_convert_fusion.4), channel_id=1, source_target_pairs={{0,8},{1,9},{2,10},{3,11},{4,12},{5,13},{6,14},{7,15},{8,0},{9,1},... | collective-permute-start | bytes 786440 | tf_op jit(solution)/shard_map/ppermute | solution.py:475
  87.5 1.4 %collective-permute-done.26 = bf16[32,4096]{1,0:T(8,128)(2,1)S(1)} collective-permute-done((bf16[32,4096]{1,0:T(8,128)(2,1)S(1)}, bf16[32,4096]{1,0:T(8,128)(2,1)S(1)}, u32[]{:S(2)}, u32[]{:S(2)}) %collective-permute-start.26) | collective-permute-done | bytes 262176 | tf_op jit(solution)/shard_map/ppermute | solution.py:475
  89.1 1.6 %collective-permute-start.28 = (bf16[32,4096]{1,0:T(8,128)(2,1)S(1)}, bf16[32,4096]{1,0:T(8,128)(2,1)S(1)}, u32[]{:S(2)}, u32[]{:S(2)}) collective-permute-start(bf16[32,4096]{1,0:T(8,128)(2,1)S(1)} %add_convert_fusion.2), channel_id=1, source_target_pairs={{0,4},{1,5},{2,6},{3,7},{4,0},{5,1},{6,2},{7,3},{8,12},{9,13},{10,... | collective-permute-start | bytes 786440 | tf_op jit(solution)/shard_map/ppermute | solution.py:475
  91.2 0.8 copy.22
  92.0 5.5 %collective-permute-done.24 = bf16[32,4096]{1,0:T(8,128)(2,1)S(1)} collective-permute-done((bf16[32,4096]{1,0:T(8,128)(2,1)S(1)}, bf16[32,4096]{1,0:T(8,128)(2,1)S(1)}, u32[]{:S(2)}, u32[]{:S(2)}) %collective-permute-start.24) | collective-permute-done | bytes 262176 | tf_op jit(solution)/shard_map/ppermute | solution.py:475
  97.5 2.2 %collective-permute-done.28 = bf16[32,4096]{1,0:T(8,128)(2,1)S(1)} collective-permute-done((bf16[32,4096]{1,0:T(8,128)(2,1)S(1)}, bf16[32,4096]{1,0:T(8,128)(2,1)S(1)}, u32[]{:S(2)}, u32[]{:S(2)}) %collective-permute-start.28) | collective-permute-done | bytes 262176 | tf_op jit(solution)/shard_map/ppermute | solution.py:475
  99.7 0.9 add_convert_fusion
  (60 shorter events, 6.4 us)
Async XLA Ops:
  2.6 16.8 %collective-permute-start = (bf16[32,4224]{1,0:T(8,128)(2,1)}, bf16[32,4224]{1,0:T(8,128)(2,1)S(1)}, u32[]{:S(2)}, u32[]{:S(2)}) collective-permute-start(bf16[32,4224]{1,0:T(8,128)(2,1)} %shard_map.167.before.held.refs_0_), channel_id=1, source_target_pairs={{0,8},{1,9},{2,10},{3,11},{4,12},{5,13},{6,14},{7,15},{8,0},{9,1},... | collective-permute-start | bytes 811016 | tf_op jit(solution)/shard_map/ppermute | solution.py:475
  6.6 12.8 %collective-permute-start.1 = (bf16[32,4224]{1,0:T(8,128)(2,1)}, bf16[32,4224]{1,0:T(8,128)(2,1)S(1)}, u32[]{:S(2)}, u32[]{:S(2)}) collective-permute-start(bf16[32,4224]{1,0:T(8,128)(2,1)} %shard_map.167.before.held.refs_0_), channel_id=1, source_target_pairs={{0,4},{1,5},{2,6},{3,7},{4,0},{5,1},{6,2},{7,3},{8,12},{9,13},{10,... | collective-permute-start | bytes 811016 | tf_op jit(solution)/shard_map/ppermute | solution.py:475
  8.2 11.2 %collective-permute-start.2 = (bf16[32,4224]{1,0:T(8,128)(2,1)}, bf16[32,4224]{1,0:T(8,128)(2,1)S(1)}, u32[]{:S(2)}, u32[]{:S(2)}) collective-permute-start(bf16[32,4224]{1,0:T(8,128)(2,1)} %shard_map.167.before.held.refs_0_), channel_id=1, source_target_pairs={{0,2},{1,3},{2,0},{3,1},{4,6},{5,7},{6,4},{7,5},{8,10},{9,11},{10,... | collective-permute-start | bytes 811016 | tf_op jit(solution)/shard_map/ppermute | solution.py:475
  19.4 13.1 %collective-permute-start.3 = (bf16[32,4224]{1,0:T(8,128)(2,1)S(1)}, bf16[32,4224]{1,0:T(8,128)(2,1)S(1)}, u32[]{:S(2)}, u32[]{:S(2)}) collective-permute-start(bf16[32,4224]{1,0:T(8,128)(2,1)S(1)} %collective-permute-done.refs_8_), channel_id=1, source_target_pairs={{0,4},{1,5},{2,6},{3,7},{4,0},{5,1},{6,2},{7,3},{8,12},{9,13},{10,... | collective-permute-start | bytes 811016 | tf_op jit(solution)/shard_map/ppermute | solution.py:475
  20.9 11.7 %collective-permute-start.5 = (bf16[32,4224]{1,0:T(8,128)(2,1)S(1)}, bf16[32,4224]{1,0:T(8,128)(2,1)S(1)}, u32[]{:S(2)}, u32[]{:S(2)}) collective-permute-start(bf16[32,4224]{1,0:T(8,128)(2,1)S(1)} %collective-permute-done.refs_8_), channel_id=1, source_target_pairs={{0,2},{1,3},{2,0},{3,1},{4,6},{5,7},{6,4},{7,5},{8,10},{9,11},{10,... | collective-permute-start | bytes 811016 | tf_op jit(solution)/shard_map/ppermute | solution.py:475
  22.4 11.4 %collective-permute-start.4 = (bf16[32,4224]{1,0:T(8,128)(2,1)S(1)}, bf16[32,4224]{1,0:T(8,128)(2,1)S(1)}, u32[]{:S(2)}, u32[]{:S(2)}) collective-permute-start(bf16[32,4224]{1,0:T(8,128)(2,1)S(1)} %collective-permute-done.1.refs_4_), channel_id=1, source_target_pairs={{0,2},{1,3},{2,0},{3,1},{4,6},{5,7},{6,4},{7,5},{8,10},{9,11},{10,... | collective-permute-start | bytes 811016 | tf_op jit(solution)/shard_map/ppermute | solution.py:475
  22.9 13.6 %copy-start.1 = (bf16[32,2,256]{2,1,0:T(2,128)(2,1)S(1)}, bf16[32,2,256]{2,1,0:T(2,128)(2,1)}, u32[]{:S(2)}) copy-start(bf16[32,2,256]{2,1,0:T(2,128)(2,1)} %fresh.3) | copy-start | bytes 98308
  22.9 13.6 %copy-start.3 = (s32[32]{0:T(128)S(1)}, s32[32]{0:T(128)}, u32[]{:S(2)}) copy-start(s32[32]{0:T(128)} %lengths.3) | copy-start | bytes 388
  33.8 7.5 %collective-permute-start.6 = (bf16[32,4224]{1,0:T(8,128)(2,1)S(1)}, bf16[32,4224]{1,0:T(8,128)(2,1)}, u32[]{:S(2)}, u32[]{:S(2)}) collective-permute-start(bf16[32,4224]{1,0:T(8,128)(2,1)S(1)} %collective-permute-done.3.refs_12_), channel_id=1, source_target_pairs={{0,2},{1,3},{2,0},{3,1},{4,6},{5,7},{6,4},{7,5},{8,10},{9,11},{10,... | collective-permute-start | bytes 811016 | tf_op jit(solution)/shard_map/ppermute | solution.py:475
  35.4 6.0 %collective-permute-start.7 = (bf16[32,4224]{1,0:T(8,128)(2,1)S(1)}, bf16[32,4224]{1,0:T(8,128)(2,1)S(1)}, u32[]{:S(2)}, u32[]{:S(2)}) collective-permute-start(bf16[32,4224]{1,0:T(8,128)(2,1)S(1)} %copy-done), channel_id=1, source_target_pairs={{0,1},{1,0},{2,3},{3,2},{4,5},{5,4},{6,7},{7,6},{8,9},{9,8},{10,11... | collective-permute-start | bytes 811016 | tf_op jit(solution)/shard_map/ppermute | solution.py:475
  35.4 6.5 %collective-permute-start.11 = (bf16[32,4224]{1,0:T(8,128)(2,1)S(1)}, bf16[32,4224]{1,0:T(8,128)(2,1)S(1)}, u32[]{:S(2)}, u32[]{:S(2)}) collective-permute-start(bf16[32,4224]{1,0:T(8,128)(2,1)S(1)} %collective-permute-done.refs_8_), channel_id=1, source_target_pairs={{0,1},{1,0},{2,3},{3,2},{4,5},{5,4},{6,7},{7,6},{8,9},{9,8},{10,11... | collective-permute-start | bytes 811016 | tf_op jit(solution)/shard_map/ppermute | solution.py:475
  35.9 6.1 %collective-permute-start.9 = (bf16[32,4224]{1,0:T(8,128)(2,1)S(1)}, bf16[32,4224]{1,0:T(8,128)(2,1)S(1)}, u32[]{:S(2)}, u32[]{:S(2)}) collective-permute-start(bf16[32,4224]{1,0:T(8,128)(2,1)S(1)} %collective-permute-done.1.refs_4_), channel_id=1, source_target_pairs={{0,1},{1,0},{2,3},{3,2},{4,5},{5,4},{6,7},{7,6},{8,9},{9,8},{10,11... | collective-permute-start | bytes 811016 | tf_op jit(solution)/shard_map/ppermute | solution.py:475
  35.9 6.5 %collective-permute-start.8 = (bf16[32,4224]{1,0:T(8,128)(2,1)S(1)}, bf16[32,4224]{1,0:T(8,128)(2,1)S(1)}, u32[]{:S(2)}, u32[]{:S(2)}) collective-permute-start(bf16[32,4224]{1,0:T(8,128)(2,1)S(1)} %collective-permute-done.2.refs_2_), channel_id=1, source_target_pairs={{0,1},{1,0},{2,3},{3,2},{4,5},{5,4},{6,7},{7,6},{8,9},{9,8},{10,11... | collective-permute-start | bytes 811016 | tf_op jit(solution)/shard_map/ppermute | solution.py:475
  41.3 1.7 %collective-permute-start.13 = (bf16[32,4224]{1,0:T(8,128)(2,1)S(1)}, bf16[32,4224]{1,0:T(8,128)(2,1)}, u32[]{:S(2)}, u32[]{:S(2)}) collective-permute-start(bf16[32,4224]{1,0:T(8,128)(2,1)S(1)} %collective-permute-done.3.refs_12_), channel_id=1, source_target_pairs={{0,1},{1,0},{2,3},{3,2},{4,5},{5,4},{6,7},{7,6},{8,9},{9,8},{10,11... | collective-permute-start | bytes 811016 | tf_op jit(solution)/shard_map/ppermute | solution.py:475
  41.4 2.0 %collective-permute-start.10 = (bf16[32,4224]{1,0:T(8,128)(2,1)S(1)}, bf16[32,4224]{1,0:T(8,128)(2,1)}, u32[]{:S(2)}, u32[]{:S(2)}) collective-permute-start(bf16[32,4224]{1,0:T(8,128)(2,1)S(1)} %collective-permute-done.4.refs_6_), channel_id=1, source_target_pairs={{0,1},{1,0},{2,3},{3,2},{4,5},{5,4},{6,7},{7,6},{8,9},{9,8},{10,11... | collective-permute-start | bytes 811016 | tf_op jit(solution)/shard_map/ppermute | solution.py:475
  41.9 2.3 %collective-permute-start.12 = (bf16[32,4224]{1,0:T(8,128)(2,1)S(1)}, bf16[32,4224]{1,0:T(8,128)(2,1)}, u32[]{:S(2)}, u32[]{:S(2)}) collective-permute-start(bf16[32,4224]{1,0:T(8,128)(2,1)S(1)} %collective-permute-done.5.refs_10_), channel_id=1, source_target_pairs={{0,1},{1,0},{2,3},{3,2},{4,5},{5,4},{6,7},{7,6},{8,9},{9,8},{10,11... | collective-permute-start | bytes 811016 | tf_op jit(solution)/shard_map/ppermute | solution.py:475
  42.0 2.4 %collective-permute-start.14 = (bf16[32,4224]{1,0:T(8,128)(2,1)}, bf16[32,4224]{1,0:T(8,128)(2,1)}, u32[]{:S(2)}, u32[]{:S(2)}) collective-permute-start(bf16[32,4224]{1,0:T(8,128)(2,1)} %collective-permute-done.6.refs_14_), channel_id=1, source_target_pairs={{0,1},{1,0},{2,3},{3,2},{4,5},{5,4},{6,7},{7,6},{8,9},{9,8},{10,11... | collective-permute-start | bytes 811016 | tf_op jit(solution)/shard_map/ppermute | solution.py:475
  63.8 1.6 %collective-permute-start.15 = (bf16[32,4096]{1,0:T(8,128)(2,1)S(1)}, bf16[32,4096]{1,0:T(8,128)(2,1)S(1)}, u32[]{:S(2)}, u32[]{:S(2)}) collective-permute-start(bf16[32,4096]{1,0:T(8,128)(2,1)S(1)} %get-tuple-element.65), channel_id=1, source_target_pairs={{0,1},{1,0},{2,3},{3,2},{4,5},{5,4},{6,7},{7,6},{8,9},{9,8},{10,11... | collective-permute-start | bytes 786440 | tf_op jit(solution)/shard_map/ppermute | solution.py:475
  65.5 1.6 %collective-permute-start.17 = (bf16[32,4096]{1,0:T(8,128)(2,1)S(1)}, bf16[32,4096]{1,0:T(8,128)(2,1)S(1)}, u32[]{:S(2)}, u32[]{:S(2)}) collective-permute-start(bf16[32,4096]{1,0:T(8,128)(2,1)S(1)} %get-tuple-element.75), channel_id=1, source_target_pairs={{0,1},{1,0},{2,3},{3,2},{4,5},{5,4},{6,7},{7,6},{8,9},{9,8},{10,11... | collective-permute-start | bytes 786440 | tf_op jit(solution)/shard_map/ppermute | solution.py:475
  65.7 1.8 %collective-permute-start.18 = (bf16[32,4096]{1,0:T(8,128)(2,1)S(1)}, bf16[32,4096]{1,0:T(8,128)(2,1)S(1)}, u32[]{:S(2)}, u32[]{:S(2)}) collective-permute-start(bf16[32,4096]{1,0:T(8,128)(2,1)S(1)} %get-tuple-element.76), channel_id=1, source_target_pairs={{0,1},{1,0},{2,3},{3,2},{4,5},{5,4},{6,7},{7,6},{8,9},{9,8},{10,11... | collective-permute-start | bytes 786440 | tf_op jit(solution)/shard_map/ppermute | solution.py:475
  66.0 8.4 %collective-permute-start.16 = (bf16[32,4096]{1,0:T(8,128)(2,1)S(1)}, bf16[32,4096]{1,0:T(8,128)(2,1)S(1)}, u32[]{:S(2)}, u32[]{:S(2)}) collective-permute-start(bf16[32,4096]{1,0:T(8,128)(2,1)S(1)} %add_convert_fusion.7._), channel_id=1, source_target_pairs={{0,2},{1,3},{2,0},{3,1},{4,6},{5,7},{6,4},{7,5},{8,10},{9,11},{10,... | collective-permute-start | bytes 786440 | tf_op jit(solution)/shard_map/ppermute | solution.py:475
  66.6 16.5 %collective-permute-start.27 = (bf16[32,4096]{1,0:T(8,128)(2,1)S(1)}, bf16[32,4096]{1,0:T(8,128)(2,1)S(1)}, u32[]{:S(2)}, u32[]{:S(2)}) collective-permute-start(bf16[32,4096]{1,0:T(8,128)(2,1)S(1)} %get-tuple-element.95), channel_id=1, source_target_pairs={{0,1},{1,0},{2,3},{3,2},{4,5},{5,4},{6,7},{7,6},{8,9},{9,8},{10,11... | collective-permute-start | bytes 786440 | tf_op jit(solution)/shard_map/ppermute | solution.py:475
  66.6 8.4 %collective-permute-start.23 = (bf16[32,4096]{1,0:T(8,128)(2,1)S(1)}, bf16[32,4096]{1,0:T(8,128)(2,1)S(1)}, u32[]{:S(2)}, u32[]{:S(2)}) collective-permute-start(bf16[32,4096]{1,0:T(8,128)(2,1)S(1)} %get-tuple-element.89), channel_id=1, source_target_pairs={{0,1},{1,0},{2,3},{3,2},{4,5},{5,4},{6,7},{7,6},{8,9},{9,8},{10,11... | collective-permute-start | bytes 786440 | tf_op jit(solution)/shard_map/ppermute | solution.py:475
  67.1 8.6 %collective-permute-start.20 = (bf16[32,4096]{1,0:T(8,128)(2,1)S(1)}, bf16[32,4096]{1,0:T(8,128)(2,1)S(1)}, u32[]{:S(2)}, u32[]{:S(2)}) collective-permute-start(bf16[32,4096]{1,0:T(8,128)(2,1)S(1)} %get-tuple-element.80), channel_id=1, source_target_pairs={{0,1},{1,0},{2,3},{3,2},{4,5},{5,4},{6,7},{7,6},{8,9},{9,8},{10,11... | collective-permute-start | bytes 786440 | tf_op jit(solution)/shard_map/ppermute | solution.py:475
  67.4 20.1 %collective-permute-start.25 = (bf16[32,4096]{1,0:T(8,128)(2,1)S(1)}, bf16[32,4096]{1,0:T(8,128)(2,1)S(1)}, u32[]{:S(2)}, u32[]{:S(2)}) collective-permute-start(bf16[32,4096]{1,0:T(8,128)(2,1)S(1)} %get-tuple-element.92), channel_id=1, source_target_pairs={{0,1},{1,0},{2,3},{3,2},{4,5},{5,4},{6,7},{7,6},{8,9},{9,8},{10,11... | collective-permute-start | bytes 786440 | tf_op jit(solution)/shard_map/ppermute | solution.py:475
  74.6 7.6 %collective-permute-start.21 = (bf16[32,4096]{1,0:T(8,128)(2,1)S(1)}, bf16[32,4096]{1,0:T(8,128)(2,1)S(1)}, u32[]{:S(2)}, u32[]{:S(2)}) collective-permute-start(bf16[32,4096]{1,0:T(8,128)(2,1)S(1)} %get-tuple-element.86), channel_id=1, source_target_pairs={{0,4},{1,5},{2,6},{3,7},{4,0},{5,1},{6,2},{7,3},{8,12},{9,13},{10,... | collective-permute-start | bytes 786440 | tf_op jit(solution)/shard_map/ppermute | solution.py:475
  75.0 7.3 %collective-permute-start.22 = (bf16[32,4096]{1,0:T(8,128)(2,1)S(1)}, bf16[32,4096]{1,0:T(8,128)(2,1)S(1)}, u32[]{:S(2)}, u32[]{:S(2)}) collective-permute-start(bf16[32,4096]{1,0:T(8,128)(2,1)S(1)} %get-tuple-element.87), channel_id=1, source_target_pairs={{0,2},{1,3},{2,0},{3,1},{4,6},{5,7},{6,4},{7,5},{8,10},{9,11},{10,... | collective-permute-start | bytes 786440 | tf_op jit(solution)/shard_map/ppermute | solution.py:475
  75.7 16.3 %collective-permute-start.19 = (bf16[32,4096]{1,0:T(8,128)(2,1)S(1)}, bf16[32,4096]{1,0:T(8,128)(2,1)S(1)}, u32[]{:S(2)}, u32[]{:S(2)}) collective-permute-start(bf16[32,4096]{1,0:T(8,128)(2,1)S(1)} %get-tuple-element.79), channel_id=1, source_target_pairs={{0,1},{1,0},{2,3},{3,2},{4,5},{5,4},{6,7},{7,6},{8,9},{9,8},{10,11... | collective-permute-start | bytes 786440 | tf_op jit(solution)/shard_map/ppermute | solution.py:475
  82.4 6.6 %collective-permute-start.26 = (bf16[32,4096]{1,0:T(8,128)(2,1)S(1)}, bf16[32,4096]{1,0:T(8,128)(2,1)S(1)}, u32[]{:S(2)}, u32[]{:S(2)}) collective-permute-start(bf16[32,4096]{1,0:T(8,128)(2,1)S(1)} %add_convert_fusion.3), channel_id=1, source_target_pairs={{0,2},{1,3},{2,0},{3,1},{4,6},{5,7},{6,4},{7,5},{8,10},{9,11},{10,... | collective-permute-start | bytes 786440 | tf_op jit(solution)/shard_map/ppermute | solution.py:475
  83.2 14.4 %collective-permute-start.24 = (bf16[32,4096]{1,0:T(8,128)(2,1)S(1)}, bf16[32,4096]{1,0:T(8,128)(2,1)S(1)}, u32[]{:S(2)}, u32[]{:S(2)}) collective-permute-start(bf16[32,4096]{1,0:T(8,128)(2,1)S(1)} %add_convert_fusion.4), channel_id=1, source_target_pairs={{0,8},{1,9},{2,10},{3,11},{4,12},{5,13},{6,14},{7,15},{8,0},{9,1},... | collective-permute-start | bytes 786440 | tf_op jit(solution)/shard_map/ppermute | solution.py:475
  89.1 10.6 %collective-permute-start.28 = (bf16[32,4096]{1,0:T(8,128)(2,1)S(1)}, bf16[32,4096]{1,0:T(8,128)(2,1)S(1)}, u32[]{:S(2)}, u32[]{:S(2)}) collective-permute-start(bf16[32,4096]{1,0:T(8,128)(2,1)S(1)} %add_convert_fusion.2), channel_id=1, source_target_pairs={{0,4},{1,5},{2,6},{3,7},{4,0},{5,1},{6,2},{7,3},{8,12},{9,13},{10,... | collective-permute-start | bytes 786440 | tf_op jit(solution)/shard_map/ppermute | solution.py:475
  90.6 9.0 %collective-permute-start.29 = (bf16[32,4096]{1,0:T(8,128)(2,1)S(1)}, bf16[32,4096]{1,0:T(8,128)(2,1)S(1)}, u32[]{:S(2)}, u32[]{:S(2)}) collective-permute-start(bf16[32,4096]{1,0:T(8,128)(2,1)S(1)} %add_convert_fusion.1), channel_id=1, source_target_pairs={{0,2},{1,3},{2,0},{3,1},{4,6},{5,7},{6,4},{7,5},{8,10},{9,11},{10,... | collective-permute-start | bytes 786440 | tf_op jit(solution)/shard_map/ppermute | solution.py:475
  (6 other events, 39.7 us)

commit v4 on v3

--- a/solution.py
+++ b/solution.py
@@ -223,24 +223,25 @@
 
 
 class Leave:
-    def __init__(self, codes, scale, down_map, up_map, scratch):
-        self.words, self.scale, self.down, self.up, self.weights, self.sems = scratch
+    def __init__(self, first, codes, scale, down_map, up_map, scratch):
+        self.words, self.scale, self.down, self.up, self.sems = scratch
+        self.first = first
+        self.columns = self.words.shape[1]
         self.pairs = [
-            (codes.at[0], self.words),
+            (codes.at[0, :, pl.ds(first, self.columns)], self.words),
             (scale.at[0], self.scale),
             (down_map, self.down),
             (up_map.at[0], self.up),
         ]
 
     @staticmethod
-    def scratch(codes, scale, up_map):
-        _, third, width = codes.shape
+    def scratch(columns, codes, scale, up_map):
+        third = codes.shape[1]
         return [
-            pltpu.VMEM((third, width), jnp.int32),
+            pltpu.VMEM((third, columns), jnp.int32),
             pltpu.VMEM(scale.shape[1:], bf16),
             pltpu.VMEM((RANK, 3 * third), bf16),
             pltpu.VMEM(up_map.shape[1:], bf16),
-            pltpu.VMEM((3 * third, width), bf16),
             pltpu.SemaphoreType.DMA((4,)),
         ]
 
@@ -251,25 +252,63 @@
         for move in self.moves:
             move.wait()
 
-    def decode(self, tables, strip, strips):
+    def decode(self, tables, strip, strips, weights, at):
         rows = self.words.shape[0]
-        first = strip * LANES if isinstance(strip, int) else pl.multiple_of(strip * LANES, LANES)
+        strip = strip * LANES if isinstance(strip, int) else pl.multiple_of(strip * LANES, LANES)
         adapter = lax.dot_general(
             self.down[...],
-            self.up[:, pl.ds(first, strips * LANES)],
+            self.up[:, pl.ds(self.first + strip, strips * LANES)],
             (((0,), (0,)), ((), ())),
             preferred_element_type=f32,
         ) * adapter_scale
         for j in range(strips):
-            here = pl.ds(first + j * LANES, LANES)
+            here = pl.ds(strip + j * LANES, LANES)
+            there = pl.ds(self.first + strip + j * LANES, LANES)
+            target = pl.ds(at + strip + j * LANES, LANES)
             for nibble in range(3):
                 for g in range(rows // GROUP):
                     row = nibble * rows + g * GROUP
                     packed = self.words[pl.ds(g * GROUP, GROUP), here]
-                    factor = self.scale[pl.ds(row // GROUP, 1), here].astype(f32)
+                    factor = self.scale[pl.ds(row // GROUP, 1), there].astype(f32)
                     value = decode(tables, packed, nibble) * factor
                     value = value + adapter[row : row + GROUP, j * LANES : (j + 1) * LANES]
-                    self.weights[pl.ds(row, GROUP), here] = value.astype(bf16)
+                    weights[pl.ds(row, GROUP), target] = value.astype(bf16)
+
+
+def leave_kernel(codes, scale, down_map, up_map, before, out, made, weights, out_sem, *scratch):
+    leave = Leave(0, codes, scale, down_map, up_map, scratch)
+    leave.start()
+    made[...] = jnp.zeros_like(made)
+    tables = level_tables()
+    leave.ready()
+    blocks = leave.columns // BLOCK
+
+    def leaving(k):
+        here = pl.ds(pl.multiple_of(k * BLOCK, BLOCK), BLOCK)
+        return pltpu.make_async_copy(weights.at[:, here], out.at[:, here], out_sem.at[k])
+
+    @pl.loop(0, blocks)
+    def _(k):
+        leave.decode(tables, k * (BLOCK // LANES), BLOCK // LANES, weights, 0)
+        leaving(k).start()
+
+    @pl.loop(0, blocks)
+    def _(k):
+        leaving(k).wait()
+
+
+def leave_weights(columns, codes, scale, down_map, up_map, before):
+    rows = 3 * codes.shape[1]
+    return pl.pallas_call(
+        leave_kernel,
+        in_specs=in_hbm(4) + [pl.BlockSpec(memory_space=pl.ANY)],
+        out_specs=in_hbm(1) + [pl.BlockSpec(memory_space=pltpu.VMEM)],
+        out_shape=[jax.ShapeDtypeStruct((rows, columns), bf16), jax.ShapeDtypeStruct((8, LANES), f32)],
+        scratch_shapes=[pltpu.VMEM((rows, columns), bf16), pltpu.SemaphoreType.DMA((columns // BLOCK,))]
+        + Leave.scratch(columns, codes, scale, up_map),
+        compiler_params=params(54),
+        cost_estimate=pl.CostEstimate(flops=2 * 10**9, bytes_accessed=8 * 10**6, transcendentals=0),
+    )(codes, scale, down_map[0].T, up_map, before)
 
 
 def pick_rows(own, tables, rows, slots):
@@ -307,12 +346,16 @@
 
 def expert_kernel(count, own, *refs):
     blocks, refs = refs[:count], refs[count:]
-    enter, codes, scale, down_map, up_map, _ = refs[:6]
+    enter, made, codes, scale, down_map, up_map = refs[:6]
     outs, refs = refs[6 : count + 6], refs[count + 6 :]
-    picked, spread, weight, active, enter_of, enter_sem = refs[:6]
-    leave = Leave(codes, scale, down_map, up_map, refs[6:])
+    rows_of, picked, spread, weight, active, enter_of, leave_of, rows_sem, enter_sem, made_sem = refs[:10]
+    rows = blocks[0].shape[0]
+    arriving_rows = [
+        copy(blocks[r], rows_of.at[pl.ds(r * rows, rows)], rows_sem.at[r]) for r in range(count)
+    ]
+    begin = made.shape[1]
+    leave = Leave(begin, codes, scale, down_map, up_map, refs[10:])
     leave.start()
-    rows = blocks[0].shape[0]
     width = picked.shape[1]
     sets, span, slots = spread.shape
     tiles = enter_of.shape[0]
@@ -324,20 +367,24 @@
 
     for tile in range(FLYING):
         arriving(tile).start()
+    made_move = copy(made, leave_of.at[:, pl.ds(0, begin)], made_sem)
+    for move in arriving_rows:
+        move.wait()
     for g in range(sets):
-        members = blocks[g * each : (g + 1) * each]
-        tables = [member[:, width:].astype(f32) for member in members]
+        tables = [
+            rows_of[pl.ds(g * span + b * rows, rows), pl.ds(width, LANES)].astype(f32) for b in range(each)
+        ]
         gather, scatter, factor = pick_rows(own[0], tables, rows, slots)
         here = pl.ds(g * slots, slots)
         spread[g] = scatter
         weight[here, :] = factor
         for n in range(width // wide):
             lanes = pl.ds(n * wide, wide)
-            source = jnp.concatenate([member[:, lanes] for member in members], axis=0)
+            source = rows_of[pl.ds(g * span, span), lanes]
             picked[here, lanes] = jnp.dot(gather, source, preferred_element_type=f32).astype(bf16)
     levels = level_tables()
     leave.ready()
-    strips = width // LANES
+    strips = leave.columns // LANES
     per_tile = strips // tiles
 
     @pl.loop(0, tiles)
@@ -349,20 +396,21 @@
             arriving(tile + FLYING).start()
 
         joined = jnp.dot(picked[...], enter_of[tile], preferred_element_type=f32)
-        leave.decode(levels, tile * per_tile, per_tile)
+        leave.decode(levels, tile * per_tile, per_tile, leave_of, begin)
         gate = joined[:, :LANES]
         value = gate / (1.0 + jnp.exp(-gate)) * joined[:, LANES:]
         active[tile] = value.astype(bf16)
 
     if tiles * per_tile < strips:
-        leave.decode(levels, tiles * per_tile, strips - tiles * per_tile)
+        leave.decode(levels, tiles * per_tile, strips - tiles * per_tile, leave_of, begin)
+    made_move.wait()
 
     @pl.loop(0, width // wide)
     def _(n):
         lanes = pl.ds(pl.multiple_of(n * wide, wide), wide)
         entry = jnp.concatenate([active[t] for t in range(tiles)], axis=1)
         factor = jnp.concatenate([weight[...]] * (wide // slots), axis=1)
-        result = jnp.dot(entry, leave.weights[:, lanes], preferred_element_type=f32)
+        result = jnp.dot(entry, leave_of[:, lanes], preferred_element_type=f32)
         result = (result * factor).astype(bf16)
         for g in range(sets):
             own_rows = result[g * slots : (g + 1) * slots]
@@ -371,7 +419,7 @@
                 outs[g * each + b][:, lanes] = full[b * rows : (b + 1) * rows]
 
 
-def expert(own, blocks, enter, codes, scale, down_map, up_map, before):
+def expert(own, blocks, enter, made, codes, scale, down_map, up_map):
     count = len(blocks)
     tiles = enter.shape[0]
     rows, padded = blocks[0].shape
@@ -382,23 +430,25 @@
     return pl.pallas_call(
         functools.partial(expert_kernel, count),
         in_specs=[pl.BlockSpec(memory_space=pltpu.SMEM)]
-        + [vmem] * count
-        + in_hbm(5)
-        + [pl.BlockSpec(memory_space=pl.ANY)],
+        + in_hbm(count + 6),
         out_specs=[vmem] * count,
         out_shape=[jax.ShapeDtypeStruct((rows, width), bf16)] * count,
         scratch_shapes=[
+            pltpu.VMEM((count * rows, padded), bf16),
             pltpu.VMEM((sets * LANES, width), bf16),
             pltpu.VMEM((sets, each * rows, LANES), bf16),
             pltpu.VMEM((sets * LANES, LANES), f32),
             pltpu.VMEM((tiles, sets * LANES, LANES), bf16),
             pltpu.VMEM(enter.shape, bf16),
+            pltpu.VMEM((made.shape[0], width), bf16),
+            pltpu.SemaphoreType.DMA((count,)),
             pltpu.SemaphoreType.DMA((tiles,)),
+            pltpu.SemaphoreType.DMA,
         ]
-        + Leave.scratch(codes, scale, up_map),
-        compiler_params=params(46),
+        + Leave.scratch(width - made.shape[1], codes, scale, up_map),
+        compiler_params=params(48),
         cost_estimate=pl.CostEstimate(flops=8 * 10**9, bytes_accessed=22 * 10**6, transcendentals=0),
-    )(own, *blocks, enter, codes, scale, down_map[0].T, up_map, before)
+    )(own, *blocks, enter, made, codes, scale, down_map[0].T, up_map)
 
 
 def attend_kernel(
@@ -527,13 +577,17 @@
         if now < 2:
             weights, done = make_enter(now, done, weights if now else done)
         elif now == 2:
-            done = context = attention(done, 0)
-        *held, done = lax.optimization_barrier((*held, done))
+            others = [r | 1 for r in even if stage(r) == now]
+            done, *swapped = lax.optimization_barrier((done, *[blocks[r] for r in others]))
+            blocks.update(zip(others, swapped))
+            first_columns, done = leave_weights(hidden.shape[1] // 2, *leave_args, done)
         if now == 2:
-            context = done
+            *held, first_columns = lax.optimization_barrier((*held, first_columns))
+        else:
+            *held, done = lax.optimization_barrier((*held, done))
         blocks.update(zip(arriving, held))
     own = lax.axis_index("ep").astype(jnp.int32).reshape(1)
-    produced = expert(own, [blocks[r] for r in range(count)], weights, *leave_args, done)
+    produced = expert(own, [blocks[r] for r in range(count)], weights, first_columns, *leave_args)
 
     tie = lambda *values: list(lax.optimization_barrier(values))
     sums = {r: [produced[r]] for r in range(0, count, 2)}
@@ -547,14 +601,15 @@
     before, *held = tie(sent, *[sums[r][1] for r in early])
     for r, value in zip(early, held):
         sums[r][1] = value
-    later = attention(before, 1)
-    arrived, later = tie(arrived, later)
-    context = jnp.concatenate([context, later]).reshape(rows, HEADS * HEAD)
+    context = attention(before, 0)
+    arrived, context = tie(arrived, context)
     sums[first ^ bits[1]].append(arrived)
     for r in range(first - 2, 0, -4):
         pair = tie(*[add(sums.pop(q)).astype(bf16) for q in (r, r - 2)])
         for q, value in zip((r, r - 2), pair):
             sums[q ^ low_bit(q)].append(swap(value, low_bit(q)))
+    later = attention(pair[1], 1)
+    context = jnp.concatenate([context, later]).reshape(rows, HEADS * HEAD)
     return (context, add(sums[0]).astype(bf16))
 
 

time: 101 us -> 98 us (0.970)
  waiting for transfers between devices: 23.2 us -> 17.5 us
  Pallas kernels: 47 us -> 50.8 us
  local copies, waits for them, and re-layouts: 3.2 us -> 0.9 us
  starting transfers between devices: 24.8 us -> 26.2 us
    pallas_call x0 -> x1, Pallas kernels: none -> 7.27 us  [leave_weights(): pl.pallas_call(leave_kernel, in_specs=in_hbm(4) + [pl.BlockSpec(memory_sp...]
    ppermute x30, waiting for transfers between devices: 23.2 us -> 17.5 us  [swap(): return lax.ppermute(value, 'ep', [(i, i ^ bit) for i in range(count)])]
    pallas_call x1, Pallas kernels: 17.7 us -> 14.3 us  [expert(): pl.pallas_call(functools.partial(expert_kernel, count), in_specs=[pl.Bloc...]
    unnamed x18 -> x26, local copies, waits for them, and re-layouts: 3.2 us -> 0.9 us
    ppermute x30, starting transfers between devices: 24.8 us -> 26.2 us  [swap(): return lax.ppermute(value, 'ep', [(i, i ^ bit) for i in range(count)])]
  transfers between devices with their start and end apart: 30 -> 30, of which waited for: 13 -> 10; matrix products, arithmetic and copies ran while one was open for 1% -> 1% of each run, Pallas kernels for 27% -> 35%
where the time goes in v4:
time: 98 us; the launch traced here: 97.8 us
  Pallas kernels  50.8 us (52%)
  starting transfers between devices  26.2 us (27%)
  waiting for transfers between devices  17.5 us (18%)
  other arithmetic  1.47 us (2%)
    ppermute x30, starting transfers between devices, swap(): return lax.ppermute(value, 'ep', [(i, i ^ bit) for i in range(count)])  26.2 us
    pallas_call x2, Pallas kernels, enter_weights(): pl.pallas_call(functools.partial(enter_kernel, part, rows), in_specs=in_h...  19.2 us
    ppermute x30, waiting for transfers between devices, swap(): return lax.ppermute(value, 'ep', [(i, i ^ bit) for i in range(count)])  17.5 us
    pallas_call x1, Pallas kernels, expert(): pl.pallas_call(functools.partial(expert_kernel, count), in_specs=[pl.Bloc...  14.3 us
    pallas_call x2, Pallas kernels, attend(): pl.pallas_call(functools.partial(attend_kernel, first=part * rows, block=...  8.16 us
    pallas_call x1, Pallas kernels, leave_weights(): pl.pallas_call(leave_kernel, in_specs=in_hbm(4) + [pl.BlockSpec(memory_sp...  7.27 us
    pallas_call x1, Pallas kernels, norm_rows(): pl.pallas_call(norm_kernel, grid=(1,), in_specs=[whole((rows, width)), wh...  1.96 us
  transfers between devices with their start and end apart: 30, of which 10 were waited for; matrix products, arithmetic and copies ran while one was open for 1% of the time, Pallas kernels for 35%

profile of v4, /device:TPU:0, one launch (start us, length us, event | category | flops | bytes accessed | tf_op | source)
XLA Modules:
  0.0 97.8 jit_solution(8939418708378031797)
XLA Ops:
  0.6 2.0 %shard_map.167.before.held.refs_0_ = bf16[32,4224]{1,0:T(8,128)(2,1)} custom-call(bf16[32,4096]{1,0:T(8,128)(2,1)} %hidden.1, bf16[4096]{0:T(1024)(128)(2,1)} %gain.1, s32[8,32]{1,0:T(8,128)} %bitcast.24, f32[8,32]{1,0:T(8,128)} %bitcast.25), custom_call_target="tpu_custom_call" | custom-call | tf_op jit(solution)/shard_map/pallas_call | solution.py:81
  2.6 4.0 %collective-permute-start.1 = (bf16[32,4224]{1,0:T(8,128)(2,1)}, bf16[32,4224]{1,0:T(8,128)(2,1)S(1)}, u32[]{:S(2)}, u32[]{:S(2)}) collective-permute-start(bf16[32,4224]{1,0:T(8,128)(2,1)} %shard_map.167.before.held.refs_0_), channel_id=1, source_target_pairs={{0,8},{1,9},{2,10},{3,11},{4,12},{5,13},{6,14},{7,15},{8,0},{9,1},... | collective-permute-start | bytes 811016 | tf_op jit(solution)/shard_map/ppermute | solution.py:525
  6.6 1.6 %collective-permute-start.2 = (bf16[32,4224]{1,0:T(8,128)(2,1)}, bf16[32,4224]{1,0:T(8,128)(2,1)S(1)}, u32[]{:S(2)}, u32[]{:S(2)}) collective-permute-start(bf16[32,4224]{1,0:T(8,128)(2,1)} %shard_map.167.before.held.refs_0_), channel_id=1, source_target_pairs={{0,4},{1,5},{2,6},{3,7},{4,0},{5,1},{6,2},{7,3},{8,12},{9,13},{10,... | collective-permute-start | bytes 811016 | tf_op jit(solution)/shard_map/ppermute | solution.py:525
  8.2 1.5 %collective-permute-start.3 = (bf16[32,4224]{1,0:T(8,128)(2,1)}, bf16[32,4224]{1,0:T(8,128)(2,1)S(1)}, u32[]{:S(2)}, u32[]{:S(2)}) collective-permute-start(bf16[32,4224]{1,0:T(8,128)(2,1)} %shard_map.167.before.held.refs_0_), channel_id=1, source_target_pairs={{0,2},{1,3},{2,0},{3,1},{4,6},{5,7},{6,4},{7,5},{8,10},{9,11},{10,... | collective-permute-start | bytes 811016 | tf_op jit(solution)/shard_map/ppermute | solution.py:525
  9.7 9.6 %shard_map.168 = (bf16[6,4096,256]{2,1,0:T(8,128)(2,1)}, f32[8,128]{1,0:T(8,128)}) custom-call(s32[1,4096,512]{2,1,0:T(8,128)} %codes.4, bf16[1,64,1536]{2,1,0:T(8,128)(2,1)} %scale.4, bf16[32,4096]{1,0:T(8,128)(2,1)} %bitcast.20, bf16[1,2,16,768]{3,2,1,0:T(8,128)(2,1)} %up_map.4, bf16[32,4224]{1,0:T(8,128)(2,1)} %shard_map.167.before.held.refs_0_, ...), custom_call_target="tpu_custom_call" | custom-call | flops 4000000000 | bytes 20000000 | tf_op jit(solution)/shard_map/pallas_call | solution.py:199
  19.4 1.5 %collective-permute-start.6 = (bf16[32,4224]{1,0:T(8,128)(2,1)S(1)}, bf16[32,4224]{1,0:T(8,128)(2,1)S(1)}, u32[]{:S(2)}, u32[]{:S(2)}) collective-permute-start(bf16[32,4224]{1,0:T(8,128)(2,1)S(1)} %collective-permute-done.1.refs_8_), channel_id=1, source_target_pairs={{0,4},{1,5},{2,6},{3,7},{4,0},{5,1},{6,2},{7,3},{8,12},{9,13},{10,... | collective-permute-start | bytes 811016 | tf_op jit(solution)/shard_map/ppermute | solution.py:525
  20.9 1.5 %collective-permute-start.8 = (bf16[32,4224]{1,0:T(8,128)(2,1)S(1)}, bf16[32,4224]{1,0:T(8,128)(2,1)S(1)}, u32[]{:S(2)}, u32[]{:S(2)}) collective-permute-start(bf16[32,4224]{1,0:T(8,128)(2,1)S(1)} %collective-permute-done.1.refs_8_), channel_id=1, source_target_pairs={{0,2},{1,3},{2,0},{3,1},{4,6},{5,7},{6,4},{7,5},{8,10},{9,11},{10,... | collective-permute-start | bytes 811016 | tf_op jit(solution)/shard_map/ppermute | solution.py:525
  22.4 0.5 collective-permute-start.7
  22.9 9.6 %shard_map.169 = (bf16[6,4096,256]{2,1,0:T(8,128)(2,1)}, f32[8,128]{1,0:T(8,128)}) custom-call(s32[1,4096,512]{2,1,0:T(8,128)} %codes.4, bf16[1,64,1536]{2,1,0:T(8,128)(2,1)} %scale.4, bf16[32,4096]{1,0:T(8,128)(2,1)} %bitcast.21, bf16[1,2,16,768]{3,2,1,0:T(8,128)(2,1)} %up_map.4, ...), custom_call_target="tpu_custom_call", output_to_operand_aliasing={{0}: (5, {})} | custom-call | flops 4000000000 | bytes 20000000 | tf_op jit(solution)/shard_map/pallas_call | solution.py:199
  32.6 1.3 %collective-permute-done.7.refs_6_ = bf16[32,4224]{1,0:T(8,128)(2,1)S(1)} collective-permute-done((bf16[32,4224]{1,0:T(8,128)(2,1)S(1)}, bf16[32,4224]{1,0:T(8,128)(2,1)S(1)}, u32[]{:S(2)}, u32[]{:S(2)}) %collective-permute-start.7) | collective-permute-done | bytes 270368 | tf_op jit(solution)/shard_map/ppermute | solution.py:525
  33.9 0.5 collective-permute-start.10
  34.4 1.5 %collective-permute-start.13 = (bf16[32,4224]{1,0:T(8,128)(2,1)S(1)}, bf16[32,4224]{1,0:T(8,128)(2,1)}, u32[]{:S(2)}, u32[]{:S(2)}) collective-permute-start(bf16[32,4224]{1,0:T(8,128)(2,1)S(1)} %collective-permute-done.6.refs_12_), channel_id=1, source_target_pairs={{0,2},{1,3},{2,0},{3,1},{4,6},{5,7},{6,4},{7,5},{8,10},{9,11},{10,... | collective-permute-start | bytes 811016 | tf_op jit(solution)/shard_map/ppermute | solution.py:525
  37.1 7.3 %shard_map.170 = (bf16[768,2048]{1,0:T(8,128)(2,1)}, f32[8,128]{1,0:T(8,128)}) custom-call(s32[1,256,4096]{2,1,0:T(8,128)} %refs_18_.1, bf16[1,12,4096]{2,1,0:T(8,128)(2,1)} %refs_19_.1, bf16[16,768]{1,0:T(8,128)(2,1)} %bitcast.17, bf16[1,16,4096]{2,1,0:T(8,128)(2,1)} %refs_21_.1, f32[8,128]{1,0:T(8,128)} %get-tuple-element.70.before), custom_call_target="tpu_custom_call" | custom-call | flops 2000000000 | bytes 8000000 | tf_op jit(solution)/shard_map/pallas_call | solution.py:302
  44.7 1.6 %collective-permute-done.14.refs_15_ = bf16[32,4224]{1,0:T(8,128)(2,1)} collective-permute-done((bf16[32,4224]{1,0:T(8,128)(2,1)}, bf16[32,4224]{1,0:T(8,128)(2,1)}, u32[]{:S(2)}, u32[]{:S(2)}) %collective-permute-start.14) | collective-permute-done | bytes 270368 | tf_op jit(solution)/shard_map/ppermute | solution.py:525
  46.4 14.3 %shard_map.171 = (bf16[32,4096]{1,0:T(8,128)(2,1)S(1)}, bf16[32,4096]{1,0:T(8,128)(2,1)S(1)}, bf16[32,4096]{1,0:T(8,128)(2,1)S(1)}, bf16[32,4096]{1,0:T(8,128)(2...) custom-call(s32[1]{0:T(128)} %bitcast.own, ...), custom_call_target="tpu_custom_call" | custom-call | flops 8000000000 | bytes 22000000 | tf_op jit(solution)/shard_map/pallas_call | solution.py:430
  60.9 1.3 %collective-permute-done.15 = bf16[32,4096]{1,0:T(8,128)(2,1)S(1)} collective-permute-done((bf16[32,4096]{1,0:T(8,128)(2,1)S(1)}, bf16[32,4096]{1,0:T(8,128)(2,1)S(1)}, u32[]{:S(2)}, u32[]{:S(2)}) %collective-permute-start.15) | collective-permute-done | bytes 262176 | tf_op jit(solution)/shard_map/ppermute | solution.py:525
  62.9 1.0 collective-permute-start.16
  64.1 0.4 collective-permute-start.23
  65.0 4.1 %shard_map.172 = bf16[16,32,128]{2,1,0:T(8,128)(2,1)S(1)} custom-call(s32[32]{0:T(128)S(1)} %copy-done.2, bf16[32,32,128]{2,1,0:T(8,128)(2,1)S(1)} %bitcast.15, bf16[32,2,256]{2,1,0:T(2,128)(2,1)S(1)} %copy-done.1, bf16[32,2,256,256]{3,2,1,0:T(8,128)(2,1)} %cache.3, bf16[32,4096]{1,0:T(8,128)(2,1)S(1)} %add_convert_fusion.7._), custom_call_target="tpu_custom_call" | custom-call | flops 500000000 | bytes 20000000 | tf_op jit(solution)/shard_map/pallas_call | solution.py:506
  69.1 2.2 %collective-permute-done.16 = bf16[32,4096]{1,0:T(8,128)(2,1)S(1)} collective-permute-done((bf16[32,4096]{1,0:T(8,128)(2,1)S(1)}, bf16[32,4096]{1,0:T(8,128)(2,1)S(1)}, u32[]{:S(2)}, u32[]{:S(2)}) %collective-permute-start.16) | collective-permute-done | bytes 262176 | tf_op jit(solution)/shard_map/ppermute | solution.py:525
  71.9 1.1 %collective-permute-start.22 = (bf16[32,4096]{1,0:T(8,128)(2,1)S(1)}, bf16[32,4096]{1,0:T(8,128)(2,1)S(1)}, u32[]{:S(2)}, u32[]{:S(2)}) collective-permute-start(bf16[32,4096]{1,0:T(8,128)(2,1)S(1)} %get-tuple-element.97), channel_id=1, source_target_pairs={{0,2},{1,3},{2,0},{3,1},{4,6},{5,7},{6,4},{7,5},{8,10},{9,11},{10,... | collective-permute-start | bytes 786440 | tf_op jit(solution)/shard_map/ppermute | solution.py:525
  73.2 6.0 %collective-permute-done.21 = bf16[32,4096]{1,0:T(8,128)(2,1)S(1)} collective-permute-done((bf16[32,4096]{1,0:T(8,128)(2,1)S(1)}, bf16[32,4096]{1,0:T(8,128)(2,1)S(1)}, u32[]{:S(2)}, u32[]{:S(2)}) %collective-permute-start.21) | collective-permute-done | bytes 262176 | tf_op jit(solution)/shard_map/ppermute | solution.py:525
  79.4 1.3 %collective-permute-start.24 = (bf16[32,4096]{1,0:T(8,128)(2,1)S(1)}, bf16[32,4096]{1,0:T(8,128)(2,1)S(1)}, u32[]{:S(2)}, u32[]{:S(2)}) collective-permute-start(bf16[32,4096]{1,0:T(8,128)(2,1)S(1)} %add_convert_fusion.3), channel_id=1, source_target_pairs={{0,2},{1,3},{2,0},{3,1},{4,6},{5,7},{6,4},{7,5},{8,10},{9,11},{10,... | collective-permute-start | bytes 786440 | tf_op jit(solution)/shard_map/ppermute | solution.py:525
  80.8 3.4 %collective-permute-start.27 = (bf16[32,4096]{1,0:T(8,128)(2,1)S(1)}, bf16[32,4096]{1,0:T(8,128)(2,1)S(1)}, u32[]{:S(2)}, u32[]{:S(2)}) collective-permute-start(bf16[32,4096]{1,0:T(8,128)(2,1)S(1)} %add_convert_fusion.4), channel_id=1, source_target_pairs={{0,8},{1,9},{2,10},{3,11},{4,12},{5,13},{6,14},{7,15},{8,0},{9,1},... | collective-permute-start | bytes 786440 | tf_op jit(solution)/shard_map/ppermute | solution.py:525
  84.2 1.9 %collective-permute-done.24 = bf16[32,4096]{1,0:T(8,128)(2,1)S(1)} collective-permute-done((bf16[32,4096]{1,0:T(8,128)(2,1)S(1)}, bf16[32,4096]{1,0:T(8,128)(2,1)S(1)}, u32[]{:S(2)}, u32[]{:S(2)}) %collective-permute-start.24) | collective-permute-done | bytes 262176 | tf_op jit(solution)/shard_map/ppermute | solution.py:525
  86.2 1.5 %collective-permute-start.28 = (bf16[32,4096]{1,0:T(8,128)(2,1)S(1)}, bf16[32,4096]{1,0:T(8,128)(2,1)S(1)}, u32[]{:S(2)}, u32[]{:S(2)}) collective-permute-start(bf16[32,4096]{1,0:T(8,128)(2,1)S(1)} %add_convert_fusion.2), channel_id=1, source_target_pairs={{0,4},{1,5},{2,6},{3,7},{4,0},{5,1},{6,2},{7,3},{8,12},{9,13},{10,... | collective-permute-start | bytes 786440 | tf_op jit(solution)/shard_map/ppermute | solution.py:525
  87.7 1.4 %collective-permute-start.29 = (bf16[32,4096]{1,0:T(8,128)(2,1)S(1)}, bf16[32,4096]{1,0:T(8,128)(2,1)S(1)}, u32[]{:S(2)}, u32[]{:S(2)}) collective-permute-start(bf16[32,4096]{1,0:T(8,128)(2,1)S(1)} %add_convert_fusion.1._), channel_id=1, source_target_pairs={{0,2},{1,3},{2,0},{3,1},{4,6},{5,7},{6,4},{7,5},{8,10},{9,11},{10,... | collective-permute-start | bytes 786440 | tf_op jit(solution)/shard_map/ppermute | solution.py:525
  89.1 4.1 %shard_map.173 = bf16[16,32,128]{2,1,0:T(8,128)(2,1)S(1)} custom-call(s32[32]{0:T(128)S(1)} %copy-done.2, bf16[32,32,128]{2,1,0:T(8,128)(2,1)S(1)} %bitcast.16, bf16[32,2,256]{2,1,0:T(2,128)(2,1)S(1)} %copy-done.1, bf16[32,2,256,256]{3,2,1,0:T(8,128)(2,1)} %cache.3, bf16[32,4096]{1,0:T(8,128)(2,1)S(1)} %add_convert_fusion.1._), custom_call_target="tpu_custom_call" | custom-call | flops 500000000 | bytes 20000000 | tf_op jit(solution)/shard_map/pallas_call | solution.py:506
  93.2 0.8 copy.22
  94.0 0.6 collective-permute-done.27
  94.6 2.3 %collective-permute-done.28 = bf16[32,4096]{1,0:T(8,128)(2,1)S(1)} collective-permute-done((bf16[32,4096]{1,0:T(8,128)(2,1)S(1)}, bf16[32,4096]{1,0:T(8,128)(2,1)S(1)}, u32[]{:S(2)}, u32[]{:S(2)}) %collective-permute-start.28) | collective-permute-done | bytes 262176 | tf_op jit(solution)/shard_map/ppermute | solution.py:525
  96.9 0.9 add_convert_fusion
  (69 shorter events, 4.3 us)
Async XLA Ops:
  2.6 16.7 %collective-permute-start.1 = (bf16[32,4224]{1,0:T(8,128)(2,1)}, bf16[32,4224]{1,0:T(8,128)(2,1)S(1)}, u32[]{:S(2)}, u32[]{:S(2)}) collective-permute-start(bf16[32,4224]{1,0:T(8,128)(2,1)} %shard_map.167.before.held.refs_0_), channel_id=1, source_target_pairs={{0,8},{1,9},{2,10},{3,11},{4,12},{5,13},{6,14},{7,15},{8,0},{9,1},... | collective-permute-start | bytes 811016 | tf_op jit(solution)/shard_map/ppermute | solution.py:525
  6.6 12.8 %collective-permute-start.2 = (bf16[32,4224]{1,0:T(8,128)(2,1)}, bf16[32,4224]{1,0:T(8,128)(2,1)S(1)}, u32[]{:S(2)}, u32[]{:S(2)}) collective-permute-start(bf16[32,4224]{1,0:T(8,128)(2,1)} %shard_map.167.before.held.refs_0_), channel_id=1, source_target_pairs={{0,4},{1,5},{2,6},{3,7},{4,0},{5,1},{6,2},{7,3},{8,12},{9,13},{10,... | collective-permute-start | bytes 811016 | tf_op jit(solution)/shard_map/ppermute | solution.py:525
  8.2 11.2 %collective-permute-start.3 = (bf16[32,4224]{1,0:T(8,128)(2,1)}, bf16[32,4224]{1,0:T(8,128)(2,1)S(1)}, u32[]{:S(2)}, u32[]{:S(2)}) collective-permute-start(bf16[32,4224]{1,0:T(8,128)(2,1)} %shard_map.167.before.held.refs_0_), channel_id=1, source_target_pairs={{0,2},{1,3},{2,0},{3,1},{4,6},{5,7},{6,4},{7,5},{8,10},{9,11},{10,... | collective-permute-start | bytes 811016 | tf_op jit(solution)/shard_map/ppermute | solution.py:525
  19.4 13.1 %collective-permute-start.6 = (bf16[32,4224]{1,0:T(8,128)(2,1)S(1)}, bf16[32,4224]{1,0:T(8,128)(2,1)S(1)}, u32[]{:S(2)}, u32[]{:S(2)}) collective-permute-start(bf16[32,4224]{1,0:T(8,128)(2,1)S(1)} %collective-permute-done.1.refs_8_), channel_id=1, source_target_pairs={{0,4},{1,5},{2,6},{3,7},{4,0},{5,1},{6,2},{7,3},{8,12},{9,13},{10,... | collective-permute-start | bytes 811016 | tf_op jit(solution)/shard_map/ppermute | solution.py:525
  20.9 11.7 %collective-permute-start.8 = (bf16[32,4224]{1,0:T(8,128)(2,1)S(1)}, bf16[32,4224]{1,0:T(8,128)(2,1)S(1)}, u32[]{:S(2)}, u32[]{:S(2)}) collective-permute-start(bf16[32,4224]{1,0:T(8,128)(2,1)S(1)} %collective-permute-done.1.refs_8_), channel_id=1, source_target_pairs={{0,2},{1,3},{2,0},{3,1},{4,6},{5,7},{6,4},{7,5},{8,10},{9,11},{10,... | collective-permute-start | bytes 811016 | tf_op jit(solution)/shard_map/ppermute | solution.py:525
  22.4 11.5 %collective-permute-start.7 = (bf16[32,4224]{1,0:T(8,128)(2,1)S(1)}, bf16[32,4224]{1,0:T(8,128)(2,1)S(1)}, u32[]{:S(2)}, u32[]{:S(2)}) collective-permute-start(bf16[32,4224]{1,0:T(8,128)(2,1)S(1)} %collective-permute-done.2.refs_4_), channel_id=1, source_target_pairs={{0,2},{1,3},{2,0},{3,1},{4,6},{5,7},{6,4},{7,5},{8,10},{9,11},{10,... | collective-permute-start | bytes 811016 | tf_op jit(solution)/shard_map/ppermute | solution.py:525
  22.9 23.4 %copy-start.4 = (bf16[1,16,4096]{2,1,0:T(8,128)(2,1)S(1)}, bf16[1,16,4096]{2,1,0:T(8,128)(2,1)}, u32[]{:S(2)}) copy-start(bf16[1,16,4096]{2,1,0:T(8,128)(2,1)} %refs_21_.1) | copy-start | bytes 393220
  22.9 23.4 %copy-start.5 = (bf16[1,768,16]{1,2,0:T(8,128)(2,1)S(1)}, bf16[1,768,16]{1,2,0:T(8,128)(2,1)}, u32[]{:S(2)}) copy-start(bf16[1,768,16]{1,2,0:T(8,128)(2,1)} %param.30) | copy-start | bytes 73732
  33.9 2.3 %collective-permute-start.11 = (bf16[32,4224]{1,0:T(8,128)(2,1)S(1)}, bf16[32,4224]{1,0:T(8,128)(2,1)S(1)}, u32[]{:S(2)}, u32[]{:S(2)}) collective-permute-start(bf16[32,4224]{1,0:T(8,128)(2,1)S(1)} %collective-permute-done.6.refs_12_), channel_id=1, source_target_pairs={{0,1},{1,0},{2,3},{3,2},{4,5},{5,4},{6,7},{7,6},{8,9},{9,8},{10,11... | collective-permute-start | bytes 811016 | tf_op jit(solution)/shard_map/ppermute | solution.py:525
  33.9 2.6 %collective-permute-start.10 = (bf16[32,4224]{1,0:T(8,128)(2,1)S(1)}, bf16[32,4224]{1,0:T(8,128)(2,1)}, u32[]{:S(2)}, u32[]{:S(2)}) collective-permute-start(bf16[32,4224]{1,0:T(8,128)(2,1)S(1)} %collective-permute-done.8.refs_10_), channel_id=1, source_target_pairs={{0,1},{1,0},{2,3},{3,2},{4,5},{5,4},{6,7},{7,6},{8,9},{9,8},{10,11... | collective-permute-start | bytes 811016 | tf_op jit(solution)/shard_map/ppermute | solution.py:525
  34.4 2.3 %collective-permute-start.9 = (bf16[32,4224]{1,0:T(8,128)(2,1)S(1)}, bf16[32,4224]{1,0:T(8,128)(2,1)}, u32[]{:S(2)}, u32[]{:S(2)}) collective-permute-start(bf16[32,4224]{1,0:T(8,128)(2,1)S(1)} %collective-permute-done.7.refs_6_), channel_id=1, source_target_pairs={{0,1},{1,0},{2,3},{3,2},{4,5},{5,4},{6,7},{7,6},{8,9},{9,8},{10,11... | collective-permute-start | bytes 811016 | tf_op jit(solution)/shard_map/ppermute | solution.py:525
  34.4 9.9 %collective-permute-start.13 = (bf16[32,4224]{1,0:T(8,128)(2,1)S(1)}, bf16[32,4224]{1,0:T(8,128)(2,1)}, u32[]{:S(2)}, u32[]{:S(2)}) collective-permute-start(bf16[32,4224]{1,0:T(8,128)(2,1)S(1)} %collective-permute-done.6.refs_12_), channel_id=1, source_target_pairs={{0,2},{1,3},{2,0},{3,1},{4,6},{5,7},{6,4},{7,5},{8,10},{9,11},{10,... | collective-permute-start | bytes 811016 | tf_op jit(solution)/shard_map/ppermute | solution.py:525
  36.0 8.7 %collective-permute-start = (bf16[32,4224]{1,0:T(8,128)(2,1)S(1)}, bf16[32,4224]{1,0:T(8,128)(2,1)S(1)}, u32[]{:S(2)}, u32[]{:S(2)}) collective-permute-start(bf16[32,4224]{1,0:T(8,128)(2,1)S(1)} %copy-done), channel_id=1, source_target_pairs={{0,1},{1,0},{2,3},{3,2},{4,5},{5,4},{6,7},{7,6},{8,9},{9,8},{10,11... | collective-permute-start | bytes 811016 | tf_op jit(solution)/shard_map/ppermute | solution.py:525
  36.2 8.4 %collective-permute-start.12 = (bf16[32,4224]{1,0:T(8,128)(2,1)S(1)}, bf16[32,4224]{1,0:T(8,128)(2,1)}, u32[]{:S(2)}, u32[]{:S(2)}) collective-permute-start(bf16[32,4224]{1,0:T(8,128)(2,1)S(1)} %collective-permute-done.1.refs_8_), channel_id=1, source_target_pairs={{0,1},{1,0},{2,3},{3,2},{4,5},{5,4},{6,7},{7,6},{8,9},{9,8},{10,11... | collective-permute-start | bytes 811016 | tf_op jit(solution)/shard_map/ppermute | solution.py:525
  36.6 8.1 %collective-permute-start.5 = (bf16[32,4224]{1,0:T(8,128)(2,1)S(1)}, bf16[32,4224]{1,0:T(8,128)(2,1)S(1)}, u32[]{:S(2)}, u32[]{:S(2)}) collective-permute-start(bf16[32,4224]{1,0:T(8,128)(2,1)S(1)} %collective-permute-done.2.refs_4_), channel_id=1, source_target_pairs={{0,1},{1,0},{2,3},{3,2},{4,5},{5,4},{6,7},{7,6},{8,9},{9,8},{10,11... | collective-permute-start | bytes 811016 | tf_op jit(solution)/shard_map/ppermute | solution.py:525
  36.8 7.9 %collective-permute-start.4 = (bf16[32,4224]{1,0:T(8,128)(2,1)S(1)}, bf16[32,4224]{1,0:T(8,128)(2,1)S(1)}, u32[]{:S(2)}, u32[]{:S(2)}) collective-permute-start(bf16[32,4224]{1,0:T(8,128)(2,1)S(1)} %collective-permute-done.3.refs_2_), channel_id=1, source_target_pairs={{0,1},{1,0},{2,3},{3,2},{4,5},{5,4},{6,7},{7,6},{8,9},{9,8},{10,11... | collective-permute-start | bytes 811016 | tf_op jit(solution)/shard_map/ppermute | solution.py:525
  44.4 2.0 %collective-permute-start.14 = (bf16[32,4224]{1,0:T(8,128)(2,1)}, bf16[32,4224]{1,0:T(8,128)(2,1)}, u32[]{:S(2)}, u32[]{:S(2)}) collective-permute-start(bf16[32,4224]{1,0:T(8,128)(2,1)} %collective-permute-done.13.refs_14_), channel_id=1, source_target_pairs={{0,1},{1,0},{2,3},{3,2},{4,5},{5,4},{6,7},{7,6},{8,9},{9,8},{10,11... | collective-permute-start | bytes 811016 | tf_op jit(solution)/shard_map/ppermute | solution.py:525
  60.7 1.6 %collective-permute-start.15 = (bf16[32,4096]{1,0:T(8,128)(2,1)S(1)}, bf16[32,4096]{1,0:T(8,128)(2,1)S(1)}, u32[]{:S(2)}, u32[]{:S(2)}) collective-permute-start(bf16[32,4096]{1,0:T(8,128)(2,1)S(1)} %get-tuple-element.75), channel_id=1, source_target_pairs={{0,1},{1,0},{2,3},{3,2},{4,5},{5,4},{6,7},{7,6},{8,9},{9,8},{10,11... | collective-permute-start | bytes 786440 | tf_op jit(solution)/shard_map/ppermute | solution.py:525
  62.3 2.2 %collective-permute-start.17 = (bf16[32,4096]{1,0:T(8,128)(2,1)S(1)}, bf16[32,4096]{1,0:T(8,128)(2,1)S(1)}, u32[]{:S(2)}, u32[]{:S(2)}) collective-permute-start(bf16[32,4096]{1,0:T(8,128)(2,1)S(1)} %get-tuple-element.85), channel_id=1, source_target_pairs={{0,1},{1,0},{2,3},{3,2},{4,5},{5,4},{6,7},{7,6},{8,9},{9,8},{10,11... | collective-permute-start | bytes 786440 | tf_op jit(solution)/shard_map/ppermute | solution.py:525
  62.6 2.0 %collective-permute-start.18 = (bf16[32,4096]{1,0:T(8,128)(2,1)S(1)}, bf16[32,4096]{1,0:T(8,128)(2,1)S(1)}, u32[]{:S(2)}, u32[]{:S(2)}) collective-permute-start(bf16[32,4096]{1,0:T(8,128)(2,1)S(1)} %get-tuple-element.86), channel_id=1, source_target_pairs={{0,1},{1,0},{2,3},{3,2},{4,5},{5,4},{6,7},{7,6},{8,9},{9,8},{10,11... | collective-permute-start | bytes 786440 | tf_op jit(solution)/shard_map/ppermute | solution.py:525
  62.9 8.4 %collective-permute-start.16 = (bf16[32,4096]{1,0:T(8,128)(2,1)S(1)}, bf16[32,4096]{1,0:T(8,128)(2,1)S(1)}, u32[]{:S(2)}, u32[]{:S(2)}) collective-permute-start(bf16[32,4096]{1,0:T(8,128)(2,1)S(1)} %add_convert_fusion.7._), channel_id=1, source_target_pairs={{0,2},{1,3},{2,0},{3,1},{4,6},{5,7},{6,4},{7,5},{8,10},{9,11},{10,... | collective-permute-start | bytes 786440 | tf_op jit(solution)/shard_map/ppermute | solution.py:525
  63.9 16.8 %collective-permute-start.25 = (bf16[32,4096]{1,0:T(8,128)(2,1)S(1)}, bf16[32,4096]{1,0:T(8,128)(2,1)S(1)}, u32[]{:S(2)}, u32[]{:S(2)}) collective-permute-start(bf16[32,4096]{1,0:T(8,128)(2,1)S(1)} %get-tuple-element.103), channel_id=1, source_target_pairs={{0,1},{1,0},{2,3},{3,2},{4,5},{5,4},{6,7},{7,6},{8,9},{9,8},{10,11... | collective-permute-start | bytes 786440 | tf_op jit(solution)/shard_map/ppermute | solution.py:525
  64.1 7.9 %collective-permute-start.23 = (bf16[32,4096]{1,0:T(8,128)(2,1)S(1)}, bf16[32,4096]{1,0:T(8,128)(2,1)S(1)}, u32[]{:S(2)}, u32[]{:S(2)}) collective-permute-start(bf16[32,4096]{1,0:T(8,128)(2,1)S(1)} %get-tuple-element.99), channel_id=1, source_target_pairs={{0,1},{1,0},{2,3},{3,2},{4,5},{5,4},{6,7},{7,6},{8,9},{9,8},{10,11... | collective-permute-start | bytes 786440 | tf_op jit(solution)/shard_map/ppermute | solution.py:525
  64.5 8.6 %collective-permute-start.20 = (bf16[32,4096]{1,0:T(8,128)(2,1)S(1)}, bf16[32,4096]{1,0:T(8,128)(2,1)S(1)}, u32[]{:S(2)}, u32[]{:S(2)}) collective-permute-start(bf16[32,4096]{1,0:T(8,128)(2,1)S(1)} %get-tuple-element.90), channel_id=1, source_target_pairs={{0,1},{1,0},{2,3},{3,2},{4,5},{5,4},{6,7},{7,6},{8,9},{9,8},{10,11... | collective-permute-start | bytes 786440 | tf_op jit(solution)/shard_map/ppermute | solution.py:525
  64.6 19.6 %collective-permute-start.19 = (bf16[32,4096]{1,0:T(8,128)(2,1)S(1)}, bf16[32,4096]{1,0:T(8,128)(2,1)S(1)}, u32[]{:S(2)}, u32[]{:S(2)}) collective-permute-start(bf16[32,4096]{1,0:T(8,128)(2,1)S(1)} %get-tuple-element.89), channel_id=1, source_target_pairs={{0,1},{1,0},{2,3},{3,2},{4,5},{5,4},{6,7},{7,6},{8,9},{9,8},{10,11... | collective-permute-start | bytes 786440 | tf_op jit(solution)/shard_map/ppermute | solution.py:525
  71.5 7.7 %collective-permute-start.21 = (bf16[32,4096]{1,0:T(8,128)(2,1)S(1)}, bf16[32,4096]{1,0:T(8,128)(2,1)S(1)}, u32[]{:S(2)}, u32[]{:S(2)}) collective-permute-start(bf16[32,4096]{1,0:T(8,128)(2,1)S(1)} %get-tuple-element.96), channel_id=1, source_target_pairs={{0,4},{1,5},{2,6},{3,7},{4,0},{5,1},{6,2},{7,3},{8,12},{9,13},{10,... | collective-permute-start | bytes 786440 | tf_op jit(solution)/shard_map/ppermute | solution.py:525
  71.9 7.3 %collective-permute-start.22 = (bf16[32,4096]{1,0:T(8,128)(2,1)S(1)}, bf16[32,4096]{1,0:T(8,128)(2,1)S(1)}, u32[]{:S(2)}, u32[]{:S(2)}) collective-permute-start(bf16[32,4096]{1,0:T(8,128)(2,1)S(1)} %get-tuple-element.97), channel_id=1, source_target_pairs={{0,2},{1,3},{2,0},{3,1},{4,6},{5,7},{6,4},{7,5},{8,10},{9,11},{10,... | collective-permute-start | bytes 786440 | tf_op jit(solution)/shard_map/ppermute | solution.py:525
  73.1 20.9 %collective-permute-start.26 = (bf16[32,4096]{1,0:T(8,128)(2,1)S(1)}, bf16[32,4096]{1,0:T(8,128)(2,1)S(1)}, u32[]{:S(2)}, u32[]{:S(2)}) collective-permute-start(bf16[32,4096]{1,0:T(8,128)(2,1)S(1)} %get-tuple-element.106), channel_id=1, source_target_pairs={{0,1},{1,0},{2,3},{3,2},{4,5},{5,4},{6,7},{7,6},{8,9},{9,8},{10,11... | collective-permute-start | bytes 786440 | tf_op jit(solution)/shard_map/ppermute | solution.py:525
  79.4 6.7 %collective-permute-start.24 = (bf16[32,4096]{1,0:T(8,128)(2,1)S(1)}, bf16[32,4096]{1,0:T(8,128)(2,1)S(1)}, u32[]{:S(2)}, u32[]{:S(2)}) collective-permute-start(bf16[32,4096]{1,0:T(8,128)(2,1)S(1)} %add_convert_fusion.3), channel_id=1, source_target_pairs={{0,2},{1,3},{2,0},{3,1},{4,6},{5,7},{6,4},{7,5},{8,10},{9,11},{10,... | collective-permute-start | bytes 786440 | tf_op jit(solution)/shard_map/ppermute | solution.py:525
  80.8 13.8 %collective-permute-start.27 = (bf16[32,4096]{1,0:T(8,128)(2,1)S(1)}, bf16[32,4096]{1,0:T(8,128)(2,1)S(1)}, u32[]{:S(2)}, u32[]{:S(2)}) collective-permute-start(bf16[32,4096]{1,0:T(8,128)(2,1)S(1)} %add_convert_fusion.4), channel_id=1, source_target_pairs={{0,8},{1,9},{2,10},{3,11},{4,12},{5,13},{6,14},{7,15},{8,0},{9,1},... | collective-permute-start | bytes 786440 | tf_op jit(solution)/shard_map/ppermute | solution.py:525
  86.2 10.8 %collective-permute-start.28 = (bf16[32,4096]{1,0:T(8,128)(2,1)S(1)}, bf16[32,4096]{1,0:T(8,128)(2,1)S(1)}, u32[]{:S(2)}, u32[]{:S(2)}) collective-permute-start(bf16[32,4096]{1,0:T(8,128)(2,1)S(1)} %add_convert_fusion.2), channel_id=1, source_target_pairs={{0,4},{1,5},{2,6},{3,7},{4,0},{5,1},{6,2},{7,3},{8,12},{9,13},{10,... | collective-permute-start | bytes 786440 | tf_op jit(solution)/shard_map/ppermute | solution.py:525
  87.7 9.2 %collective-permute-start.29 = (bf16[32,4096]{1,0:T(8,128)(2,1)S(1)}, bf16[32,4096]{1,0:T(8,128)(2,1)S(1)}, u32[]{:S(2)}, u32[]{:S(2)}) collective-permute-start(bf16[32,4096]{1,0:T(8,128)(2,1)S(1)} %add_convert_fusion.1._), channel_id=1, source_target_pairs={{0,2},{1,3},{2,0},{3,1},{4,6},{5,7},{6,4},{7,5},{8,10},{9,11},{10,... | collective-permute-start | bytes 786440 | tf_op jit(solution)/shard_map/ppermute | solution.py:525
  (10 other events, 158.1 us)

commit v5 on v4

--- a/solution.py
+++ b/solution.py
@@ -14,7 +14,7 @@
 RANK = 16
 LANES = 128
 GROUP = 64
-FLYING = 3
+FLYING = 6
 AHEAD = 2
 BLOCK = 512
 code_levels = (

time: 98 us -> 98 us (level)
  no operation moved by 1% of the time
where the time goes in v5:
time: 98 us; the launch traced here: 97.8 us
  Pallas kernels  50.8 us (52%)
  starting transfers between devices  26.2 us (27%)
  waiting for transfers between devices  17.5 us (18%)
  other arithmetic  1.47 us (2%)
    ppermute x30, starting transfers between devices, swap(): return lax.ppermute(value, 'ep', [(i, i ^ bit) for i in range(count)])  26.2 us
    pallas_call x2, Pallas kernels, enter_weights(): pl.pallas_call(functools.partial(enter_kernel, part, rows), in_specs=in_h...  19.2 us
    ppermute x30, waiting for transfers between devices, swap(): return lax.ppermute(value, 'ep', [(i, i ^ bit) for i in range(count)])  17.5 us
    pallas_call x1, Pallas kernels, expert(): pl.pallas_call(functools.partial(expert_kernel, count), in_specs=[pl.Bloc...  14.3 us
    pallas_call x2, Pallas kernels, attend(): pl.pallas_call(functools.partial(attend_kernel, first=part * rows, block=...  8.17 us
    pallas_call x1, Pallas kernels, leave_weights(): pl.pallas_call(leave_kernel, in_specs=in_hbm(4) + [pl.BlockSpec(memory_sp...  7.27 us
    pallas_call x1, Pallas kernels, norm_rows(): pl.pallas_call(norm_kernel, grid=(1,), in_specs=[whole((rows, width)), wh...  1.96 us
  transfers between devices with their start and end apart: 30, of which 10 were waited for; matrix products, arithmetic and copies ran while one was open for 1% of the time, Pallas kernels for 35%

profile of v5, /device:TPU:0, one launch (start us, length us, event | category | flops | bytes accessed | tf_op | source)
XLA Modules:
  0.0 97.8 jit_solution(8535636462338336526)
XLA Ops:
  0.6 2.0 %shard_map.167.before.held.refs_0_ = bf16[32,4224]{1,0:T(8,128)(2,1)} custom-call(bf16[32,4096]{1,0:T(8,128)(2,1)} %hidden.1, bf16[4096]{0:T(1024)(128)(2,1)} %gain.1, s32[8,32]{1,0:T(8,128)} %bitcast.24, f32[8,32]{1,0:T(8,128)} %bitcast.25), custom_call_target="tpu_custom_call" | custom-call | tf_op jit(solution)/shard_map/pallas_call | solution.py:81
  2.6 4.0 %collective-permute-start.1 = (bf16[32,4224]{1,0:T(8,128)(2,1)}, bf16[32,4224]{1,0:T(8,128)(2,1)S(1)}, u32[]{:S(2)}, u32[]{:S(2)}) collective-permute-start(bf16[32,4224]{1,0:T(8,128)(2,1)} %shard_map.167.before.held.refs_0_), channel_id=1, source_target_pairs={{0,8},{1,9},{2,10},{3,11},{4,12},{5,13},{6,14},{7,15},{8,0},{9,1},... | collective-permute-start | bytes 811016 | tf_op jit(solution)/shard_map/ppermute | solution.py:525
  6.6 1.6 %collective-permute-start.2 = (bf16[32,4224]{1,0:T(8,128)(2,1)}, bf16[32,4224]{1,0:T(8,128)(2,1)S(1)}, u32[]{:S(2)}, u32[]{:S(2)}) collective-permute-start(bf16[32,4224]{1,0:T(8,128)(2,1)} %shard_map.167.before.held.refs_0_), channel_id=1, source_target_pairs={{0,4},{1,5},{2,6},{3,7},{4,0},{5,1},{6,2},{7,3},{8,12},{9,13},{10,... | collective-permute-start | bytes 811016 | tf_op jit(solution)/shard_map/ppermute | solution.py:525
  8.2 1.5 %collective-permute-start.3 = (bf16[32,4224]{1,0:T(8,128)(2,1)}, bf16[32,4224]{1,0:T(8,128)(2,1)S(1)}, u32[]{:S(2)}, u32[]{:S(2)}) collective-permute-start(bf16[32,4224]{1,0:T(8,128)(2,1)} %shard_map.167.before.held.refs_0_), channel_id=1, source_target_pairs={{0,2},{1,3},{2,0},{3,1},{4,6},{5,7},{6,4},{7,5},{8,10},{9,11},{10,... | collective-permute-start | bytes 811016 | tf_op jit(solution)/shard_map/ppermute | solution.py:525
  9.7 9.6 %shard_map.168 = (bf16[6,4096,256]{2,1,0:T(8,128)(2,1)}, f32[8,128]{1,0:T(8,128)}) custom-call(s32[1,4096,512]{2,1,0:T(8,128)} %codes.4, bf16[1,64,1536]{2,1,0:T(8,128)(2,1)} %scale.4, bf16[32,4096]{1,0:T(8,128)(2,1)} %bitcast.20, bf16[1,2,16,768]{3,2,1,0:T(8,128)(2,1)} %up_map.4, bf16[32,4224]{1,0:T(8,128)(2,1)} %shard_map.167.before.held.refs_0_, ...), custom_call_target="tpu_custom_call" | custom-call | flops 4000000000 | bytes 20000000 | tf_op jit(solution)/shard_map/pallas_call | solution.py:199
  19.4 1.5 %collective-permute-start.6 = (bf16[32,4224]{1,0:T(8,128)(2,1)S(1)}, bf16[32,4224]{1,0:T(8,128)(2,1)S(1)}, u32[]{:S(2)}, u32[]{:S(2)}) collective-permute-start(bf16[32,4224]{1,0:T(8,128)(2,1)S(1)} %collective-permute-done.1.refs_8_), channel_id=1, source_target_pairs={{0,4},{1,5},{2,6},{3,7},{4,0},{5,1},{6,2},{7,3},{8,12},{9,13},{10,... | collective-permute-start | bytes 811016 | tf_op jit(solution)/shard_map/ppermute | solution.py:525
  20.9 1.5 %collective-permute-start.8 = (bf16[32,4224]{1,0:T(8,128)(2,1)S(1)}, bf16[32,4224]{1,0:T(8,128)(2,1)S(1)}, u32[]{:S(2)}, u32[]{:S(2)}) collective-permute-start(bf16[32,4224]{1,0:T(8,128)(2,1)S(1)} %collective-permute-done.1.refs_8_), channel_id=1, source_target_pairs={{0,2},{1,3},{2,0},{3,1},{4,6},{5,7},{6,4},{7,5},{8,10},{9,11},{10,... | collective-permute-start | bytes 811016 | tf_op jit(solution)/shard_map/ppermute | solution.py:525
  22.4 0.5 collective-permute-start.7
  22.9 9.6 %shard_map.169 = (bf16[6,4096,256]{2,1,0:T(8,128)(2,1)}, f32[8,128]{1,0:T(8,128)}) custom-call(s32[1,4096,512]{2,1,0:T(8,128)} %codes.4, bf16[1,64,1536]{2,1,0:T(8,128)(2,1)} %scale.4, bf16[32,4096]{1,0:T(8,128)(2,1)} %bitcast.21, bf16[1,2,16,768]{3,2,1,0:T(8,128)(2,1)} %up_map.4, ...), custom_call_target="tpu_custom_call", output_to_operand_aliasing={{0}: (5, {})} | custom-call | flops 4000000000 | bytes 20000000 | tf_op jit(solution)/shard_map/pallas_call | solution.py:199
  32.6 1.3 %collective-permute-done.7.refs_6_ = bf16[32,4224]{1,0:T(8,128)(2,1)S(1)} collective-permute-done((bf16[32,4224]{1,0:T(8,128)(2,1)S(1)}, bf16[32,4224]{1,0:T(8,128)(2,1)S(1)}, u32[]{:S(2)}, u32[]{:S(2)}) %collective-permute-start.7) | collective-permute-done | bytes 270368 | tf_op jit(solution)/shard_map/ppermute | solution.py:525
  33.9 0.5 collective-permute-start.10
  34.4 1.5 %collective-permute-start.13 = (bf16[32,4224]{1,0:T(8,128)(2,1)S(1)}, bf16[32,4224]{1,0:T(8,128)(2,1)}, u32[]{:S(2)}, u32[]{:S(2)}) collective-permute-start(bf16[32,4224]{1,0:T(8,128)(2,1)S(1)} %collective-permute-done.6.refs_12_), channel_id=1, source_target_pairs={{0,2},{1,3},{2,0},{3,1},{4,6},{5,7},{6,4},{7,5},{8,10},{9,11},{10,... | collective-permute-start | bytes 811016 | tf_op jit(solution)/shard_map/ppermute | solution.py:525
  37.1 7.3 %shard_map.170 = (bf16[768,2048]{1,0:T(8,128)(2,1)}, f32[8,128]{1,0:T(8,128)}) custom-call(s32[1,256,4096]{2,1,0:T(8,128)} %refs_18_.1, bf16[1,12,4096]{2,1,0:T(8,128)(2,1)} %refs_19_.1, bf16[16,768]{1,0:T(8,128)(2,1)} %bitcast.17, bf16[1,16,4096]{2,1,0:T(8,128)(2,1)} %refs_21_.1, f32[8,128]{1,0:T(8,128)} %get-tuple-element.70.before), custom_call_target="tpu_custom_call" | custom-call | flops 2000000000 | bytes 8000000 | tf_op jit(solution)/shard_map/pallas_call | solution.py:302
  44.7 1.6 %collective-permute-done.14.refs_15_ = bf16[32,4224]{1,0:T(8,128)(2,1)} collective-permute-done((bf16[32,4224]{1,0:T(8,128)(2,1)}, bf16[32,4224]{1,0:T(8,128)(2,1)}, u32[]{:S(2)}, u32[]{:S(2)}) %collective-permute-start.14) | collective-permute-done | bytes 270368 | tf_op jit(solution)/shard_map/ppermute | solution.py:525
  46.4 14.3 %shard_map.171 = (bf16[32,4096]{1,0:T(8,128)(2,1)S(1)}, bf16[32,4096]{1,0:T(8,128)(2,1)S(1)}, bf16[32,4096]{1,0:T(8,128)(2,1)S(1)}, bf16[32,4096]{1,0:T(8,128)(2...) custom-call(s32[1]{0:T(128)} %bitcast.own, ...), custom_call_target="tpu_custom_call" | custom-call | flops 8000000000 | bytes 22000000 | tf_op jit(solution)/shard_map/pallas_call | solution.py:430
  60.9 1.3 %collective-permute-done.15 = bf16[32,4096]{1,0:T(8,128)(2,1)S(1)} collective-permute-done((bf16[32,4096]{1,0:T(8,128)(2,1)S(1)}, bf16[32,4096]{1,0:T(8,128)(2,1)S(1)}, u32[]{:S(2)}, u32[]{:S(2)}) %collective-permute-start.15) | collective-permute-done | bytes 262176 | tf_op jit(solution)/shard_map/ppermute | solution.py:525
  62.9 1.0 collective-permute-start.16
  64.1 0.4 collective-permute-start.23
  65.0 4.1 %shard_map.172 = bf16[16,32,128]{2,1,0:T(8,128)(2,1)S(1)} custom-call(s32[32]{0:T(128)S(1)} %copy-done.2, bf16[32,32,128]{2,1,0:T(8,128)(2,1)S(1)} %bitcast.15, bf16[32,2,256]{2,1,0:T(2,128)(2,1)S(1)} %copy-done.1, bf16[32,2,256,256]{3,2,1,0:T(8,128)(2,1)} %cache.3, bf16[32,4096]{1,0:T(8,128)(2,1)S(1)} %add_convert_fusion.7._), custom_call_target="tpu_custom_call" | custom-call | flops 500000000 | bytes 20000000 | tf_op jit(solution)/shard_map/pallas_call | solution.py:506
  69.1 2.2 %collective-permute-done.16 = bf16[32,4096]{1,0:T(8,128)(2,1)S(1)} collective-permute-done((bf16[32,4096]{1,0:T(8,128)(2,1)S(1)}, bf16[32,4096]{1,0:T(8,128)(2,1)S(1)}, u32[]{:S(2)}, u32[]{:S(2)}) %collective-permute-start.16) | collective-permute-done | bytes 262176 | tf_op jit(solution)/shard_map/ppermute | solution.py:525
  71.9 1.1 %collective-permute-start.22 = (bf16[32,4096]{1,0:T(8,128)(2,1)S(1)}, bf16[32,4096]{1,0:T(8,128)(2,1)S(1)}, u32[]{:S(2)}, u32[]{:S(2)}) collective-permute-start(bf16[32,4096]{1,0:T(8,128)(2,1)S(1)} %get-tuple-element.97), channel_id=1, source_target_pairs={{0,2},{1,3},{2,0},{3,1},{4,6},{5,7},{6,4},{7,5},{8,10},{9,11},{10,... | collective-permute-start | bytes 786440 | tf_op jit(solution)/shard_map/ppermute | solution.py:525
  73.2 6.0 %collective-permute-done.21 = bf16[32,4096]{1,0:T(8,128)(2,1)S(1)} collective-permute-done((bf16[32,4096]{1,0:T(8,128)(2,1)S(1)}, bf16[32,4096]{1,0:T(8,128)(2,1)S(1)}, u32[]{:S(2)}, u32[]{:S(2)}) %collective-permute-start.21) | collective-permute-done | bytes 262176 | tf_op jit(solution)/shard_map/ppermute | solution.py:525
  79.4 1.3 %collective-permute-start.24 = (bf16[32,4096]{1,0:T(8,128)(2,1)S(1)}, bf16[32,4096]{1,0:T(8,128)(2,1)S(1)}, u32[]{:S(2)}, u32[]{:S(2)}) collective-permute-start(bf16[32,4096]{1,0:T(8,128)(2,1)S(1)} %add_convert_fusion.3), channel_id=1, source_target_pairs={{0,2},{1,3},{2,0},{3,1},{4,6},{5,7},{6,4},{7,5},{8,10},{9,11},{10,... | collective-permute-start | bytes 786440 | tf_op jit(solution)/shard_map/ppermute | solution.py:525
  80.8 3.4 %collective-permute-start.27 = (bf16[32,4096]{1,0:T(8,128)(2,1)S(1)}, bf16[32,4096]{1,0:T(8,128)(2,1)S(1)}, u32[]{:S(2)}, u32[]{:S(2)}) collective-permute-start(bf16[32,4096]{1,0:T(8,128)(2,1)S(1)} %add_convert_fusion.4), channel_id=1, source_target_pairs={{0,8},{1,9},{2,10},{3,11},{4,12},{5,13},{6,14},{7,15},{8,0},{9,1},... | collective-permute-start | bytes 786440 | tf_op jit(solution)/shard_map/ppermute | solution.py:525
  84.2 1.9 %collective-permute-done.24 = bf16[32,4096]{1,0:T(8,128)(2,1)S(1)} collective-permute-done((bf16[32,4096]{1,0:T(8,128)(2,1)S(1)}, bf16[32,4096]{1,0:T(8,128)(2,1)S(1)}, u32[]{:S(2)}, u32[]{:S(2)}) %collective-permute-start.24) | collective-permute-done | bytes 262176 | tf_op jit(solution)/shard_map/ppermute | solution.py:525
  86.2 1.5 %collective-permute-start.28 = (bf16[32,4096]{1,0:T(8,128)(2,1)S(1)}, bf16[32,4096]{1,0:T(8,128)(2,1)S(1)}, u32[]{:S(2)}, u32[]{:S(2)}) collective-permute-start(bf16[32,4096]{1,0:T(8,128)(2,1)S(1)} %add_convert_fusion.2), channel_id=1, source_target_pairs={{0,4},{1,5},{2,6},{3,7},{4,0},{5,1},{6,2},{7,3},{8,12},{9,13},{10,... | collective-permute-start | bytes 786440 | tf_op jit(solution)/shard_map/ppermute | solution.py:525
  87.7 1.4 %collective-permute-start.29 = (bf16[32,4096]{1,0:T(8,128)(2,1)S(1)}, bf16[32,4096]{1,0:T(8,128)(2,1)S(1)}, u32[]{:S(2)}, u32[]{:S(2)}) collective-permute-start(bf16[32,4096]{1,0:T(8,128)(2,1)S(1)} %add_convert_fusion.1._), channel_id=1, source_target_pairs={{0,2},{1,3},{2,0},{3,1},{4,6},{5,7},{6,4},{7,5},{8,10},{9,11},{10,... | collective-permute-start | bytes 786440 | tf_op jit(solution)/shard_map/ppermute | solution.py:525
  89.1 4.1 %shard_map.173 = bf16[16,32,128]{2,1,0:T(8,128)(2,1)S(1)} custom-call(s32[32]{0:T(128)S(1)} %copy-done.2, bf16[32,32,128]{2,1,0:T(8,128)(2,1)S(1)} %bitcast.16, bf16[32,2,256]{2,1,0:T(2,128)(2,1)S(1)} %copy-done.1, bf16[32,2,256,256]{3,2,1,0:T(8,128)(2,1)} %cache.3, bf16[32,4096]{1,0:T(8,128)(2,1)S(1)} %add_convert_fusion.1._), custom_call_target="tpu_custom_call" | custom-call | flops 500000000 | bytes 20000000 | tf_op jit(solution)/shard_map/pallas_call | solution.py:506
  93.2 0.8 copy.22
  94.0 0.6 collective-permute-done.27
  94.6 2.3 %collective-permute-done.28 = bf16[32,4096]{1,0:T(8,128)(2,1)S(1)} collective-permute-done((bf16[32,4096]{1,0:T(8,128)(2,1)S(1)}, bf16[32,4096]{1,0:T(8,128)(2,1)S(1)}, u32[]{:S(2)}, u32[]{:S(2)}) %collective-permute-start.28) | collective-permute-done | bytes 262176 | tf_op jit(solution)/shard_map/ppermute | solution.py:525
  96.9 0.9 add_convert_fusion
  (69 shorter events, 4.3 us)
Async XLA Ops:
  2.6 16.7 %collective-permute-start.1 = (bf16[32,4224]{1,0:T(8,128)(2,1)}, bf16[32,4224]{1,0:T(8,128)(2,1)S(1)}, u32[]{:S(2)}, u32[]{:S(2)}) collective-permute-start(bf16[32,4224]{1,0:T(8,128)(2,1)} %shard_map.167.before.held.refs_0_), channel_id=1, source_target_pairs={{0,8},{1,9},{2,10},{3,11},{4,12},{5,13},{6,14},{7,15},{8,0},{9,1},... | collective-permute-start | bytes 811016 | tf_op jit(solution)/shard_map/ppermute | solution.py:525
  6.6 12.8 %collective-permute-start.2 = (bf16[32,4224]{1,0:T(8,128)(2,1)}, bf16[32,4224]{1,0:T(8,128)(2,1)S(1)}, u32[]{:S(2)}, u32[]{:S(2)}) collective-permute-start(bf16[32,4224]{1,0:T(8,128)(2,1)} %shard_map.167.before.held.refs_0_), channel_id=1, source_target_pairs={{0,4},{1,5},{2,6},{3,7},{4,0},{5,1},{6,2},{7,3},{8,12},{9,13},{10,... | collective-permute-start | bytes 811016 | tf_op jit(solution)/shard_map/ppermute | solution.py:525
  8.2 11.2 %collective-permute-start.3 = (bf16[32,4224]{1,0:T(8,128)(2,1)}, bf16[32,4224]{1,0:T(8,128)(2,1)S(1)}, u32[]{:S(2)}, u32[]{:S(2)}) collective-permute-start(bf16[32,4224]{1,0:T(8,128)(2,1)} %shard_map.167.before.held.refs_0_), channel_id=1, source_target_pairs={{0,2},{1,3},{2,0},{3,1},{4,6},{5,7},{6,4},{7,5},{8,10},{9,11},{10,... | collective-permute-start | bytes 811016 | tf_op jit(solution)/shard_map/ppermute | solution.py:525
  19.4 13.1 %collective-permute-start.6 = (bf16[32,4224]{1,0:T(8,128)(2,1)S(1)}, bf16[32,4224]{1,0:T(8,128)(2,1)S(1)}, u32[]{:S(2)}, u32[]{:S(2)}) collective-permute-start(bf16[32,4224]{1,0:T(8,128)(2,1)S(1)} %collective-permute-done.1.refs_8_), channel_id=1, source_target_pairs={{0,4},{1,5},{2,6},{3,7},{4,0},{5,1},{6,2},{7,3},{8,12},{9,13},{10,... | collective-permute-start | bytes 811016 | tf_op jit(solution)/shard_map/ppermute | solution.py:525
  20.9 11.7 %collective-permute-start.8 = (bf16[32,4224]{1,0:T(8,128)(2,1)S(1)}, bf16[32,4224]{1,0:T(8,128)(2,1)S(1)}, u32[]{:S(2)}, u32[]{:S(2)}) collective-permute-start(bf16[32,4224]{1,0:T(8,128)(2,1)S(1)} %collective-permute-done.1.refs_8_), channel_id=1, source_target_pairs={{0,2},{1,3},{2,0},{3,1},{4,6},{5,7},{6,4},{7,5},{8,10},{9,11},{10,... | collective-permute-start | bytes 811016 | tf_op jit(solution)/shard_map/ppermute | solution.py:525
  22.4 11.5 %collective-permute-start.7 = (bf16[32,4224]{1,0:T(8,128)(2,1)S(1)}, bf16[32,4224]{1,0:T(8,128)(2,1)S(1)}, u32[]{:S(2)}, u32[]{:S(2)}) collective-permute-start(bf16[32,4224]{1,0:T(8,128)(2,1)S(1)} %collective-permute-done.2.refs_4_), channel_id=1, source_target_pairs={{0,2},{1,3},{2,0},{3,1},{4,6},{5,7},{6,4},{7,5},{8,10},{9,11},{10,... | collective-permute-start | bytes 811016 | tf_op jit(solution)/shard_map/ppermute | solution.py:525
  22.9 23.4 %copy-start.4 = (bf16[1,16,4096]{2,1,0:T(8,128)(2,1)S(1)}, bf16[1,16,4096]{2,1,0:T(8,128)(2,1)}, u32[]{:S(2)}) copy-start(bf16[1,16,4096]{2,1,0:T(8,128)(2,1)} %refs_21_.1) | copy-start | bytes 393220
  22.9 23.4 %copy-start.5 = (bf16[1,768,16]{1,2,0:T(8,128)(2,1)S(1)}, bf16[1,768,16]{1,2,0:T(8,128)(2,1)}, u32[]{:S(2)}) copy-start(bf16[1,768,16]{1,2,0:T(8,128)(2,1)} %param.30) | copy-start | bytes 73732
  33.9 2.3 %collective-permute-start.11 = (bf16[32,4224]{1,0:T(8,128)(2,1)S(1)}, bf16[32,4224]{1,0:T(8,128)(2,1)S(1)}, u32[]{:S(2)}, u32[]{:S(2)}) collective-permute-start(bf16[32,4224]{1,0:T(8,128)(2,1)S(1)} %collective-permute-done.6.refs_12_), channel_id=1, source_target_pairs={{0,1},{1,0},{2,3},{3,2},{4,5},{5,4},{6,7},{7,6},{8,9},{9,8},{10,11... | collective-permute-start | bytes 811016 | tf_op jit(solution)/shard_map/ppermute | solution.py:525
  33.9 2.6 %collective-permute-start.10 = (bf16[32,4224]{1,0:T(8,128)(2,1)S(1)}, bf16[32,4224]{1,0:T(8,128)(2,1)}, u32[]{:S(2)}, u32[]{:S(2)}) collective-permute-start(bf16[32,4224]{1,0:T(8,128)(2,1)S(1)} %collective-permute-done.8.refs_10_), channel_id=1, source_target_pairs={{0,1},{1,0},{2,3},{3,2},{4,5},{5,4},{6,7},{7,6},{8,9},{9,8},{10,11... | collective-permute-start | bytes 811016 | tf_op jit(solution)/shard_map/ppermute | solution.py:525
  34.4 2.3 %collective-permute-start.9 = (bf16[32,4224]{1,0:T(8,128)(2,1)S(1)}, bf16[32,4224]{1,0:T(8,128)(2,1)}, u32[]{:S(2)}, u32[]{:S(2)}) collective-permute-start(bf16[32,4224]{1,0:T(8,128)(2,1)S(1)} %collective-permute-done.7.refs_6_), channel_id=1, source_target_pairs={{0,1},{1,0},{2,3},{3,2},{4,5},{5,4},{6,7},{7,6},{8,9},{9,8},{10,11... | collective-permute-start | bytes 811016 | tf_op jit(solution)/shard_map/ppermute | solution.py:525
  34.4 9.9 %collective-permute-start.13 = (bf16[32,4224]{1,0:T(8,128)(2,1)S(1)}, bf16[32,4224]{1,0:T(8,128)(2,1)}, u32[]{:S(2)}, u32[]{:S(2)}) collective-permute-start(bf16[32,4224]{1,0:T(8,128)(2,1)S(1)} %collective-permute-done.6.refs_12_), channel_id=1, source_target_pairs={{0,2},{1,3},{2,0},{3,1},{4,6},{5,7},{6,4},{7,5},{8,10},{9,11},{10,... | collective-permute-start | bytes 811016 | tf_op jit(solution)/shard_map/ppermute | solution.py:525
  36.0 8.7 %collective-permute-start = (bf16[32,4224]{1,0:T(8,128)(2,1)S(1)}, bf16[32,4224]{1,0:T(8,128)(2,1)S(1)}, u32[]{:S(2)}, u32[]{:S(2)}) collective-permute-start(bf16[32,4224]{1,0:T(8,128)(2,1)S(1)} %copy-done), channel_id=1, source_target_pairs={{0,1},{1,0},{2,3},{3,2},{4,5},{5,4},{6,7},{7,6},{8,9},{9,8},{10,11... | collective-permute-start | bytes 811016 | tf_op jit(solution)/shard_map/ppermute | solution.py:525
  36.2 8.4 %collective-permute-start.12 = (bf16[32,4224]{1,0:T(8,128)(2,1)S(1)}, bf16[32,4224]{1,0:T(8,128)(2,1)}, u32[]{:S(2)}, u32[]{:S(2)}) collective-permute-start(bf16[32,4224]{1,0:T(8,128)(2,1)S(1)} %collective-permute-done.1.refs_8_), channel_id=1, source_target_pairs={{0,1},{1,0},{2,3},{3,2},{4,5},{5,4},{6,7},{7,6},{8,9},{9,8},{10,11... | collective-permute-start | bytes 811016 | tf_op jit(solution)/shard_map/ppermute | solution.py:525
  36.6 8.1 %collective-permute-start.5 = (bf16[32,4224]{1,0:T(8,128)(2,1)S(1)}, bf16[32,4224]{1,0:T(8,128)(2,1)S(1)}, u32[]{:S(2)}, u32[]{:S(2)}) collective-permute-start(bf16[32,4224]{1,0:T(8,128)(2,1)S(1)} %collective-permute-done.2.refs_4_), channel_id=1, source_target_pairs={{0,1},{1,0},{2,3},{3,2},{4,5},{5,4},{6,7},{7,6},{8,9},{9,8},{10,11... | collective-permute-start | bytes 811016 | tf_op jit(solution)/shard_map/ppermute | solution.py:525
  36.8 7.9 %collective-permute-start.4 = (bf16[32,4224]{1,0:T(8,128)(2,1)S(1)}, bf16[32,4224]{1,0:T(8,128)(2,1)S(1)}, u32[]{:S(2)}, u32[]{:S(2)}) collective-permute-start(bf16[32,4224]{1,0:T(8,128)(2,1)S(1)} %collective-permute-done.3.refs_2_), channel_id=1, source_target_pairs={{0,1},{1,0},{2,3},{3,2},{4,5},{5,4},{6,7},{7,6},{8,9},{9,8},{10,11... | collective-permute-start | bytes 811016 | tf_op jit(solution)/shard_map/ppermute | solution.py:525
  44.4 2.0 %collective-permute-start.14 = (bf16[32,4224]{1,0:T(8,128)(2,1)}, bf16[32,4224]{1,0:T(8,128)(2,1)}, u32[]{:S(2)}, u32[]{:S(2)}) collective-permute-start(bf16[32,4224]{1,0:T(8,128)(2,1)} %collective-permute-done.13.refs_14_), channel_id=1, source_target_pairs={{0,1},{1,0},{2,3},{3,2},{4,5},{5,4},{6,7},{7,6},{8,9},{9,8},{10,11... | collective-permute-start | bytes 811016 | tf_op jit(solution)/shard_map/ppermute | solution.py:525
  60.7 1.6 %collective-permute-start.15 = (bf16[32,4096]{1,0:T(8,128)(2,1)S(1)}, bf16[32,4096]{1,0:T(8,128)(2,1)S(1)}, u32[]{:S(2)}, u32[]{:S(2)}) collective-permute-start(bf16[32,4096]{1,0:T(8,128)(2,1)S(1)} %get-tuple-element.75), channel_id=1, source_target_pairs={{0,1},{1,0},{2,3},{3,2},{4,5},{5,4},{6,7},{7,6},{8,9},{9,8},{10,11... | collective-permute-start | bytes 786440 | tf_op jit(solution)/shard_map/ppermute | solution.py:525
  62.3 2.2 %collective-permute-start.17 = (bf16[32,4096]{1,0:T(8,128)(2,1)S(1)}, bf16[32,4096]{1,0:T(8,128)(2,1)S(1)}, u32[]{:S(2)}, u32[]{:S(2)}) collective-permute-start(bf16[32,4096]{1,0:T(8,128)(2,1)S(1)} %get-tuple-element.85), channel_id=1, source_target_pairs={{0,1},{1,0},{2,3},{3,2},{4,5},{5,4},{6,7},{7,6},{8,9},{9,8},{10,11... | collective-permute-start | bytes 786440 | tf_op jit(solution)/shard_map/ppermute | solution.py:525
  62.6 2.0 %collective-permute-start.18 = (bf16[32,4096]{1,0:T(8,128)(2,1)S(1)}, bf16[32,4096]{1,0:T(8,128)(2,1)S(1)}, u32[]{:S(2)}, u32[]{:S(2)}) collective-permute-start(bf16[32,4096]{1,0:T(8,128)(2,1)S(1)} %get-tuple-element.86), channel_id=1, source_target_pairs={{0,1},{1,0},{2,3},{3,2},{4,5},{5,4},{6,7},{7,6},{8,9},{9,8},{10,11... | collective-permute-start | bytes 786440 | tf_op jit(solution)/shard_map/ppermute | solution.py:525
  62.9 8.4 %collective-permute-start.16 = (bf16[32,4096]{1,0:T(8,128)(2,1)S(1)}, bf16[32,4096]{1,0:T(8,128)(2,1)S(1)}, u32[]{:S(2)}, u32[]{:S(2)}) collective-permute-start(bf16[32,4096]{1,0:T(8,128)(2,1)S(1)} %add_convert_fusion.7._), channel_id=1, source_target_pairs={{0,2},{1,3},{2,0},{3,1},{4,6},{5,7},{6,4},{7,5},{8,10},{9,11},{10,... | collective-permute-start | bytes 786440 | tf_op jit(solution)/shard_map/ppermute | solution.py:525
  63.9 16.8 %collective-permute-start.25 = (bf16[32,4096]{1,0:T(8,128)(2,1)S(1)}, bf16[32,4096]{1,0:T(8,128)(2,1)S(1)}, u32[]{:S(2)}, u32[]{:S(2)}) collective-permute-start(bf16[32,4096]{1,0:T(8,128)(2,1)S(1)} %get-tuple-element.103), channel_id=1, source_target_pairs={{0,1},{1,0},{2,3},{3,2},{4,5},{5,4},{6,7},{7,6},{8,9},{9,8},{10,11... | collective-permute-start | bytes 786440 | tf_op jit(solution)/shard_map/ppermute | solution.py:525
  64.1 7.9 %collective-permute-start.23 = (bf16[32,4096]{1,0:T(8,128)(2,1)S(1)}, bf16[32,4096]{1,0:T(8,128)(2,1)S(1)}, u32[]{:S(2)}, u32[]{:S(2)}) collective-permute-start(bf16[32,4096]{1,0:T(8,128)(2,1)S(1)} %get-tuple-element.99), channel_id=1, source_target_pairs={{0,1},{1,0},{2,3},{3,2},{4,5},{5,4},{6,7},{7,6},{8,9},{9,8},{10,11... | collective-permute-start | bytes 786440 | tf_op jit(solution)/shard_map/ppermute | solution.py:525
  64.5 8.6 %collective-permute-start.20 = (bf16[32,4096]{1,0:T(8,128)(2,1)S(1)}, bf16[32,4096]{1,0:T(8,128)(2,1)S(1)}, u32[]{:S(2)}, u32[]{:S(2)}) collective-permute-start(bf16[32,4096]{1,0:T(8,128)(2,1)S(1)} %get-tuple-element.90), channel_id=1, source_target_pairs={{0,1},{1,0},{2,3},{3,2},{4,5},{5,4},{6,7},{7,6},{8,9},{9,8},{10,11... | collective-permute-start | bytes 786440 | tf_op jit(solution)/shard_map/ppermute | solution.py:525
  64.6 19.6 %collective-permute-start.19 = (bf16[32,4096]{1,0:T(8,128)(2,1)S(1)}, bf16[32,4096]{1,0:T(8,128)(2,1)S(1)}, u32[]{:S(2)}, u32[]{:S(2)}) collective-permute-start(bf16[32,4096]{1,0:T(8,128)(2,1)S(1)} %get-tuple-element.89), channel_id=1, source_target_pairs={{0,1},{1,0},{2,3},{3,2},{4,5},{5,4},{6,7},{7,6},{8,9},{9,8},{10,11... | collective-permute-start | bytes 786440 | tf_op jit(solution)/shard_map/ppermute | solution.py:525
  71.5 7.7 %collective-permute-start.21 = (bf16[32,4096]{1,0:T(8,128)(2,1)S(1)}, bf16[32,4096]{1,0:T(8,128)(2,1)S(1)}, u32[]{:S(2)}, u32[]{:S(2)}) collective-permute-start(bf16[32,4096]{1,0:T(8,128)(2,1)S(1)} %get-tuple-element.96), channel_id=1, source_target_pairs={{0,4},{1,5},{2,6},{3,7},{4,0},{5,1},{6,2},{7,3},{8,12},{9,13},{10,... | collective-permute-start | bytes 786440 | tf_op jit(solution)/shard_map/ppermute | solution.py:525
  71.9 7.3 %collective-permute-start.22 = (bf16[32,4096]{1,0:T(8,128)(2,1)S(1)}, bf16[32,4096]{1,0:T(8,128)(2,1)S(1)}, u32[]{:S(2)}, u32[]{:S(2)}) collective-permute-start(bf16[32,4096]{1,0:T(8,128)(2,1)S(1)} %get-tuple-element.97), channel_id=1, source_target_pairs={{0,2},{1,3},{2,0},{3,1},{4,6},{5,7},{6,4},{7,5},{8,10},{9,11},{10,... | collective-permute-start | bytes 786440 | tf_op jit(solution)/shard_map/ppermute | solution.py:525
  73.1 20.9 %collective-permute-start.26 = (bf16[32,4096]{1,0:T(8,128)(2,1)S(1)}, bf16[32,4096]{1,0:T(8,128)(2,1)S(1)}, u32[]{:S(2)}, u32[]{:S(2)}) collective-permute-start(bf16[32,4096]{1,0:T(8,128)(2,1)S(1)} %get-tuple-element.106), channel_id=1, source_target_pairs={{0,1},{1,0},{2,3},{3,2},{4,5},{5,4},{6,7},{7,6},{8,9},{9,8},{10,11... | collective-permute-start | bytes 786440 | tf_op jit(solution)/shard_map/ppermute | solution.py:525
  79.4 6.7 %collective-permute-start.24 = (bf16[32,4096]{1,0:T(8,128)(2,1)S(1)}, bf16[32,4096]{1,0:T(8,128)(2,1)S(1)}, u32[]{:S(2)}, u32[]{:S(2)}) collective-permute-start(bf16[32,4096]{1,0:T(8,128)(2,1)S(1)} %add_convert_fusion.3), channel_id=1, source_target_pairs={{0,2},{1,3},{2,0},{3,1},{4,6},{5,7},{6,4},{7,5},{8,10},{9,11},{10,... | collective-permute-start | bytes 786440 | tf_op jit(solution)/shard_map/ppermute | solution.py:525
  80.8 13.8 %collective-permute-start.27 = (bf16[32,4096]{1,0:T(8,128)(2,1)S(1)}, bf16[32,4096]{1,0:T(8,128)(2,1)S(1)}, u32[]{:S(2)}, u32[]{:S(2)}) collective-permute-start(bf16[32,4096]{1,0:T(8,128)(2,1)S(1)} %add_convert_fusion.4), channel_id=1, source_target_pairs={{0,8},{1,9},{2,10},{3,11},{4,12},{5,13},{6,14},{7,15},{8,0},{9,1},... | collective-permute-start | bytes 786440 | tf_op jit(solution)/shard_map/ppermute | solution.py:525
  86.2 10.8 %collective-permute-start.28 = (bf16[32,4096]{1,0:T(8,128)(2,1)S(1)}, bf16[32,4096]{1,0:T(8,128)(2,1)S(1)}, u32[]{:S(2)}, u32[]{:S(2)}) collective-permute-start(bf16[32,4096]{1,0:T(8,128)(2,1)S(1)} %add_convert_fusion.2), channel_id=1, source_target_pairs={{0,4},{1,5},{2,6},{3,7},{4,0},{5,1},{6,2},{7,3},{8,12},{9,13},{10,... | collective-permute-start | bytes 786440 | tf_op jit(solution)/shard_map/ppermute | solution.py:525
  87.7 9.2 %collective-permute-start.29 = (bf16[32,4096]{1,0:T(8,128)(2,1)S(1)}, bf16[32,4096]{1,0:T(8,128)(2,1)S(1)}, u32[]{:S(2)}, u32[]{:S(2)}) collective-permute-start(bf16[32,4096]{1,0:T(8,128)(2,1)S(1)} %add_convert_fusion.1._), channel_id=1, source_target_pairs={{0,2},{1,3},{2,0},{3,1},{4,6},{5,7},{6,4},{7,5},{8,10},{9,11},{10,... | collective-permute-start | bytes 786440 | tf_op jit(solution)/shard_map/ppermute | solution.py:525
  (10 other events, 158.1 us)
